TPU v7x, 128 devices: a whole 4x4x4 slice. The times are simulated.
128 devices in a mesh: row: 32 (over y, z, x_lo), col: 4 (over x_hi, core).
Axes of the slice: x: 4 (x_hi: 2, x_lo: 2; x = x_hi * 2 + x_lo), y: 4, z: 4, core: 2. Of those that a mesh axis runs over, the one named last changes fastest.
Arguments:
- amp_first: bfloat16 [512, 65536], P('col', 'row'), may hold values from -6 to 6
- amp_second: bfloat16 [512, 16384], P('row', 'col'), may hold values from -6 to 6
- integrals: bfloat16 [65536, 16384], P('row', 'col'), may hold values from -0.0234375 to 0.0234375
- tile_order: int32 [4, 16], P('col'), may hold values from 0 to 15, each once within a row
Outputs:
- ladder_first: bfloat16 [512, 65536], P('col', 'row')
- ladder_second: bfloat16 [512, 16384], P('row', 'col')
Inputs may be any that keep to these rules, and one draw needn't show every extreme that they name: Each row of tile_order holds every number from 0 to 15 once.
All inputs are finite; a program needn't handle non-finite values.
Results may differ from a plain program's by a relative error of at most 0.001.
Values may be sent and summed in bfloat16 or wider, within the bound.
No kernel may reach another device: no remote copies, remote signals or barrier semaphores. Data moves between devices by JAX's collectives and lax.ppermute only.
A program may use at most 128 MiB of HBM per device.

v0:
```python
import jax
import jax.numpy as jnp
from jax import lax
from jax.sharding import PartitionSpec as P

TILE = 256


def reorder(block, order_row):
    count = block.shape[0]
    tiles = block.reshape(count, order_row.shape[0], TILE)
    return jnp.take(tiles, order_row, axis=1).reshape(count, block.shape[1])


def against(paired, integrals):
    return lax.dot_general(
        paired, integrals, (((1,), (1,)), ((), ())), preferred_element_type=jnp.float32
    )


def whole_direct(amp_second, integrals, order_row):
    gathered_second = lax.all_gather(amp_second, "row", axis=0, tiled=True)
    return against(reorder(gathered_second, order_row), integrals)


def whole_mirror(amp_first, integrals):
    gathered_first = lax.all_gather(amp_first, "col", axis=0, tiled=True)
    return jnp.dot(gathered_first, integrals, preferred_element_type=jnp.float32)


def on_device(amp_first, amp_second, integrals, tile_order):
    order_row = tile_order[0]
    direct_terms = whole_direct(amp_second, integrals, order_row)
    mirror_terms = whole_mirror(amp_first, integrals)
    ladder_first = lax.psum_scatter(direct_terms, "col", scatter_dimension=0, tiled=True)
    ladder_second = lax.psum_scatter(mirror_terms, "row", scatter_dimension=0, tiled=True)
    return (ladder_first.astype(jnp.bfloat16), ladder_second.astype(jnp.bfloat16))


def solution(mesh):
    in_specs = (P("col", "row"), P("row", "col"), P("row", "col"), P("col", None))
    out_specs = (P("col", "row"), P("row", "col"))
    return jax.shard_map(
        on_device, mesh=mesh, in_specs=in_specs, out_specs=out_specs, check_vma=False
    )
```

profile of v0, /device:TPU:0, one launch (start us, length us, event | category | flops | bytes accessed | tf_op | source)
XLA Modules:
  0.0 477.8 jit_solution(1651329161116934813)
XLA Ops:
  7.2 0.0 all-gather.3.cloned.1.call-start
  7.2 0.7 all-gather.3.cloned.1.call-update
  7.9 0.0 all-gather.5.cloned.1.call-start
  7.9 0.7 all-gather.5.cloned.1.call-update
  8.6 0.0 reduce-scatter.3.cloned.1.call-start
  8.7 0.7 fusion
  9.4 0.7 compare_and_fusion
  10.0 0.1 broadcast_in_dim.14
  10.1 167.8 %all-gather.3.cloned.1.call-done = bf16[512,4096]{1,0:T(8,128)(2,1)} async-done(((bf16[16,4096]{1,0:T(8,128)(2,1)}), bf16[512,4096]{1,0:T(8,128)(2,1)}) %all-gather.3.cloned.1.call-update) | async-done | bytes 4194320 | tf_op jit(solution)/shard_map/all_gather | solution.py:22
  177.9 6.5 %copy.9 = bf16[512,4096]{0,1:T(8,128)(2,1)} copy(bf16[512,4096]{1,0:T(8,128)(2,1)} %all-gather.3.cloned.1.call-done) | data formatting | bytes 8388608 | tf_op jit(solution)/shard_map/all_gather | solution.py:22
  184.4 6.4 %copy.10 = bf16[512,16,256]{2,0,1:T(8,128)(2,1)} copy(bf16[512,16,256]{0,2,1:T(8,128)(2,1)} %bitcast.15) | data formatting | bytes 8388608 | tf_op jit(solution)/shard_map/reshape | solution.py:11
  190.9 5.0 %gather_fusion = bf16[16,512,256]{2,1,0:T(8,128)(2,1)} fusion(bf16[512,16,256]{2,0,1:T(8,128)(2,1)} %copy.10, s32[1024]{0:T(1024)S(1)} %pad_clamp_fusion), kind=kCustom, calls=%fused_computation | custom fusion | bytes 8388672 | tf_op jit(solution)/shard_map/jit(_take)/gather | solution.py:12
  195.8 6.4 %copy.11 = bf16[512,16,256]{0,2,1:T(8,128)(2,1)} copy(bf16[512,16,256]{2,0,1:T(8,128)(2,1)} %bitcast.14) | data formatting | bytes 8388608 | tf_op jit(solution)/shard_map/jit(_take)/gather | solution.py:12
  202.2 2.6 bitcast_select_fusion
  204.9 13.9 %fusion.1 = f32[512,2048]{1,0:T(8,128)} fusion(bf16[512,4096]{0,1:T(8,128)(2,1)S(1)} %bitcast_select_fusion, bf16[2048,4096]{1,0:T(8,128)(2,1)} %param.6), kind=kOutput, calls=%fused_computation.7 | convolution fusion | flops 8589934592 | bytes 25165824 | tf_op jit(solution)/shard_map/dot_general | solution.py:16
  218.8 0.0 reduce-scatter.3.cloned.1.call-update
  218.8 0.0 reduce-scatter.5.cloned.1.call-start
  218.9 0.0 all-gather.5.cloned.1.call-done
  218.9 15.0 %fusion.2 = f32[512,4096]{1,0:T(8,128)} fusion(bf16[512,2048]{1,0:T(8,128)(2,1)} %all-gather.5.cloned.1.call-done, bf16[2048,4096]{1,0:T(8,128)(2,1)} %param.6), kind=kOutput, calls=%fused_computation.8 | convolution fusion | flops 8589934592 | bytes 27262976 | tf_op jit(solution)/shard_map/dot_general | solution.py:28
  233.9 0.0 reduce-scatter.5.cloned.1.call-update
  233.9 36.7 %reduce-scatter.3.cloned.1.call-done = f32[128,2048]{1,0:T(8,128)} async-done(((f32[512,2048]{1,0:T(8,128)}), f32[128,2048]{1,0:T(8,128)}) %reduce-scatter.3.cloned.1.call-update) | async-done | bytes 1048592 | tf_op jit(solution)/shard_map/reduce_scatter | solution.py:35
  270.6 2.1 convert_element_type.6
  272.7 197.0 %reduce-scatter.5.cloned.1.call-done = f32[16,4096]{1,0:T(8,128)} async-done(((f32[512,4096]{1,0:T(8,128)}), f32[16,4096]{1,0:T(8,128)}) %reduce-scatter.5.cloned.1.call-update) | async-done | bytes 262160 | tf_op jit(solution)/shard_map/reduce_scatter | solution.py:36
  469.7 1.6 convert_element_type.7
  (2 shorter events, 0.0 us)
Async XLA Ops:
  7.2 170.8 %all-gather.3.cloned.1.call-start = ((), (), s32[]{:S(2)}) async-start(), calls=%async_computation.2 | async-start | bytes 4325376 | tf_op jit(solution)/shard_map/all_gather | solution.py:22
  7.9 211.0 %all-gather.5.cloned.1.call-start = ((), (), s32[]{:S(2)}) async-start(), calls=%async_computation.4 | async-start | bytes 2621440 | tf_op jit(solution)/shard_map/all_gather | solution.py:27
  8.6 262.0 %reduce-scatter.3.cloned.1.call-start = ((), (), s32[]{:S(2)}) async-start(), calls=%async_computation.3 | async-start | bytes 5242880 | tf_op jit(solution)/shard_map/reduce_scatter | solution.py:35
  218.8 250.9 %reduce-scatter.5.cloned.1.call-start = ((), (), s32[]{:S(2)}) async-start(), calls=%async_computation.5 | async-start | bytes 8650752 | tf_op jit(solution)/shard_map/reduce_scatter | solution.py:36
Sparse Core Ops, SparseCore 0:
  9.6 168.2 all-gather.2
  179.6 26.8 all-gather.4
  218.9 51.6 reduce-scatter.2
  273.0 196.6 reduce-scatter.4
where the time goes:
time: 478 us
  waiting for transfers between devices  403 us (84%)
  matrix products  28.9 us (6%)
  local copies, waits for them, and re-layouts  24.4 us (5%)
  between operations  13.8 us (3%)
  other arithmetic  7.63 us (2%)
    reduce_scatter x1, waiting for transfers between devices, on_device(): lax.psum_scatter(mirror_terms, 'row', scatter_dimension=0, tiled=True)  197 us
    all_gather x1, waiting for transfers between devices, whole_direct(): gathered_second = lax.all_gather(amp_second, 'row', axis=0, tiled=True)  168 us
    reduce_scatter x1, waiting for transfers between devices, on_device(): lax.psum_scatter(direct_terms, 'col', scatter_dimension=0, tiled=True)  36.7 us
    dot_general x1, matrix products, whole_mirror(): jnp.dot(gathered_first, integrals, preferred_element_type=jnp.float32)  15 us
    dot_general x1, matrix products, against(): lax.dot_general(paired, integrals, (((1,), (1,)), ((), ())), preferred_el...  13.9 us
    gather x2, local copies, waits for them, and re-layouts, reorder(): return jnp.take(tiles, order_row, axis=1).reshape(count, block.shape[1])  11.4 us
  transfers between devices with their start and end apart: 4, of which 3 were waited for; matrix products, arithmetic and copies ran while one was open for 12% of the time, Pallas kernels for 0%

commit v1 on v0

v1 whole, which is shorter than its diff:
```python
import functools

import jax
import jax.numpy as jnp
from jax import lax
from jax.experimental import pallas as pl
from jax.experimental.pallas import tpu as pltpu
from jax.sharding import PartitionSpec as P

F32, BF16 = jnp.float32, jnp.bfloat16
TILE = 256
OCC, NA_D, NB_D, CT = 512, 2048, 4096, 16
TN = 512
HALF = NB_D // 2
VMEM_LIMIT = 28 * 2**20


def exchange_pairs(y=0, z=0, xl=0, xh=0, core=0):
    row_flip = y * 8 + z * 2 + xl
    col_flip = xh * 2 + core
    return [
        (row * 4 + col, (row ^ row_flip) * 4 + (col ^ col_flip))
        for row in range(32)
        for col in range(4)
    ]


def swap(value, **flips):
    return lax.ppermute(value, ("row", "col"), exchange_pairs(**flips))


def cost(flops, moved):
    return pl.CostEstimate(flops=flops, bytes_accessed=moved, transcendentals=0)


def call(kernel, grid, scalars, operands, in_specs, outs, scratch, flops, name):
    out_specs = [spec for spec, _ in outs]
    out_shape = [shape for _, shape in outs]
    moved = sum(a.size * a.dtype.itemsize for a in operands) + sum(
        s.size * s.dtype.itemsize for s in out_shape
    )
    return pl.pallas_call(
        kernel,
        grid_spec=pltpu.PrefetchScalarGridSpec(
            num_scalar_prefetch=1,
            grid=grid,
            in_specs=in_specs,
            out_specs=out_specs,
            scratch_shapes=scratch,
        ),
        out_shape=out_shape,
        compiler_params=pltpu.CompilerParams(vmem_limit_bytes=VMEM_LIMIT),
        cost_estimate=cost(flops, moved),
        name=name,
    )(scalars, *operands)


def whole(shape):
    return pl.BlockSpec(shape, lambda i, s: (0,) * len(shape))


def mirror_kernel(y_first, start, s_ref, f0, f1, f2, f3, i_ref, o0, o1, o2, o3, lhs):
    y_col, z_xl = s_ref[0], s_ref[1]

    @pl.when(pl.program_id(0) == 0)
    def _():
        for rel_col, f in enumerate((f0, f1, f2, f3)):
            rel_y = rel_col ^ y_col
            for zx in range(8):
                rel = zx ^ z_xl
                if y_first:
                    slot = rel_y * 8 + rel
                else:
                    slot = ((rel >> 1) * 4 + rel_y) * 2 + (rel & 1)
                lhs[pl.ds(pl.multiple_of(slot * 16, 16), 16), :] = f[zx * 16 : zx * 16 + 16]

    column = pl.multiple_of(start + pl.program_id(0) * TN, TN)
    sums = jnp.dot(lhs[...], i_ref[:, pl.ds(column, TN)], preferred_element_type=F32)
    for k, o in enumerate((o0, o1, o2, o3)):
        o[...] = sums[k * 128 : k * 128 + 128]


def mirror(scalars, firsts, integrals, y_first, start):
    out = (pl.BlockSpec((128, TN), lambda i, s: (0, i)), jax.ShapeDtypeStruct((128, HALF), F32))
    return call(
        functools.partial(mirror_kernel, y_first, start),
        (HALF // TN,),
        scalars,
        (*firsts, integrals),
        [whole((128, NA_D))] * 4 + [pl.BlockSpec(memory_space=pltpu.VMEM)],
        [out] * 4,
        [pltpu.VMEM((OCC, NA_D), BF16)],
        2 * OCC * NA_D * HALF,
        "mirror_p" if y_first else "mirror_q",
    )


def direct_kernel(n_in, layout, s_ref, *refs):
    ins, i_ref, keep, send, lhs = refs[:n_in], refs[n_in], refs[-3], refs[-2], refs[-1]
    y_col = s_ref[0]

    @pl.when(pl.program_id(0) == 0)
    def _():
        for source, first, rel_z, rel_y in layout:
            slot = (rel_y ^ y_col) * 2 + rel_z
            rows = pl.ds(pl.multiple_of(slot * 32, 32), 32)
            for k in range(CT):
                tile = pl.multiple_of(s_ref[2 + k] * TILE, TILE)
                lhs[rows, k * TILE : (k + 1) * TILE] = ins[source][
                    first : first + 32, pl.ds(tile, TILE)
                ]

    row = pl.multiple_of(pl.program_id(0) * TN, TN)
    sums = lax.dot_general(
        lhs[...], i_ref[pl.ds(row, TN), :], (((1,), (1,)), ((), ())), preferred_element_type=F32
    )
    keep[0:64] = sums[0:64]
    send[0:64] = sums[64:128]
    keep[64:128] = sums[128:192]
    send[64:128] = sums[192:256]


def direct(scalars, blocks, layout, integrals, name):
    out = (pl.BlockSpec((128, TN), lambda i, s: (0, i)), jax.ShapeDtypeStruct((128, NA_D), F32))
    return call(
        functools.partial(direct_kernel, len(blocks), layout),
        (NA_D // TN,),
        scalars,
        (*blocks, integrals),
        [whole(b.shape) for b in blocks] + [pl.BlockSpec(memory_space=pltpu.VMEM)],
        [out] * 2,
        [pltpu.VMEM((256, NB_D), BF16)],
        2 * 256 * NA_D * NB_D,
        name,
    )


def sum_kernel(n_in, rows, s_ref, *refs):
    ins, outs = refs[:n_in], refs[n_in:]
    for k, o in enumerate(outs):
        part = slice(k * rows, k * rows + rows)
        total = ins[0][part]
        for other in ins[1:]:
            total = total + other[part]
        o[...] = total


def add_split(scalars, parts, rows, name):
    height, width = parts[0].shape
    count = height // rows
    return call(
        functools.partial(sum_kernel, len(parts), rows),
        (width // TN,),
        scalars,
        parts,
        [pl.BlockSpec((height, TN), lambda i, s: (0, i))] * len(parts),
        [(pl.BlockSpec((rows, TN), lambda i, s: (0, i)), jax.ShapeDtypeStruct((rows, width), F32))]
        * count,
        [],
        0,
        name,
    )


def finish_kernel(s_ref, k0, r0, k1, r1, o_ref):
    z_xl = s_ref[1]
    for chunk, (k, r) in enumerate(((k0, r0), (k1, r1))):
        for part in range(4):
            rel = FINISH_Z[chunk][part // 2] * 2 + part % 2
            rows = pl.ds(pl.multiple_of((rel ^ z_xl) * 16, 16), 16)
            own = slice(part * 16, part * 16 + 16)
            o_ref[rows, :] = (k[own] + r[own]).astype(BF16)


FINISH_Z = ((0, 1), (3, 2))


def finish_first(scalars, parts):
    return call(
        finish_kernel,
        (NA_D // TN,),
        scalars,
        parts,
        [pl.BlockSpec((64, TN), lambda i, s: (0, i))] * 4,
        [(pl.BlockSpec((128, TN), lambda i, s: (0, i)), jax.ShapeDtypeStruct((128, NA_D), BF16))],
        [],
        0,
        "finish_first",
    )[0]


def on_device(amp_first, amp_second, integrals, tile_order):
    row, col = lax.axis_index("row"), lax.axis_index("col")
    place = jnp.stack([(row // 8) ^ col, row % 8]).astype(jnp.int32)
    scalars = jnp.concatenate([place, tile_order[0]])

    other = swap(amp_second, xl=1)
    first_core = swap(amp_first, core=1)
    first_xh = swap(amp_first, xh=1)
    block = jnp.concatenate([amp_second, other])
    by_z = [block] + [swap(block, z=r) for r in (1, 2, 3)]
    by_y = [swap(block, y=r) for r in (1, 2, 3)]
    first_both = swap(first_xh, core=1)
    firsts = (amp_first, first_core, first_xh, first_both)
    rest = jnp.concatenate(by_y)
    rest_z = [rest] + [swap(rest, z=r) for r in (1, 2, 3)]

    p = mirror(scalars, firsts, integrals, True, 0)
    q = mirror(scalars, firsts, integrals, False, HALF)
    p = [p[0]] + [swap(p[r], y=r) for r in (1, 2, 3)]
    q = [q[0]] + [swap(q[r], z=r) for r in (1, 2, 3)]
    p = add_split(scalars, p, 32, "sum_p")
    q = add_split(scalars, q, 32, "sum_q")
    p = [p[0]] + [swap(p[r], z=r) for r in (1, 2, 3)]
    q = [q[0]] + [swap(q[r], y=r) for r in (1, 2, 3)]
    p = add_split(scalars, p, 16, "last_p")
    q = add_split(scalars, q, 16, "last_q")
    p = (p[0] + swap(p[1], xl=1)).astype(BF16)
    q = (q[0] + swap(q[1], xl=1)).astype(BF16)
    ladder_second = jnp.concatenate([p, q], axis=1)

    ends = []
    for chunk, zs in enumerate(FINISH_Z):
        blocks, layout = [], []
        for zi, z in enumerate(zs):
            layout.append((len(blocks), 0, zi, 0))
            layout += [(len(blocks) + 1, (y - 1) * 32, zi, y) for y in (1, 2, 3)]
            blocks += [by_z[z], rest_z[z]]
        keep, send = direct(scalars, blocks, layout, integrals, f"direct_{chunk}")
        keep, send = add_split(scalars, (keep, swap(send, core=1)), 64, f"core_{chunk}")
        ends += [keep, swap(send, xh=1)]
    ladder_first = finish_first(scalars, ends)
    return ladder_first, ladder_second


def solution(mesh):
    in_specs = (P("col", "row"), P("row", "col"), P("row", "col"), P("col", None))
    out_specs = (P("col", "row"), P("row", "col"))
    return jax.shard_map(
        on_device, mesh=mesh, in_specs=in_specs, out_specs=out_specs, check_vma=False
    )
```

time: 478 us -> 170 us (0.36)
  waiting for transfers between devices: 403 us -> 71.4 us
  starting transfers between devices: 0.16 us -> 48.7 us
  Pallas kernels: 0 us -> 33.5 us
  matrix products: 28.9 us -> 0 us
  between operations: 13.8 us -> 0.81 us
  local copies, waits for them, and re-layouts: 24.4 us -> 13.6 us
  other arithmetic: 7.63 us -> 1.43 us
    reduce_scatter x2 -> x0, waiting for transfers between devices: 234 us -> none  [the longest x1 197 us: on_device(): lax.psum_scatter(mirror_terms, 'row', scatter_dimension=0, tiled=True)]
    all_gather x2 -> x0, waiting for transfers between devices: 168 us -> none  [the longest x1 168 us: whole_direct(): gathered_second = lax.all_gather(amp_second, 'row', axis=0, tiled=True)]
    ppermute x0 -> x31, waiting for transfers between devices: none -> 71.4 us  [swap(): return lax.ppermute(value, ('row', 'col'), exchange_pairs(**flips))]
    ppermute x0 -> x31, starting transfers between devices: none -> 48.7 us  [swap(): return lax.ppermute(value, ('row', 'col'), exchange_pairs(**flips))]
    pallas_call x0 -> x11, Pallas kernels: none -> 33.5 us  [call(): pl.pallas_call(kernel, grid_spec=pltpu.PrefetchScalarGridSpec(num_scalar_...]
    dot_general x2 -> x0, matrix products: 28.9 us -> none  [the longest x1 15 us: whole_mirror(): jnp.dot(gathered_first, integrals, preferred_element_type=jnp.float32)]
    unnamed x0 -> x9, local copies, waits for them, and re-layouts: none -> 13.6 us
    gather x2 -> x0, local copies, waits for them, and re-layouts: 11.4 us -> none  [reorder(): return jnp.take(tiles, order_row, axis=1).reshape(count, block.shape[1])]
  transfers between devices with their start and end apart: 4 -> 31, of which waited for: 3 -> 12; matrix products, arithmetic and copies ran while one was open for 12% -> 1% of each run, Pallas kernels for 0% -> 19%
where the time goes in v1:
time: 170 us; the launch traced here: 169 us
  waiting for transfers between devices  71.4 us (42%)
  starting transfers between devices  48.7 us (29%)
  Pallas kernels  33.5 us (20%)
  local copies, waits for them, and re-layouts  13.6 us (8%)
    ppermute x31, waiting for transfers between devices, swap(): return lax.ppermute(value, ('row', 'col'), exchange_pairs(**flips))  71.4 us
    ppermute x31, starting transfers between devices, swap(): return lax.ppermute(value, ('row', 'col'), exchange_pairs(**flips))  48.7 us
    pallas_call x11, Pallas kernels, call(): pl.pallas_call(kernel, grid_spec=pltpu.PrefetchScalarGridSpec(num_scalar_...  33.5 us
    unnamed x9, local copies, waits for them, and re-layouts  13.6 us
  transfers between devices with their start and end apart: 31, of which 12 were waited for; matrix products, arithmetic and copies ran while one was open for 1% of the time, Pallas kernels for 19%

profile of v1, /device:TPU:0, one launch (start us, length us, event | category | flops | bytes accessed | tf_op | source)
XLA Modules:
  0.0 169.5 jit_solution(13786657092953039853)
XLA Ops:
  0.6 1.7 collective-permute-start
  2.3 0.9 constant_dynamic-update-slice_fusion.1
  3.2 2.8 %collective-permute-done = bf16[16,4096]{1,0:T(8,128)(2,1)S(1)} collective-permute-done((bf16[16,4096]{1,0:T(8,128)(2,1)}, bf16[16,4096]{1,0:T(8,128)(2,1)S(1)}, u32[]{:S(2)}, u32[]{:S(2)}) %collective-permute-start) | collective-permute-done | bytes 131104 | tf_op jit(solution)/shard_map/ppermute | solution.py:29
  6.0 1.9 %collective-permute-start.1 = (bf16[32,4096]{1,0:T(8,128)(2,1)S(1)}, bf16[32,4096]{1,0:T(8,128)(2,1)S(1)}, u32[]{:S(2)}, u32[]{:S(2)}) collective-permute-start(bf16[32,4096]{1,0:T(8,128)(2,1)S(1)} %constant_dynamic-update-slice_fusion.refs_0_), channel_id=1, source_target_pairs={{0,32},{1,33},{2,34},{3,35},{4,36},{5,37},{6,38},{7,39},{8,40},{9,... | collective-permute-start | bytes 786440 | tf_op jit(solution)/shard_map/ppermute | solution.py:29
  7.9 3.0 %collective-permute-start.15 = (bf16[128,2048]{1,0:T(8,128)(2,1)}, bf16[128,2048]{1,0:T(8,128)(2,1)S(1)}, u32[]{:S(2)}, u32[]{:S(2)}) collective-permute-start(bf16[128,2048]{1,0:T(8,128)(2,1)} %f0.3), channel_id=1, source_target_pairs={{0,2},{1,3},{2,0},{3,1},{4,6},{5,7},{6,4},{7,5},{8,10},{9,11},{10,... | collective-permute-start | bytes 1572872 | tf_op jit(solution)/shard_map/ppermute | solution.py:29
  10.9 0.0 collective-permute-start.14
  10.9 0.7 pad_add_fusion.s_ref
  11.7 2.9 %collective-permute-start.2 = (bf16[32,4096]{1,0:T(8,128)(2,1)S(1)}, bf16[32,4096]{1,0:T(8,128)(2,1)S(1)}, u32[]{:S(2)}, u32[]{:S(2)}) collective-permute-start(bf16[32,4096]{1,0:T(8,128)(2,1)S(1)} %constant_dynamic-update-slice_fusion.refs_0_), channel_id=1, source_target_pairs={{0,64},{1,65},{2,66},{3,67},{4,68},{5,69},{6,70},{7,71},{8,72},{9,... | collective-permute-start | bytes 786440 | tf_op jit(solution)/shard_map/ppermute | solution.py:29
  14.6 0.2 collective-permute-start.3
  14.8 0.0 collective-permute-done.1
  14.8 3.9 %collective-permute-start.10 = (bf16[32,4096]{1,0:T(8,128)(2,1)S(1)}, bf16[32,4096]{1,0:T(8,128)(2,1)S(1)}, u32[]{:S(2)}, u32[]{:S(2)}) collective-permute-start(bf16[32,4096]{1,0:T(8,128)(2,1)S(1)} %constant_dynamic-update-slice_fusion.refs_0_), channel_id=1, source_target_pairs={{0,16},{1,17},{2,18},{3,19},{4,20},{5,21},{6,22},{7,23},{8,24},{9,... | collective-permute-start | bytes 786440 | tf_op jit(solution)/shard_map/ppermute | solution.py:29
  18.7 3.3 %collective-permute-done.2 = bf16[32,4096]{1,0:T(8,128)(2,1)S(1)} collective-permute-done((bf16[32,4096]{1,0:T(8,128)(2,1)S(1)}, bf16[32,4096]{1,0:T(8,128)(2,1)S(1)}, u32[]{:S(2)}, u32[]{:S(2)}) %collective-permute-start.2) | collective-permute-done | bytes 262176 | tf_op jit(solution)/shard_map/ppermute | solution.py:29
  22.0 4.0 %collective-permute-start.8 = (bf16[32,4096]{1,0:T(8,128)(2,1)S(1)}, bf16[32,4096]{1,0:T(8,128)(2,1)S(1)}, u32[]{:S(2)}, u32[]{:S(2)}) collective-permute-start(bf16[32,4096]{1,0:T(8,128)(2,1)S(1)} %constant_dynamic-update-slice_fusion.refs_0_), channel_id=1, source_target_pairs={{0,24},{1,25},{2,26},{3,27},{4,28},{5,29},{6,30},{7,31},{8,16},{9,... | collective-permute-start | bytes 786440 | tf_op jit(solution)/shard_map/ppermute | solution.py:29
  26.0 0.0 collective-permute-done.15.f2
  26.0 0.0 collective-permute-start.16
  26.1 1.4 collective-permute-done.3
  27.5 4.0 %collective-permute-start.11 = (bf16[96,4096]{1,0:T(8,128)(2,1)S(1)}, bf16[96,4096]{1,0:T(8,128)(2,1)S(1)}, u32[]{:S(2)}, u32[]{:S(2)}) collective-permute-start(bf16[96,4096]{1,0:T(8,128)(2,1)S(1)} %constant_dynamic-update-slice_fusion.2.refs_1_), channel_id=1, source_target_pairs={{0,16},{1,17},{2,18},{3,19},{4,20},{5,21},{6,22},{7,23},{8,24},{9,... | collective-permute-start | bytes 2359304 | tf_op jit(solution)/shard_map/ppermute | solution.py:29
  31.5 0.0 collective-permute-done.14.f1
  31.5 0.0 collective-permute-done.16.f3
  31.5 5.8 %copy-done = bf16[2048,4096]{1,0:T(8,128)(2,1)S(1)} copy-done((bf16[2048,4096]{1,0:T(8,128)(2,1)S(1)}, bf16[2048,4096]{1,0:T(8,128)(2,1)}, u32[]{:S(2)}) %copy-start) | copy-done | bytes 16777240
  37.3 1.0 copy-done.2
  38.3 6.2 %mirror_p.1 = (f32[128,2048]{1,0:T(8,128)S(1)}, f32[128,2048]{1,0:T(8,128)S(1)}, f32[128,2048]{1,0:T(8,128)S(1)}, f32[128,2048]{1,0:T(8,128)S(1)}) custom-call(s32[18]{0:T(128)S(1)} %pad_add_fusion.s_ref, bf16[128,2048]{1,0:T(8,128)(2,1)S(1)} %copy-done.2, bf16[128,2048]{1,0:T(8,128)(2,1)S(1)} %collective-permute-done.14.f1, ...), custom_call_target="tpu_custom_call" | custom-call | flops 4294967296 | bytes 23068672 | tf_op jit(solution)/shard_map/mirror_p/pallas_call | solution.py:42
  44.5 0.5 collective-permute-start.17
  45.0 1.0 collective-permute-start.4
  46.1 1.1 collective-permute-start.5
  47.2 9.4 %collective-permute-done.4.refs_2_ = bf16[32,4096]{1,0:T(8,128)(2,1)S(1)} collective-permute-done((bf16[32,4096]{1,0:T(8,128)(2,1)S(1)}, bf16[32,4096]{1,0:T(8,128)(2,1)S(1)}, u32[]{:S(2)}, u32[]{:S(2)}) %collective-permute-start.4) | collective-permute-done | bytes 262176 | tf_op jit(solution)/shard_map/ppermute | solution.py:29
  56.5 1.0 collective-permute-start.18
  57.5 2.1 %collective-permute-start.19 = (f32[128,2048]{1,0:T(8,128)S(1)}, f32[128,2048]{1,0:T(8,128)S(1)}, u32[]{:S(2)}, u32[]{:S(2)}) collective-permute-start(f32[128,2048]{1,0:T(8,128)S(1)} %get-tuple-element.41), channel_id=1, source_target_pairs={{0,96},{1,97},{2,98},{3,99},{4,100},{5,101},{6,102},{7,103},{8,104... | collective-permute-start | bytes 3145736 | tf_op jit(solution)/shard_map/ppermute | solution.py:29
  59.6 7.0 %mirror_q.1 = (f32[128,2048]{1,0:T(8,128)S(1)}, f32[128,2048]{1,0:T(8,128)S(1)}, f32[128,2048]{1,0:T(8,128)}, f32[128,2048]{1,0:T(8,128)}) custom-call(s32[18]{0:T(128)S(1)} %pad_add_fusion.s_ref, bf16[128,2048]{1,0:T(8,128)(2,1)S(1)} %copy-done.2, bf16[128,2048]{1,0:T(8,128)(2,1)S(1)} %collective-permute-done.14.f1, ...), custom_call_target="tpu_custom_call" | custom-call | flops 4294967296 | bytes 23068672 | tf_op jit(solution)/shard_map/mirror_q/pallas_call | solution.py:42
  66.6 1.0 collective-permute-start.24
  67.6 5.8 %collective-permute-done.5.refs_3_ = bf16[96,4096]{1,0:T(8,128)(2,1)S(1)} collective-permute-done((bf16[96,4096]{1,0:T(8,128)(2,1)S(1)}, bf16[96,4096]{1,0:T(8,128)(2,1)S(1)}, u32[]{:S(2)}, u32[]{:S(2)}) %collective-permute-start.5) | collective-permute-done | bytes 786464 | tf_op jit(solution)/shard_map/ppermute | solution.py:29
  73.4 1.1 collective-permute-start.25
  74.5 0.0 collective-permute-done.17.refs_1_
  74.5 2.6 %collective-permute-start.26 = (f32[128,2048]{1,0:T(8,128)}, f32[128,2048]{1,0:T(8,128)S(1)}, u32[]{:S(2)}, u32[]{:S(2)}) collective-permute-start(f32[128,2048]{1,0:T(8,128)} %get-tuple-element.51), channel_id=1, source_target_pairs={{0,24},{1,25},{2,26},{3,27},{4,28},{5,29},{6,30},{7,31},{8,16},{9,... | collective-permute-start | bytes 3145736 | tf_op jit(solution)/shard_map/ppermute | solution.py:29
  77.1 6.2 %direct_1.1 = (f32[128,2048]{1,0:T(8,128)S(1)}, f32[128,2048]{1,0:T(8,128)S(1)}) custom-call(s32[18]{0:T(128)S(1)} %pad_add_fusion.s_ref, bf16[32,4096]{1,0:T(8,128)(2,1)S(1)} %collective-permute-done.8.refs_0_, bf16[96,4096]{1,0:T(8,128)(2,1)S(1)} %collective-permute-done.9.refs_1_, bf16[32,4096]{1,0:T(8,128)(2,1)S(1)} %collective-permute-done.10.refs_2_, ...), custom_call_target="tpu_custom_call" | custom-call | flops 4294967296 | bytes 20971520 | tf_op jit(solution)/shard_map/direct_1/pallas_call | solution.py:42
  83.3 10.3 %collective-permute-done.18.refs_2_ = f32[128,2048]{1,0:T(8,128)S(1)} collective-permute-done((f32[128,2048]{1,0:T(8,128)S(1)}, f32[128,2048]{1,0:T(8,128)S(1)}, u32[]{:S(2)}, u32[]{:S(2)}) %collective-permute-start.18) | collective-permute-done | bytes 1048608 | tf_op jit(solution)/shard_map/ppermute | solution.py:29
  93.6 5.8 %copy-done.1 = bf16[2048,4096]{1,0:T(8,128)(2,1)S(1)} copy-done((bf16[2048,4096]{1,0:T(8,128)(2,1)S(1)}, bf16[2048,4096]{1,0:T(8,128)(2,1)}, u32[]{:S(2)}) %copy-start.1) | copy-done | bytes 16777240
  99.4 6.2 %direct_0.1 = (f32[128,2048]{1,0:T(8,128)S(1)}, f32[128,2048]{1,0:T(8,128)S(1)}) custom-call(s32[18]{0:T(128)S(1)} %pad_add_fusion.s_ref, bf16[32,4096]{1,0:T(8,128)(2,1)S(1)} %constant_dynamic-update-slice_fusion.refs_0_, bf16[96,4096]{1,0:T(8,128)(2,1)S(1)} %constant_dynamic-update-slice_fusion.2.refs_1_, ...), custom_call_target="tpu_custom_call" | custom-call | flops 4294967296 | bytes 20971520 | tf_op jit(solution)/shard_map/direct_0/pallas_call | solution.py:42
  105.6 0.6 collective-permute-start.6
  106.2 1.2 sum_p.1
  107.4 0.0 collective-permute-done.24.refs_1_
  107.4 1.1 collective-permute-start.20
  108.5 9.0 %collective-permute-done.25.refs_2_ = f32[128,2048]{1,0:T(8,128)S(1)} collective-permute-done((f32[128,2048]{1,0:T(8,128)}, f32[128,2048]{1,0:T(8,128)S(1)}, u32[]{:S(2)}, u32[]{:S(2)}) %collective-permute-start.25) | collective-permute-done | bytes 1048608 | tf_op jit(solution)/shard_map/ppermute | solution.py:29
  117.5 3.4 %collective-permute-start.21 = (f32[32,2048]{1,0:T(8,128)S(1)}, f32[32,2048]{1,0:T(8,128)S(1)}, u32[]{:S(2)}, u32[]{:S(2)}) collective-permute-start(f32[32,2048]{1,0:T(8,128)S(1)} %get-tuple-element.44), channel_id=1, source_target_pairs={{0,16},{1,17},{2,18},{3,19},{4,20},{5,21},{6,22},{7,23},{8,24},{9,... | collective-permute-start | bytes 786440 | tf_op jit(solution)/shard_map/ppermute | solution.py:29
  120.9 0.6 collective-permute-done.26.refs_3_
  121.5 2.6 %collective-permute-start.22 = (f32[32,2048]{1,0:T(8,128)S(1)}, f32[32,2048]{1,0:T(8,128)S(1)}, u32[]{:S(2)}, u32[]{:S(2)}) collective-permute-start(f32[32,2048]{1,0:T(8,128)S(1)} %get-tuple-element.45), channel_id=1, source_target_pairs={{0,24},{1,25},{2,26},{3,27},{4,28},{5,29},{6,30},{7,31},{8,16},{9,... | collective-permute-start | bytes 786440 | tf_op jit(solution)/shard_map/ppermute | solution.py:29
  124.0 1.2 sum_q.1
  125.3 0.5 collective-permute-start.27
  125.8 2.3 %collective-permute-done.21.refs_2_ = f32[32,2048]{1,0:T(8,128)S(1)} collective-permute-done((f32[32,2048]{1,0:T(8,128)S(1)}, f32[32,2048]{1,0:T(8,128)S(1)}, u32[]{:S(2)}, u32[]{:S(2)}) %collective-permute-start.21) | collective-permute-done | bytes 262176 | tf_op jit(solution)/shard_map/ppermute | solution.py:29
  128.0 1.4 collective-permute-start.28
  129.4 4.0 %collective-permute-done.22.refs_3_ = f32[32,2048]{1,0:T(8,128)S(1)} collective-permute-done((f32[32,2048]{1,0:T(8,128)S(1)}, f32[32,2048]{1,0:T(8,128)S(1)}, u32[]{:S(2)}, u32[]{:S(2)}) %collective-permute-start.22) | collective-permute-done | bytes 262176 | tf_op jit(solution)/shard_map/ppermute | solution.py:29
  133.4 2.2 %collective-permute-start.29 = (f32[32,2048]{1,0:T(8,128)S(1)}, f32[32,2048]{1,0:T(8,128)S(1)}, u32[]{:S(2)}, u32[]{:S(2)}) collective-permute-start(f32[32,2048]{1,0:T(8,128)S(1)} %get-tuple-element.55), channel_id=1, source_target_pairs={{0,96},{1,97},{2,98},{3,99},{4,100},{5,101},{6,102},{7,103},{8,104... | collective-permute-start | bytes 786440 | tf_op jit(solution)/shard_map/ppermute | solution.py:29
  135.5 0.8 last_p.1
  136.4 0.7 collective-permute-start.23
  137.0 1.0 core_1.1
  138.0 2.1 %collective-permute-start.13 = (f32[64,2048]{1,0:T(8,128)S(1)}, f32[64,2048]{1,0:T(8,128)S(1)}, u32[]{:S(2)}, u32[]{:S(2)}) collective-permute-start(f32[64,2048]{1,0:T(8,128)S(1)} %get-tuple-element.37), channel_id=1, source_target_pairs={{0,2},{1,3},{2,0},{3,1},{4,6},{5,7},{6,4},{7,5},{8,10},{9,11},{10,... | collective-permute-start | bytes 1572872 | tf_op jit(solution)/shard_map/ppermute | solution.py:29
  140.1 1.0 core_0.1
  141.1 1.6 collective-permute-start.7
  142.7 1.9 %collective-permute-done.29.refs_3_ = f32[32,2048]{1,0:T(8,128)S(1)} collective-permute-done((f32[32,2048]{1,0:T(8,128)S(1)}, f32[32,2048]{1,0:T(8,128)S(1)}, u32[]{:S(2)}, u32[]{:S(2)}) %collective-permute-start.29) | collective-permute-done | bytes 262176 | tf_op jit(solution)/shard_map/ppermute | solution.py:29
  144.6 0.8 last_q.1
  145.4 0.7 collective-permute-start.30
  146.1 20.6 %collective-permute-done.30 = f32[16,2048]{1,0:T(8,128)S(1)} collective-permute-done((f32[16,2048]{1,0:T(8,128)S(1)}, f32[16,2048]{1,0:T(8,128)S(1)}, u32[]{:S(2)}, u32[]{:S(2)}) %collective-permute-start.30) | collective-permute-done | bytes 131104 | tf_op jit(solution)/shard_map/ppermute | solution.py:29
  166.7 0.7 pad_maximum_fusion
  167.4 2.1 %finish_first.1 = bf16[128,2048]{1,0:T(8,128)(2,1)} custom-call(s32[18]{0:T(128)S(1)} %pad_add_fusion.s_ref, f32[64,2048]{1,0:T(8,128)S(1)} %get-tuple-element.32.k0, f32[64,2048]{1,0:T(8,128)S(1)} %collective-permute-done.7.r0, f32[64,2048]{1,0:T(8,128)S(1)} %get-tuple-element.36.k1, f32[64,2048]{1,0:T(8,128)S(1)} %collective-permute-done.13.r1), custom_call_target="tpu_custom_call" | custom-call | bytes 2621440 | tf_op jit(solution)/shard_map/finish_first/pallas_call | solution.py:42
  (24 shorter events, 0.1 us)
Async XLA Ops:
  0.6 5.4 %collective-permute-start = (bf16[16,4096]{1,0:T(8,128)(2,1)}, bf16[16,4096]{1,0:T(8,128)(2,1)S(1)}, u32[]{:S(2)}, u32[]{:S(2)}) collective-permute-start(bf16[16,4096]{1,0:T(8,128)(2,1)} %param.5), channel_id=1, source_target_pairs={{0,4},{1,5},{2,6},{3,7},{4,0},{5,1},{6,2},{7,3},{8,12},{9,13},{10,... | collective-permute-start | bytes 393224 | tf_op jit(solution)/shard_map/ppermute | solution.py:29
  6.0 8.8 %collective-permute-start.1 = (bf16[32,4096]{1,0:T(8,128)(2,1)S(1)}, bf16[32,4096]{1,0:T(8,128)(2,1)S(1)}, u32[]{:S(2)}, u32[]{:S(2)}) collective-permute-start(bf16[32,4096]{1,0:T(8,128)(2,1)S(1)} %constant_dynamic-update-slice_fusion.refs_0_), channel_id=1, source_target_pairs={{0,32},{1,33},{2,34},{3,35},{4,36},{5,37},{6,38},{7,39},{8,40},{9,... | collective-permute-start | bytes 786440 | tf_op jit(solution)/shard_map/ppermute | solution.py:29
  7.9 18.1 %collective-permute-start.15 = (bf16[128,2048]{1,0:T(8,128)(2,1)}, bf16[128,2048]{1,0:T(8,128)(2,1)S(1)}, u32[]{:S(2)}, u32[]{:S(2)}) collective-permute-start(bf16[128,2048]{1,0:T(8,128)(2,1)} %f0.3), channel_id=1, source_target_pairs={{0,2},{1,3},{2,0},{3,1},{4,6},{5,7},{6,4},{7,5},{8,10},{9,11},{10,... | collective-permute-start | bytes 1572872 | tf_op jit(solution)/shard_map/ppermute | solution.py:29
  10.9 20.6 %collective-permute-start.14 = (bf16[128,2048]{1,0:T(8,128)(2,1)}, bf16[128,2048]{1,0:T(8,128)(2,1)S(1)}, u32[]{:S(2)}, u32[]{:S(2)}) collective-permute-start(bf16[128,2048]{1,0:T(8,128)(2,1)} %f0.3), channel_id=1, source_target_pairs={{0,1},{1,0},{2,3},{3,2},{4,5},{5,4},{6,7},{7,6},{8,9},{9,8},{10,11... | collective-permute-start | bytes 1572872 | tf_op jit(solution)/shard_map/ppermute | solution.py:29
  11.7 10.3 %collective-permute-start.2 = (bf16[32,4096]{1,0:T(8,128)(2,1)S(1)}, bf16[32,4096]{1,0:T(8,128)(2,1)S(1)}, u32[]{:S(2)}, u32[]{:S(2)}) collective-permute-start(bf16[32,4096]{1,0:T(8,128)(2,1)S(1)} %constant_dynamic-update-slice_fusion.refs_0_), channel_id=1, source_target_pairs={{0,64},{1,65},{2,66},{3,67},{4,68},{5,69},{6,70},{7,71},{8,72},{9,... | collective-permute-start | bytes 786440 | tf_op jit(solution)/shard_map/ppermute | solution.py:29
  14.6 12.9 %collective-permute-start.3 = (bf16[32,4096]{1,0:T(8,128)(2,1)S(1)}, bf16[32,4096]{1,0:T(8,128)(2,1)S(1)}, u32[]{:S(2)}, u32[]{:S(2)}) collective-permute-start(bf16[32,4096]{1,0:T(8,128)(2,1)S(1)} %constant_dynamic-update-slice_fusion.refs_0_), channel_id=1, source_target_pairs={{0,96},{1,97},{2,98},{3,99},{4,100},{5,101},{6,102},{7,103},{8,104... | collective-permute-start | bytes 786440 | tf_op jit(solution)/shard_map/ppermute | solution.py:29
  14.8 31.2 %collective-permute-start.10 = (bf16[32,4096]{1,0:T(8,128)(2,1)S(1)}, bf16[32,4096]{1,0:T(8,128)(2,1)S(1)}, u32[]{:S(2)}, u32[]{:S(2)}) collective-permute-start(bf16[32,4096]{1,0:T(8,128)(2,1)S(1)} %constant_dynamic-update-slice_fusion.refs_0_), channel_id=1, source_target_pairs={{0,16},{1,17},{2,18},{3,19},{4,20},{5,21},{6,22},{7,23},{8,24},{9,... | collective-permute-start | bytes 786440 | tf_op jit(solution)/shard_map/ppermute | solution.py:29
  22.0 24.1 %collective-permute-start.8 = (bf16[32,4096]{1,0:T(8,128)(2,1)S(1)}, bf16[32,4096]{1,0:T(8,128)(2,1)S(1)}, u32[]{:S(2)}, u32[]{:S(2)}) collective-permute-start(bf16[32,4096]{1,0:T(8,128)(2,1)S(1)} %constant_dynamic-update-slice_fusion.refs_0_), channel_id=1, source_target_pairs={{0,24},{1,25},{2,26},{3,27},{4,28},{5,29},{6,30},{7,31},{8,16},{9,... | collective-permute-start | bytes 786440 | tf_op jit(solution)/shard_map/ppermute | solution.py:29
  26.0 5.5 %collective-permute-start.16 = (bf16[128,2048]{1,0:T(8,128)(2,1)S(1)}, bf16[128,2048]{1,0:T(8,128)(2,1)S(1)}, u32[]{:S(2)}, u32[]{:S(2)}) collective-permute-start(bf16[128,2048]{1,0:T(8,128)(2,1)S(1)} %collective-permute-done.15.f2), channel_id=1, source_target_pairs={{0,1},{1,0},{2,3},{3,2},{4,5},{5,4},{6,7},{7,6},{8,9},{9,8},{10,11... | collective-permute-start | bytes 1572872 | tf_op jit(solution)/shard_map/ppermute | solution.py:29
  27.5 30.0 %collective-permute-start.11 = (bf16[96,4096]{1,0:T(8,128)(2,1)S(1)}, bf16[96,4096]{1,0:T(8,128)(2,1)S(1)}, u32[]{:S(2)}, u32[]{:S(2)}) collective-permute-start(bf16[96,4096]{1,0:T(8,128)(2,1)S(1)} %constant_dynamic-update-slice_fusion.2.refs_1_), channel_id=1, source_target_pairs={{0,16},{1,17},{2,18},{3,19},{4,20},{5,21},{6,22},{7,23},{8,24},{9,... | collective-permute-start | bytes 2359304 | tf_op jit(solution)/shard_map/ppermute | solution.py:29
  31.5 5.8 %copy-start = (bf16[2048,4096]{1,0:T(8,128)(2,1)S(1)}, bf16[2048,4096]{1,0:T(8,128)(2,1)}, u32[]{:S(2)}) copy-start(bf16[2048,4096]{1,0:T(8,128)(2,1)} %i_ref.3) | copy-start | bytes 50331652
  37.3 1.0 copy-start.2
  44.5 30.0 %collective-permute-start.17 = (f32[128,2048]{1,0:T(8,128)S(1)}, f32[128,2048]{1,0:T(8,128)S(1)}, u32[]{:S(2)}, u32[]{:S(2)}) collective-permute-start(f32[128,2048]{1,0:T(8,128)S(1)} %get-tuple-element.39), channel_id=1, source_target_pairs={{0,32},{1,33},{2,34},{3,35},{4,36},{5,37},{6,38},{7,39},{8,40},{9,... | collective-permute-start | bytes 3145736 | tf_op jit(solution)/shard_map/ppermute | solution.py:29
  45.0 11.5 %collective-permute-start.4 = (bf16[32,4096]{1,0:T(8,128)(2,1)S(1)}, bf16[32,4096]{1,0:T(8,128)(2,1)S(1)}, u32[]{:S(2)}, u32[]{:S(2)}) collective-permute-start(bf16[32,4096]{1,0:T(8,128)(2,1)S(1)} %constant_dynamic-update-slice_fusion.refs_0_), channel_id=1, source_target_pairs={{0,8},{1,9},{2,10},{3,11},{4,12},{5,13},{6,14},{7,15},{8,0},{9,1},... | collective-permute-start | bytes 786440 | tf_op jit(solution)/shard_map/ppermute | solution.py:29
  46.0 20.5 %collective-permute-start.9 = (bf16[96,4096]{1,0:T(8,128)(2,1)S(1)}, bf16[96,4096]{1,0:T(8,128)(2,1)S(1)}, u32[]{:S(2)}, u32[]{:S(2)}) collective-permute-start(bf16[96,4096]{1,0:T(8,128)(2,1)S(1)} %constant_dynamic-update-slice_fusion.2.refs_1_), channel_id=1, source_target_pairs={{0,24},{1,25},{2,26},{3,27},{4,28},{5,29},{6,30},{7,31},{8,16},{9,... | collective-permute-start | bytes 2359304 | tf_op jit(solution)/shard_map/ppermute | solution.py:29
  46.1 27.3 %collective-permute-start.5 = (bf16[96,4096]{1,0:T(8,128)(2,1)S(1)}, bf16[96,4096]{1,0:T(8,128)(2,1)S(1)}, u32[]{:S(2)}, u32[]{:S(2)}) collective-permute-start(bf16[96,4096]{1,0:T(8,128)(2,1)S(1)} %constant_dynamic-update-slice_fusion.2.refs_1_), channel_id=1, source_target_pairs={{0,8},{1,9},{2,10},{3,11},{4,12},{5,13},{6,14},{7,15},{8,0},{9,1},... | collective-permute-start | bytes 2359304 | tf_op jit(solution)/shard_map/ppermute | solution.py:29
  56.5 37.1 %collective-permute-start.18 = (f32[128,2048]{1,0:T(8,128)S(1)}, f32[128,2048]{1,0:T(8,128)S(1)}, u32[]{:S(2)}, u32[]{:S(2)}) collective-permute-start(f32[128,2048]{1,0:T(8,128)S(1)} %get-tuple-element.40), channel_id=1, source_target_pairs={{0,64},{1,65},{2,66},{3,67},{4,68},{5,69},{6,70},{7,71},{8,72},{9,... | collective-permute-start | bytes 3145736 | tf_op jit(solution)/shard_map/ppermute | solution.py:29
  57.5 48.1 %collective-permute-start.19 = (f32[128,2048]{1,0:T(8,128)S(1)}, f32[128,2048]{1,0:T(8,128)S(1)}, u32[]{:S(2)}, u32[]{:S(2)}) collective-permute-start(f32[128,2048]{1,0:T(8,128)S(1)} %get-tuple-element.41), channel_id=1, source_target_pairs={{0,96},{1,97},{2,98},{3,99},{4,100},{5,101},{6,102},{7,103},{8,104... | collective-permute-start | bytes 3145736 | tf_op jit(solution)/shard_map/ppermute | solution.py:29
  66.6 40.8 %collective-permute-start.24 = (f32[128,2048]{1,0:T(8,128)S(1)}, f32[128,2048]{1,0:T(8,128)S(1)}, u32[]{:S(2)}, u32[]{:S(2)}) collective-permute-start(f32[128,2048]{1,0:T(8,128)S(1)} %get-tuple-element.49), channel_id=1, source_target_pairs={{0,8},{1,9},{2,10},{3,11},{4,12},{5,13},{6,14},{7,15},{8,0},{9,1},... | collective-permute-start | bytes 3145736 | tf_op jit(solution)/shard_map/ppermute | solution.py:29
  73.4 44.1 %collective-permute-start.25 = (f32[128,2048]{1,0:T(8,128)}, f32[128,2048]{1,0:T(8,128)S(1)}, u32[]{:S(2)}, u32[]{:S(2)}) collective-permute-start(f32[128,2048]{1,0:T(8,128)} %get-tuple-element.50), channel_id=1, source_target_pairs={{0,16},{1,17},{2,18},{3,19},{4,20},{5,21},{6,22},{7,23},{8,24},{9,... | collective-permute-start | bytes 3145736 | tf_op jit(solution)/shard_map/ppermute | solution.py:29
  74.5 47.0 %collective-permute-start.26 = (f32[128,2048]{1,0:T(8,128)}, f32[128,2048]{1,0:T(8,128)S(1)}, u32[]{:S(2)}, u32[]{:S(2)}) collective-permute-start(f32[128,2048]{1,0:T(8,128)} %get-tuple-element.51), channel_id=1, source_target_pairs={{0,24},{1,25},{2,26},{3,27},{4,28},{5,29},{6,30},{7,31},{8,16},{9,... | collective-permute-start | bytes 3145736 | tf_op jit(solution)/shard_map/ppermute | solution.py:29
  93.6 42.8 %collective-permute-start.12 = (f32[128,2048]{1,0:T(8,128)S(1)}, f32[128,2048]{1,0:T(8,128)S(1)}, u32[]{:S(2)}, u32[]{:S(2)}) collective-permute-start(f32[128,2048]{1,0:T(8,128)S(1)} %get-tuple-element.35), channel_id=1, source_target_pairs={{0,1},{1,0},{2,3},{3,2},{4,5},{5,4},{6,7},{7,6},{8,9},{9,8},{10,11... | collective-permute-start | bytes 3145736 | tf_op jit(solution)/shard_map/ppermute | solution.py:29
  93.6 5.8 %copy-start.1 = (bf16[2048,4096]{1,0:T(8,128)(2,1)S(1)}, bf16[2048,4096]{1,0:T(8,128)(2,1)}, u32[]{:S(2)}) copy-start(bf16[2048,4096]{1,0:T(8,128)(2,1)} %i_ref.3) | copy-start | bytes 50331652
  105.6 32.5 %collective-permute-start.6 = (f32[128,2048]{1,0:T(8,128)S(1)}, f32[128,2048]{1,0:T(8,128)S(1)}, u32[]{:S(2)}, u32[]{:S(2)}) collective-permute-start(f32[128,2048]{1,0:T(8,128)S(1)} %get-tuple-element.31), channel_id=1, source_target_pairs={{0,1},{1,0},{2,3},{3,2},{4,5},{5,4},{6,7},{7,6},{8,9},{9,8},{10,11... | collective-permute-start | bytes 3145736 | tf_op jit(solution)/shard_map/ppermute | solution.py:29
  107.4 17.9 %collective-permute-start.20 = (f32[32,2048]{1,0:T(8,128)S(1)}, f32[32,2048]{1,0:T(8,128)S(1)}, u32[]{:S(2)}, u32[]{:S(2)}) collective-permute-start(f32[32,2048]{1,0:T(8,128)S(1)} %get-tuple-element.43), channel_id=1, source_target_pairs={{0,8},{1,9},{2,10},{3,11},{4,12},{5,13},{6,14},{7,15},{8,0},{9,1},... | collective-permute-start | bytes 786440 | tf_op jit(solution)/shard_map/ppermute | solution.py:29
  117.5 10.6 %collective-permute-start.21 = (f32[32,2048]{1,0:T(8,128)S(1)}, f32[32,2048]{1,0:T(8,128)S(1)}, u32[]{:S(2)}, u32[]{:S(2)}) collective-permute-start(f32[32,2048]{1,0:T(8,128)S(1)} %get-tuple-element.44), channel_id=1, source_target_pairs={{0,16},{1,17},{2,18},{3,19},{4,20},{5,21},{6,22},{7,23},{8,24},{9,... | collective-permute-start | bytes 786440 | tf_op jit(solution)/shard_map/ppermute | solution.py:29
  121.5 11.9 %collective-permute-start.22 = (f32[32,2048]{1,0:T(8,128)S(1)}, f32[32,2048]{1,0:T(8,128)S(1)}, u32[]{:S(2)}, u32[]{:S(2)}) collective-permute-start(f32[32,2048]{1,0:T(8,128)S(1)} %get-tuple-element.45), channel_id=1, source_target_pairs={{0,24},{1,25},{2,26},{3,27},{4,28},{5,29},{6,30},{7,31},{8,16},{9,... | collective-permute-start | bytes 786440 | tf_op jit(solution)/shard_map/ppermute | solution.py:29
  125.3 15.8 %collective-permute-start.27 = (f32[32,2048]{1,0:T(8,128)S(1)}, f32[32,2048]{1,0:T(8,128)S(1)}, u32[]{:S(2)}, u32[]{:S(2)}) collective-permute-start(f32[32,2048]{1,0:T(8,128)S(1)} %get-tuple-element.53), channel_id=1, source_target_pairs={{0,32},{1,33},{2,34},{3,35},{4,36},{5,37},{6,38},{7,39},{8,40},{9,... | collective-permute-start | bytes 786440 | tf_op jit(solution)/shard_map/ppermute | solution.py:29
  128.0 14.7 %collective-permute-start.28 = (f32[32,2048]{1,0:T(8,128)S(1)}, f32[32,2048]{1,0:T(8,128)S(1)}, u32[]{:S(2)}, u32[]{:S(2)}) collective-permute-start(f32[32,2048]{1,0:T(8,128)S(1)} %get-tuple-element.54), channel_id=1, source_target_pairs={{0,64},{1,65},{2,66},{3,67},{4,68},{5,69},{6,70},{7,71},{8,72},{9,... | collective-permute-start | bytes 786440 | tf_op jit(solution)/shard_map/ppermute | solution.py:29
  133.4 11.2 %collective-permute-start.29 = (f32[32,2048]{1,0:T(8,128)S(1)}, f32[32,2048]{1,0:T(8,128)S(1)}, u32[]{:S(2)}, u32[]{:S(2)}) collective-permute-start(f32[32,2048]{1,0:T(8,128)S(1)} %get-tuple-element.55), channel_id=1, source_target_pairs={{0,96},{1,97},{2,98},{3,99},{4,100},{5,101},{6,102},{7,103},{8,104... | collective-permute-start | bytes 786440 | tf_op jit(solution)/shard_map/ppermute | solution.py:29
  136.4 9.7 %collective-permute-start.23 = (f32[16,2048]{1,0:T(8,128)S(1)}, f32[16,2048]{1,0:T(8,128)S(1)}, u32[]{:S(2)}, u32[]{:S(2)}) collective-permute-start(f32[16,2048]{1,0:T(8,128)S(1)} %get-tuple-element.47), channel_id=1, source_target_pairs={{0,4},{1,5},{2,6},{3,7},{4,0},{5,1},{6,2},{7,3},{8,12},{9,13},{10,... | collective-permute-start | bytes 393224 | tf_op jit(solution)/shard_map/ppermute | solution.py:29
  138.0 29.3 %collective-permute-start.13 = (f32[64,2048]{1,0:T(8,128)S(1)}, f32[64,2048]{1,0:T(8,128)S(1)}, u32[]{:S(2)}, u32[]{:S(2)}) collective-permute-start(f32[64,2048]{1,0:T(8,128)S(1)} %get-tuple-element.37), channel_id=1, source_target_pairs={{0,2},{1,3},{2,0},{3,1},{4,6},{5,7},{6,4},{7,5},{8,10},{9,11},{10,... | collective-permute-start | bytes 1572872 | tf_op jit(solution)/shard_map/ppermute | solution.py:29
  141.1 26.3 %collective-permute-start.7 = (f32[64,2048]{1,0:T(8,128)S(1)}, f32[64,2048]{1,0:T(8,128)S(1)}, u32[]{:S(2)}, u32[]{:S(2)}) collective-permute-start(f32[64,2048]{1,0:T(8,128)S(1)} %get-tuple-element.33), channel_id=1, source_target_pairs={{0,2},{1,3},{2,0},{3,1},{4,6},{5,7},{6,4},{7,5},{8,10},{9,11},{10,... | collective-permute-start | bytes 1572872 | tf_op jit(solution)/shard_map/ppermute | solution.py:29
  145.4 21.3 %collective-permute-start.30 = (f32[16,2048]{1,0:T(8,128)S(1)}, f32[16,2048]{1,0:T(8,128)S(1)}, u32[]{:S(2)}, u32[]{:S(2)}) collective-permute-start(f32[16,2048]{1,0:T(8,128)S(1)} %get-tuple-element.57), channel_id=1, source_target_pairs={{0,4},{1,5},{2,6},{3,7},{4,0},{5,1},{6,2},{7,3},{8,12},{9,13},{10,... | collective-permute-start | bytes 393224 | tf_op jit(solution)/shard_map/ppermute | solution.py:29

commit v2 on v0

v2 whole, which is shorter than its diff:
```python
import functools
import math

import jax
import jax.numpy as jnp
from jax import lax
from jax.experimental import pallas as pl
from jax.experimental.pallas import tpu as pltpu
from jax.sharding import PartitionSpec as P

F32, BF16, I16 = jnp.float32, jnp.bfloat16, jnp.int16
TILE = 256
OCC, NA_D, NB_D, CT = 512, 2048, 4096, 16
TN = 512
P_WIDE = 2560
Q_WIDE = NB_D - P_WIDE
LEVELS = 32766.0
OCTAVE = math.log(2.0) / 16
VMEM_LIMIT = 44 * 2**20
WEIGHT = 0.4


def exchange_pairs(y=0, z=0, xl=0, xh=0, core=0):
    row_flip = y * 8 + z * 2 + xl
    col_flip = xh * 2 + core
    return [
        (row * 4 + col, (row ^ row_flip) * 4 + (col ^ col_flip))
        for row in range(32)
        for col in range(4)
    ]


def swap(what, value, **flips):
    axis, by = next(iter(flips.items()))
    with jax.named_scope(f"{what}_{axis}{by}"):
        return lax.ppermute(value, ("row", "col"), exchange_pairs(**flips))


class Coder:
    def __init__(self, ref):
        self.ref = ref
        self.wide = ref.shape[1] - 128
        self.lane = lax.broadcasted_iota(jnp.int32, (ref.shape[0], 128), 1)
        self.exponents = jnp.zeros((ref.shape[0], 128), jnp.int32)

    def put(self, t, values):
        top = jnp.maximum(jnp.max(jnp.abs(values), axis=1, keepdims=True), 1e-30)
        exponent = jnp.ceil(jnp.log(top) * (1 / OCTAVE) + 0.01)
        inverse = jnp.exp(exponent * -OCTAVE) * LEVELS
        levels = jnp.round(values * inverse).astype(jnp.int32)
        self.ref[:, t * TN : (t + 1) * TN] = levels.astype(I16)
        self.exponents = jnp.where(self.lane == t, exponent.astype(jnp.int32), self.exponents)

    def end(self):
        self.ref[:, self.wide :] = self.exponents.astype(I16)


class Decoder:
    def __init__(self, ref):
        self.ref = ref
        exponents = ref[:, ref.shape[1] - 128 :].astype(jnp.int32).astype(F32)
        self.scales = jnp.exp(exponents * OCTAVE) * (1 / LEVELS)

    def get(self, t, rows=slice(None)):
        levels = self.ref[rows, t * TN : (t + 1) * TN].astype(jnp.int32).astype(F32)
        return levels * self.scales[rows, t : t + 1]


def rows_of(shape):
    return jax.ShapeDtypeStruct(shape, F32)


def coded(rows, wide):
    return jax.ShapeDtypeStruct((rows, wide + 128), I16)


def call(kernel, operands, out_shape, scratch, flops, name, scalars=1, in_hbm=0):
    moved = sum(a.size * a.dtype.itemsize for a in (*operands, *out_shape))
    count = len(operands) - scalars - in_hbm
    return pl.pallas_call(
        kernel,
        in_specs=[pl.BlockSpec(memory_space=pltpu.SMEM)] * scalars
        + [pl.BlockSpec(memory_space=pltpu.VMEM)] * count
        + [pl.BlockSpec(memory_space=pl.ANY)] * in_hbm,
        out_specs=[pl.BlockSpec(memory_space=pltpu.VMEM)] * len(out_shape),
        out_shape=out_shape,
        scratch_shapes=scratch,
        compiler_params=pltpu.CompilerParams(vmem_limit_bytes=VMEM_LIMIT),
        cost_estimate=pl.CostEstimate(
            flops=int(flops * WEIGHT), bytes_accessed=int(moved * WEIGHT), transcendentals=0
        ),
        name=name,
    )(*operands)


def mirror_kernel(xl_first, start, s_ref, f1, f2, f3, f0_ref, i_ref, *refs):
    outs, (lhs, f0, held, sems) = refs[:-4], refs[-4:]
    y_col, z_xl = s_ref[0], s_ref[1]
    height, wide = outs[0].shape
    copies = [
        pltpu.make_async_copy(i_ref.at[:, pl.ds(start + t * TN, TN)], held.at[t], sems.at[t])
        for t in range(wide // TN)
    ]
    copies.append(pltpu.make_async_copy(f0_ref, f0, sems.at[wide // TN]))
    copies[-1].start()
    for copy in copies[:-1]:
        copy.start()
    copies[-1].wait()
    for rel_col, f in enumerate((f0, f1, f2, f3)):
        rel_y = rel_col ^ y_col
        for zx in range(8):
            rel = zx ^ z_xl
            if xl_first:
                slot = (rel & 1) * 16 + rel_y * 4 + (rel >> 1)
            else:
                slot = rel_y * 8 + (rel & 1) * 4 + (rel >> 1)
            lhs[pl.ds(pl.multiple_of(slot * 16, 16), 16), :] = f[zx * 16 : zx * 16 + 16]
    coders = [Coder(o) for o in outs[1:]]
    for t in range(wide // TN):
        copies[t].wait()
        sums = jnp.dot(lhs[...], held[t], preferred_element_type=F32)
        outs[0][:, t * TN : (t + 1) * TN] = sums[:height]
        for k, coder in enumerate(coders):
            coder.put(t, sums[(k + 1) * height : (k + 2) * height])
    for coder in coders:
        coder.end()


def mirror(scalars, firsts, integrals, xl_first, start, wide):
    count = 2 if xl_first else 4
    height = OCC // count
    return call(
        functools.partial(mirror_kernel, xl_first, start),
        (scalars, *firsts[1:], firsts[0], integrals),
        [rows_of((height, wide))] + [coded(height, wide)] * (count - 1),
        [
            pltpu.VMEM((OCC, NA_D), BF16),
            pltpu.VMEM((128, NA_D), BF16),
            pltpu.VMEM((wide // TN, NA_D, TN), BF16),
            pltpu.SemaphoreType.DMA((wide // TN + 1,)),
        ],
        2 * OCC * NA_D * wide,
        "mirror_q" if xl_first else "mirror_p",
        in_hbm=2,
    )


def direct_kernel(s_ref, n0, n1, n2, n3, i_ref, keep, send, lhs, held, sems):
    y_col = s_ref[0]
    copies = [
        pltpu.make_async_copy(i_ref.at[pl.ds(t * TN, TN), :], held.at[t], sems.at[t])
        for t in range(NA_D // TN)
    ]
    for copy in copies:
        copy.start()
    for place, n in enumerate((n0, n1, n2, n3)):
        for rel_y in range(4):
            slot = (rel_y ^ y_col) * 4 + place
            rows = pl.ds(pl.multiple_of(slot * 16, 16), 16)
            for k in range(CT):
                tile = pl.multiple_of(s_ref[2 + k] * TILE, TILE)
                lhs[rows, k * TILE : (k + 1) * TILE] = n[
                    rel_y * 16 : rel_y * 16 + 16, pl.ds(tile, TILE)
                ]
    for t in range(NA_D // TN):
        copies[t].wait()
        columns = slice(t * TN, (t + 1) * TN)
        sums = lax.dot_general(
            lhs[...], held[t], (((1,), (1,)), ((), ())), preferred_element_type=F32
        )
        keep[0:64, columns] = sums[0:64]
        send[0:64, columns] = sums[64:128]
        keep[64:128, columns] = sums[128:192]
        send[64:128, columns] = sums[192:256]


def direct(scalars, blocks, integrals, name):
    return call(
        direct_kernel,
        (scalars, *blocks, integrals),
        [rows_of((128, NA_D))] * 2,
        [
            pltpu.VMEM((256, NB_D), BF16),
            pltpu.VMEM((NA_D // TN, TN, NB_D), BF16),
            pltpu.SemaphoreType.DMA((NA_D // TN,)),
        ],
        2 * 256 * NA_D * NB_D,
        name,
        in_hbm=1,
    )


def fold_kernel(n_in, own, *refs):
    ins, outs = [Decoder(r) for r in refs[:n_in]], refs[n_in:]
    coders = [Coder(o) for o in outs[1:]]
    height = outs[0].shape[0]
    for t in range(own.shape[1] // TN):
        for k in range(len(outs)):
            rows = slice(k * height, k * height + height)
            total = own[rows, t * TN : (t + 1) * TN]
            for other in ins:
                total = total + other.get(t, rows)
            if k == 0:
                outs[0][:, t * TN : (t + 1) * TN] = total
            else:
                coders[k - 1].put(t, total)
    for coder in coders:
        coder.end()


def fold(own, others, count, name):
    height = own.shape[0] // count
    return call(
        functools.partial(fold_kernel, len(others)),
        (own, *others),
        [rows_of((height, own.shape[1]))] + [coded(height, own.shape[1])] * (count - 1),
        [],
        0,
        name,
        scalars=0,
    )


def core_kernel(own, other, keep, send):
    coder = Coder(send)
    for t in range(NA_D // TN):
        columns = slice(t * TN, (t + 1) * TN)
        keep[:, columns] = own[0:64, columns] + other[0:64, columns]
        coder.put(t, own[64:128, columns] + other[64:128, columns])
    coder.end()


def core_fold(own, other, name):
    return call(
        core_kernel, (own, other), [rows_of((64, NA_D)), coded(64, NA_D)], [], 0, name, scalars=0
    )


PARTS = ((0, 1, 2, 6), (3, 7, 4, 5))


def finish_first_kernel(s_ref, k0, r0, k1, r1, o_ref):
    z_xl = s_ref[1]
    for rels, own, other in ((PARTS[0], k0, r0), (PARTS[1], k1, r1)):
        other = Decoder(other)
        for t in range(NA_D // TN):
            columns = slice(t * TN, (t + 1) * TN)
            total = (own[:, columns] + other.get(t)).astype(BF16)
            for part, rel in enumerate(rels):
                rows = pl.ds(pl.multiple_of((rel ^ z_xl) * 16, 16), 16)
                o_ref[rows, columns] = total[part * 16 : part * 16 + 16]


def finish_first(scalars, parts):
    return call(
        finish_first_kernel,
        (scalars, *parts),
        [jax.ShapeDtypeStruct((128, NA_D), BF16)],
        [],
        0,
        "finish_first",
    )[0]


def join_kernel(p, p1, q, q1, q2, q3, keep, *sends):
    coders = [Coder(o) for o in sends]
    for start, own, others in ((0, p, (p1,)), (P_WIDE // TN, q, (q1, q2, q3))):
        others = [Decoder(r) for r in others]
        for t in range(own.shape[1] // TN):
            for k in range(4):
                rows = slice(k * 16, k * 16 + 16)
                total = own[rows, t * TN : (t + 1) * TN]
                for other in others:
                    total = total + other.get(t, rows)
                if k == 0:
                    keep[:, (start + t) * TN : (start + t + 1) * TN] = total
                else:
                    coders[k - 1].put(start + t, total)
    for coder in coders:
        coder.end()


def join(p, q):
    return call(
        join_kernel, (*p, *q), [rows_of((16, NB_D))] + [coded(16, NB_D)] * 3, [], 0, "join", scalars=0
    )


def finish_second_kernel(own, r1, r2, r3, o_ref):
    others = [Decoder(r) for r in (r1, r2, r3)]
    for t in range(NB_D // TN):
        total = own[:, t * TN : (t + 1) * TN]
        for other in others:
            total = total + other.get(t)
        o_ref[:, t * TN : (t + 1) * TN] = total.astype(BF16)


def finish_second(parts):
    return call(
        finish_second_kernel,
        parts,
        [jax.ShapeDtypeStruct((16, NB_D), BF16)],
        [],
        0,
        "finish_second",
        scalars=0,
    )[0]


def together(*values):
    return lax.optimization_barrier(values)


def on_device(amp_first, amp_second, integrals, tile_order):
    row, col = lax.axis_index("row"), lax.axis_index("col")
    place = jnp.stack([(row // 8) ^ col, row % 8]).astype(jnp.int32)
    scalars = jnp.concatenate([place, tile_order[0]])

    first_xh = swap("first", amp_first, xh=1)
    first_core = swap("first", amp_first, core=1)
    y1, y2, y3 = [swap("second", amp_second, y=r) for r in (1, 2, 3)]
    y1, y2, y3, first_xh, first_core = together(y1, y2, y3, first_xh, first_core)
    n0 = jnp.concatenate([amp_second, y1, y2, y3])
    first_both = swap("first", first_xh, core=1)
    firsts = (amp_first, first_core, first_xh, first_both)

    x0 = swap("n", n0, xl=1)
    n1, n3 = swap("n", n0, z=1), swap("n", n0, z=3)
    p = mirror(scalars, firsts, integrals, False, 0, P_WIDE)
    x0, n1, n3, p0, *firsts = together(x0, n1, n3, p[0], *firsts)
    x1, x3 = swap("x", x0, z=1), swap("x", x0, z=3)
    q = mirror(scalars, firsts, integrals, True, P_WIDE, Q_WIDE)
    n3, x1, x3, q0, q1 = together(n3, x1, x3, *q)
    q = (q0, q1)
    n2, x2 = swap("n3", n3, z=1), swap("x1", x1, z=3)

    p1, p3 = swap("p", p[1], y=1), swap("p", p[3], y=3)
    p1, p2, p3 = together(p1, p[2], p3)
    p2 = swap("p", p2, y=2)
    n0, x0, n1, n3 = together(n0, x0, n1, n3, p1)[:4]
    p = fold(p0, [p1, p2, p3], 2, "fold_p_y")
    q = fold(q[0], [swap("q", q[1], xl=1)], 4, "fold_q_xl")
    x1, x3, n2, x2, p0, p1, *q = together(x1, x3, n2, x2, *p, *q)
    p = (p0, p1)
    p_xl = swap("p", p[1], xl=1)
    q1, q2, q3 = [swap("q", q[r], y=r) for r in (1, 2, 3)]
    parts = join((p[0], p_xl), (q[0], q1, q2, q3))
    parts = [parts[0]] + [swap("z", parts[r], z=r) for r in (1, 2, 3)]

    ends = []
    for chunk, blocks in enumerate(((n0, x0, n1, n3), (x1, x3, n2, x2))):
        keep, send = direct(scalars, blocks, integrals, f"direct_{chunk}")
        keep, send = core_fold(keep, swap(f"chunk{chunk}", send, core=1), f"core_{chunk}")
        ends += [keep, swap(f"chunk{chunk}", send, xh=1)]
    ladder_second = finish_second(parts)
    ladder_first = finish_first(scalars, ends)
    return ladder_first, ladder_second


def solution(mesh):
    in_specs = (P("col", "row"), P("row", "col"), P("row", "col"), P("col", None))
    out_specs = (P("col", "row"), P("row", "col"))
    return jax.shard_map(
        on_device, mesh=mesh, in_specs=in_specs, out_specs=out_specs, check_vma=False
    )
```

time: 478 us -> 115 us (0.24)
  waiting for transfers between devices: 403 us -> 31.6 us
  starting transfers between devices: 0.16 us -> 40.8 us
  Pallas kernels: 0 us -> 39.1 us
  matrix products: 28.9 us -> 0 us
  local copies, waits for them, and re-layouts: 24.4 us -> 2.02 us
  between operations: 13.8 us -> 0.8 us
  other arithmetic: 7.63 us -> 0.73 us
    reduce_scatter x2 -> x0, waiting for transfers between devices: 234 us -> none  [the longest x1 197 us: on_device(): lax.psum_scatter(mirror_terms, 'row', scatter_dimension=0, tiled=True)]
    all_gather x2 -> x0, waiting for transfers between devices: 168 us -> none  [the longest x1 168 us: whole_direct(): gathered_second = lax.all_gather(amp_second, 'row', axis=0, tiled=True)]
    ppermute x0 -> x28, starting transfers between devices: none -> 40.8 us  [swap(): return lax.ppermute(value, ('row', 'col'), exchange_pairs(**flips))]
    pallas_call x0 -> x11, Pallas kernels: none -> 39.1 us  [call(): pl.pallas_call(kernel, in_specs=[pl.BlockSpec(memory_space=pltpu.SMEM)] *...]
    ppermute x0 -> x28, waiting for transfers between devices: none -> 31.6 us  [swap(): return lax.ppermute(value, ('row', 'col'), exchange_pairs(**flips))]
    dot_general x2 -> x0, matrix products: 28.9 us -> none  [the longest x1 15 us: whole_mirror(): jnp.dot(gathered_first, integrals, preferred_element_type=jnp.float32)]
    gather x2 -> x0, local copies, waits for them, and re-layouts: 11.4 us -> none  [reorder(): return jnp.take(tiles, order_row, axis=1).reshape(count, block.shape[1])]
    all_gather x1 -> x0, local copies, waits for them, and re-layouts: 6.49 us -> none  [whole_direct(): gathered_second = lax.all_gather(amp_second, 'row', axis=0, tiled=True)]
  transfers between devices with their start and end apart: 4 -> 28, of which waited for: 3 -> 17; matrix products, arithmetic and copies ran while one was open for 12% -> 1% of each run, Pallas kernels for 0% -> 33%
where the time goes in v2:
time: 115 us
  starting transfers between devices  40.8 us (35%)
  Pallas kernels  39.1 us (34%)
  waiting for transfers between devices  31.6 us (27%)
  local copies, waits for them, and re-layouts  2.02 us (2%)
    ppermute x28, starting transfers between devices, swap(): return lax.ppermute(value, ('row', 'col'), exchange_pairs(**flips))  40.8 us
    pallas_call x11, Pallas kernels, call(): pl.pallas_call(kernel, in_specs=[pl.BlockSpec(memory_space=pltpu.SMEM)] *...  39.1 us
    ppermute x28, waiting for transfers between devices, swap(): return lax.ppermute(value, ('row', 'col'), exchange_pairs(**flips))  31.6 us
  transfers between devices with their start and end apart: 28, of which 17 were waited for; matrix products, arithmetic and copies ran while one was open for 1% of the time, Pallas kernels for 33%

profile of v2, /device:TPU:0, one launch (start us, length us, event | category | flops | bytes accessed | tf_op | source)
XLA Modules:
  0.0 115.0 jit_solution(17459730726710439410)
XLA Ops:
  0.6 0.1 collective-permute-start.4
  0.7 3.2 %collective-permute-start.3 = (bf16[128,2048]{1,0:T(8,128)(2,1)}, bf16[128,2048]{1,0:T(8,128)(2,1)S(1)}, u32[]{:S(2)}, u32[]{:S(2)}) collective-permute-start(bf16[128,2048]{1,0:T(8,128)(2,1)} %f0_ref.2), channel_id=1, source_target_pairs={{0,2},{1,3},{2,0},{3,1},{4,6},{5,7},{6,4},{7,5},{8,10},{9,11},{10,... | collective-permute-start | bytes 1572872 | tf_op jit(solution)/shard_map/first_xh1/ppermute | solution.py:36
  3.9 3.2 %collective-permute-start.1 = (bf16[16,4096]{1,0:T(8,128)(2,1)}, bf16[16,4096]{1,0:T(8,128)(2,1)S(1)}, u32[]{:S(2)}, u32[]{:S(2)}) collective-permute-start(bf16[16,4096]{1,0:T(8,128)(2,1)} %param.5), channel_id=1, source_target_pairs={{0,64},{1,65},{2,66},{3,67},{4,68},{5,69},{6,70},{7,71},{8,72},{9,... | collective-permute-start | bytes 393224 | tf_op jit(solution)/shard_map/second_y2/ppermute | solution.py:36
  7.1 0.7 collective-permute-start
  7.8 0.4 collective-permute-start.2
  8.2 0.9 constant_dynamic-update-slice_fusion.3
  9.1 2.9 %collective-permute-done.1 = bf16[16,4096]{1,0:T(8,128)(2,1)S(1)} collective-permute-done((bf16[16,4096]{1,0:T(8,128)(2,1)}, bf16[16,4096]{1,0:T(8,128)(2,1)S(1)}, u32[]{:S(2)}, u32[]{:S(2)}) %collective-permute-start.1) | collective-permute-done | bytes 131104 | tf_op jit(solution)/shard_map/second_y2/ppermute | solution.py:36
  12.0 2.4 %collective-permute-done = bf16[16,4096]{1,0:T(8,128)(2,1)S(1)} collective-permute-done((bf16[16,4096]{1,0:T(8,128)(2,1)}, bf16[16,4096]{1,0:T(8,128)(2,1)S(1)}, u32[]{:S(2)}, u32[]{:S(2)}) %collective-permute-start) | collective-permute-done | bytes 131104 | tf_op jit(solution)/shard_map/second_y1/ppermute | solution.py:36
  14.3 0.2 collective-permute-done.2
  14.5 0.0 collective-permute-done.4.f1
  14.5 2.3 %collective-permute-done.3.f2 = bf16[128,2048]{1,0:T(8,128)(2,1)S(1)} collective-permute-done((bf16[128,2048]{1,0:T(8,128)(2,1)}, bf16[128,2048]{1,0:T(8,128)(2,1)S(1)}, u32[]{:S(2)}, u32[]{:S(2)}) %collective-permute-start.3) | collective-permute-done | bytes 524320 | tf_op jit(solution)/shard_map/first_xh1/ppermute | solution.py:36
  16.8 0.0 collective-permute-start.8
  16.8 4.2 %collective-permute-start.7 = (bf16[64,4096]{1,0:T(8,128)(2,1)S(1)}, bf16[64,4096]{1,0:T(8,128)(2,1)S(1)}, u32[]{:S(2)}, u32[]{:S(2)}) collective-permute-start(bf16[64,4096]{1,0:T(8,128)(2,1)S(1)} %constant_dynamic-update-slice_fusion.n0), channel_id=1, source_target_pairs={{0,24},{1,25},{2,26},{3,27},{4,28},{5,29},{6,30},{7,31},{8,16},{9,... | collective-permute-start | bytes 1572872 | tf_op jit(solution)/shard_map/n_z3/ppermute | solution.py:36
  21.0 1.5 %collective-permute-start.5 = (bf16[64,4096]{1,0:T(8,128)(2,1)S(1)}, bf16[64,4096]{1,0:T(8,128)(2,1)}, u32[]{:S(2)}, u32[]{:S(2)}) collective-permute-start(bf16[64,4096]{1,0:T(8,128)(2,1)S(1)} %constant_dynamic-update-slice_fusion.n0), channel_id=1, source_target_pairs={{0,4},{1,5},{2,6},{3,7},{4,0},{5,1},{6,2},{7,3},{8,12},{9,13},{10,... | collective-permute-start | bytes 1572872 | tf_op jit(solution)/shard_map/n_xl1/ppermute | solution.py:36
  22.5 0.7 pad_add_fusion.s_ref
  23.3 1.0 copy-done
  24.3 9.2 %mirror_p.1 = (f32[128,2560]{1,0:T(8,128)S(1)}, s16[128,2688]{1,0:T(8,128)(2,1)S(1)}, s16[128,2688]{1,0:T(8,128)(2,1)S(1)}, s16[128,2688]{1,0:T(8,128)(2,1)S(1)}) custom-call(s32[18]{0:T(128)S(1)} %pad_add_fusion.s_ref, bf16[128,2048]{1,0:T(8,128)(2,1)S(1)} %collective-permute-done.4.f1, bf16[128,2048]{1,0:T(8,128)(2,1)S(1)} %collective-permute-done.3.f2, ...), custom_call_target="tpu_custom_call" | custom-call | flops 2147483648 | bytes 8899817 | tf_op jit(solution)/shard_map/mirror_p/pallas_call | solution.py:80
  33.5 0.1 collective-permute-done.7.n3
  33.6 1.5 %collective-permute-done.6.n2 = bf16[64,4096]{1,0:T(8,128)(2,1)S(1)} collective-permute-done((bf16[64,4096]{1,0:T(8,128)(2,1)S(1)}, bf16[64,4096]{1,0:T(8,128)(2,1)S(1)}, u32[]{:S(2)}, u32[]{:S(2)}) %collective-permute-start.6) | collective-permute-done | bytes 524320 | tf_op jit(solution)/shard_map/n_z1/ppermute | solution.py:36
  35.1 0.1 collective-permute-done.5.n1
  35.2 1.4 %collective-permute-start.10 = (bf16[64,4096]{1,0:T(8,128)(2,1)}, bf16[64,4096]{1,0:T(8,128)(2,1)S(1)}, u32[]{:S(2)}, u32[]{:S(2)}) collective-permute-start(bf16[64,4096]{1,0:T(8,128)(2,1)} %collective-permute-done.5.n1), channel_id=1, source_target_pairs={{0,24},{1,25},{2,26},{3,27},{4,28},{5,29},{6,30},{7,31},{8,16},{9,... | collective-permute-start | bytes 1572872 | tf_op jit(solution)/shard_map/x_z3/ppermute | solution.py:36
  36.6 0.4 collective-permute-start.9
  36.9 1.6 %collective-permute-start.11 = (s16[128,2688]{1,0:T(8,128)(2,1)S(1)}, s16[128,2688]{1,0:T(8,128)(2,1)S(1)}, u32[]{:S(2)}, u32[]{:S(2)}) collective-permute-start(s16[128,2688]{1,0:T(8,128)(2,1)S(1)} %get-tuple-element.77), channel_id=1, source_target_pairs={{0,32},{1,33},{2,34},{3,35},{4,36},{5,37},{6,38},{7,39},{8,40},{9,... | collective-permute-start | bytes 2064392 | tf_op jit(solution)/shard_map/p_y1/ppermute | solution.py:36
  38.5 2.2 %collective-permute-start.12 = (s16[128,2688]{1,0:T(8,128)(2,1)S(1)}, s16[128,2688]{1,0:T(8,128)(2,1)S(1)}, u32[]{:S(2)}, u32[]{:S(2)}) collective-permute-start(s16[128,2688]{1,0:T(8,128)(2,1)S(1)} %get-tuple-element.79), channel_id=1, source_target_pairs={{0,96},{1,97},{2,98},{3,99},{4,100},{5,101},{6,102},{7,103},{8,104... | collective-permute-start | bytes 2064392 | tf_op jit(solution)/shard_map/p_y3/ppermute | solution.py:36
  40.7 6.3 %mirror_q.1 = (f32[256,1536]{1,0:T(8,128)S(1)}, s16[256,1664]{1,0:T(8,128)(2,1)S(1)}) custom-call(s32[18]{0:T(128)S(1)} %pad_add_fusion.s_ref, bf16[128,2048]{1,0:T(8,128)(2,1)S(1)} %collective-permute-done.4.f1, bf16[128,2048]{1,0:T(8,128)(2,1)S(1)} %collective-permute-done.3.f2, bf16[128,2048]{1,0:T(8,128)(2,1)S(1)} %collective-permute-done.8.f3, ...), custom_call_target="tpu_custom_call" | custom-call | flops 1288490240 | bytes 8519708 | tf_op jit(solution)/shard_map/mirror_q/pallas_call | solution.py:80
  47.0 2.8 %collective-permute-done.10.n1 = bf16[64,4096]{1,0:T(8,128)(2,1)S(1)} collective-permute-done((bf16[64,4096]{1,0:T(8,128)(2,1)}, bf16[64,4096]{1,0:T(8,128)(2,1)S(1)}, u32[]{:S(2)}, u32[]{:S(2)}) %collective-permute-start.10) | collective-permute-done | bytes 524320 | tf_op jit(solution)/shard_map/x_z3/ppermute | solution.py:36
  49.9 0.2 collective-permute-done.9.n0
  50.1 1.5 %collective-permute-start.18 = (s16[256,1664]{1,0:T(8,128)(2,1)S(1)}, s16[256,1664]{1,0:T(8,128)(2,1)S(1)}, u32[]{:S(2)}, u32[]{:S(2)}) collective-permute-start(s16[256,1664]{1,0:T(8,128)(2,1)S(1)} %get-tuple-element.97), channel_id=1, source_target_pairs={{0,4},{1,5},{2,6},{3,7},{4,0},{5,1},{6,2},{7,3},{8,12},{9,13},{10,... | collective-permute-start | bytes 2555912 | tf_op jit(solution)/shard_map/q_xl1/ppermute | solution.py:36
  51.6 1.8 %collective-permute-done.11.refs_0_ = s16[128,2688]{1,0:T(8,128)(2,1)S(1)} collective-permute-done((s16[128,2688]{1,0:T(8,128)(2,1)S(1)}, s16[128,2688]{1,0:T(8,128)(2,1)S(1)}, u32[]{:S(2)}, u32[]{:S(2)}) %collective-permute-start.11) | collective-permute-done | bytes 688160 | tf_op jit(solution)/shard_map/p_y1/ppermute | solution.py:36
  53.4 2.5 %collective-permute-done.12.refs_2_ = s16[128,2688]{1,0:T(8,128)(2,1)S(1)} collective-permute-done((s16[128,2688]{1,0:T(8,128)(2,1)S(1)}, s16[128,2688]{1,0:T(8,128)(2,1)S(1)}, u32[]{:S(2)}, u32[]{:S(2)}) %collective-permute-start.12) | collective-permute-done | bytes 688160 | tf_op jit(solution)/shard_map/p_y3/ppermute | solution.py:36
  55.9 1.7 %collective-permute-start.17 = (s16[128,2688]{1,0:T(8,128)(2,1)S(1)}, s16[128,2688]{1,0:T(8,128)(2,1)S(1)}, u32[]{:S(2)}, u32[]{:S(2)}) collective-permute-start(s16[128,2688]{1,0:T(8,128)(2,1)S(1)} %get-tuple-element.92), channel_id=1, source_target_pairs={{0,64},{1,65},{2,66},{3,67},{4,68},{5,69},{6,70},{7,71},{8,72},{9,... | collective-permute-start | bytes 2064392 | tf_op jit(solution)/shard_map/p_y2/ppermute | solution.py:36
  57.6 1.7 %collective-permute-start.15 = (bf16[64,4096]{1,0:T(8,128)(2,1)S(1)}, bf16[64,4096]{1,0:T(8,128)(2,1)S(1)}, u32[]{:S(2)}, u32[]{:S(2)}) collective-permute-start(bf16[64,4096]{1,0:T(8,128)(2,1)S(1)} %collective-permute-done.7.n3), channel_id=1, source_target_pairs={{0,8},{1,9},{2,10},{3,11},{4,12},{5,13},{6,14},{7,15},{8,0},{9,1},... | collective-permute-start | bytes 1572872 | tf_op jit(solution)/shard_map/n3_z1/ppermute | solution.py:36
  59.3 1.5 %collective-permute-start.16 = (bf16[64,4096]{1,0:T(8,128)(2,1)S(1)}, bf16[64,4096]{1,0:T(8,128)(2,1)S(1)}, u32[]{:S(2)}, u32[]{:S(2)}) collective-permute-start(bf16[64,4096]{1,0:T(8,128)(2,1)S(1)} %collective-permute-done.9.n0), channel_id=1, source_target_pairs={{0,24},{1,25},{2,26},{3,27},{4,28},{5,29},{6,30},{7,31},{8,16},{9,... | collective-permute-start | bytes 1572872 | tf_op jit(solution)/shard_map/x1_z3/ppermute | solution.py:36
  60.8 8.6 %direct_0.1 = (f32[128,2048]{1,0:T(8,128)S(1)}, f32[128,2048]{1,0:T(8,128)S(1)}) custom-call(s32[18]{0:T(128)S(1)} %pad_add_fusion.s_ref, bf16[64,4096]{1,0:T(8,128)(2,1)S(1)} %constant_dynamic-update-slice_fusion.n0, bf16[64,4096]{1,0:T(8,128)(2,1)} %collective-permute-done.5.n1, bf16[64,4096]{1,0:T(8,128)(2,1)S(1)} %collective-permute-done.6.n2, ...), custom_call_target="tpu_custom_call" | custom-call | flops 1717986944 | bytes 8388636 | tf_op jit(solution)/shard_map/direct_0/pallas_call | solution.py:80
  69.4 0.1 collective-permute-start.13
  69.5 0.0 collective-permute-done.18.refs_0_
  69.5 1.0 fold_q_xl.1
  70.6 2.1 %collective-permute-done.17.refs_1_ = s16[128,2688]{1,0:T(8,128)(2,1)S(1)} collective-permute-done((s16[128,2688]{1,0:T(8,128)(2,1)S(1)}, s16[128,2688]{1,0:T(8,128)(2,1)S(1)}, u32[]{:S(2)}, u32[]{:S(2)}) %collective-permute-start.17) | collective-permute-done | bytes 688160 | tf_op jit(solution)/shard_map/p_y2/ppermute | solution.py:36
  72.6 1.0 fold_p_y.1
  73.6 0.0 collective-permute-done.16.n3
  73.7 8.1 %direct_1.1 = (f32[128,2048]{1,0:T(8,128)S(1)}, f32[128,2048]{1,0:T(8,128)S(1)}) custom-call(s32[18]{0:T(128)S(1)} %pad_add_fusion.s_ref, bf16[64,4096]{1,0:T(8,128)(2,1)S(1)} %collective-permute-done.9.n0, bf16[64,4096]{1,0:T(8,128)(2,1)S(1)} %collective-permute-done.10.n1, bf16[64,4096]{1,0:T(8,128)(2,1)S(1)} %collective-permute-done.15.n2, ...), custom_call_target="tpu_custom_call" | custom-call | flops 1717986944 | bytes 8388636 | tf_op jit(solution)/shard_map/direct_1/pallas_call | solution.py:80
  81.8 0.1 collective-permute-start.19
  81.8 0.3 collective-permute-start.22
  82.1 1.5 %collective-permute-start.21 = (s16[64,2688]{1,0:T(8,128)(2,1)S(1)}, s16[64,2688]{1,0:T(8,128)(2,1)S(1)}, u32[]{:S(2)}, u32[]{:S(2)}) collective-permute-start(s16[64,2688]{1,0:T(8,128)(2,1)S(1)} %get-tuple-element.111), channel_id=1, source_target_pairs={{0,4},{1,5},{2,6},{3,7},{4,0},{5,1},{6,2},{7,3},{8,12},{9,13},{10,... | collective-permute-start | bytes 1032200 | tf_op jit(solution)/shard_map/p_xl1/ppermute | solution.py:36
  83.6 3.5 %collective-permute-start.23 = (s16[64,1664]{1,0:T(8,128)(2,1)S(1)}, s16[64,1664]{1,0:T(8,128)(2,1)S(1)}, u32[]{:S(2)}, u32[]{:S(2)}) collective-permute-start(s16[64,1664]{1,0:T(8,128)(2,1)S(1)} %get-tuple-element.114), channel_id=1, source_target_pairs={{0,64},{1,65},{2,66},{3,67},{4,68},{5,69},{6,70},{7,71},{8,72},{9,... | collective-permute-start | bytes 638984 | tf_op jit(solution)/shard_map/q_y2/ppermute | solution.py:36
  87.1 0.0 collective-permute-done.13.other
  87.1 1.1 collective-permute-start.24
  88.1 0.2 core_0.1
  88.3 3.0 %collective-permute-start.14 = (s16[64,2176]{1,0:T(8,128)(2,1)S(1)}, s16[64,2176]{1,0:T(8,128)(2,1)S(1)}, u32[]{:S(2)}, u32[]{:S(2)}) collective-permute-start(s16[64,2176]{1,0:T(8,128)(2,1)S(1)} %get-tuple-element.88), channel_id=1, source_target_pairs={{0,2},{1,3},{2,0},{3,1},{4,6},{5,7},{6,4},{7,5},{8,10},{9,11},{10,... | collective-permute-start | bytes 835592 | tf_op jit(solution)/shard_map/chunk0_xh1/ppermute | solution.py:36
  91.4 0.2 core_1.1
  91.6 1.4 %collective-permute-start.20 = (s16[64,2176]{1,0:T(8,128)(2,1)S(1)}, s16[64,2176]{1,0:T(8,128)(2,1)S(1)}, u32[]{:S(2)}, u32[]{:S(2)}) collective-permute-start(s16[64,2176]{1,0:T(8,128)(2,1)S(1)} %get-tuple-element.109), channel_id=1, source_target_pairs={{0,2},{1,3},{2,0},{3,1},{4,6},{5,7},{6,4},{7,5},{8,10},{9,11},{10,... | collective-permute-start | bytes 835592 | tf_op jit(solution)/shard_map/chunk1_xh1/ppermute | solution.py:36
  93.0 2.8 %collective-permute-done.23.q2 = s16[64,1664]{1,0:T(8,128)(2,1)S(1)} collective-permute-done((s16[64,1664]{1,0:T(8,128)(2,1)S(1)}, s16[64,1664]{1,0:T(8,128)(2,1)S(1)}, u32[]{:S(2)}, u32[]{:S(2)}) %collective-permute-start.23) | collective-permute-done | bytes 213024 | tf_op jit(solution)/shard_map/q_y2/ppermute | solution.py:36
  95.8 3.8 %collective-permute-done.24.q3 = s16[64,1664]{1,0:T(8,128)(2,1)S(1)} collective-permute-done((s16[64,1664]{1,0:T(8,128)(2,1)S(1)}, s16[64,1664]{1,0:T(8,128)(2,1)S(1)}, u32[]{:S(2)}, u32[]{:S(2)}) %collective-permute-start.24) | collective-permute-done | bytes 213024 | tf_op jit(solution)/shard_map/q_y3/ppermute | solution.py:36
  99.6 2.0 %join.1 = (f32[16,4096]{1,0:T(8,128)S(1)}, s16[16,4224]{1,0:T(8,128)(2,1)S(1)}, s16[16,4224]{1,0:T(8,128)(2,1)S(1)}, s16[16,4224]{1,0:T(8,128)(2,1)S(1)}) custom-call(f32[64,2560]{1,0:T(8,128)S(1)} %get-tuple-element.110.p, s16[64,2688]{1,0:T(8,128)(2,1)S(1)} %collective-permute-done.21.p1, f32[64,1536]{1,0:T(8,128)S(1)} %get-tuple-element.112.q, ...), custom_call_target="tpu_custom_call" | custom-call | bytes 1079705 | tf_op jit(solution)/shard_map/join/pallas_call | solution.py:80
  101.6 1.9 %collective-permute-start.25 = (s16[16,4224]{1,0:T(8,128)(2,1)S(1)}, s16[16,4224]{1,0:T(8,128)(2,1)S(1)}, u32[]{:S(2)}, u32[]{:S(2)}) collective-permute-start(s16[16,4224]{1,0:T(8,128)(2,1)S(1)} %get-tuple-element.117), channel_id=1, source_target_pairs={{0,8},{1,9},{2,10},{3,11},{4,12},{5,13},{6,14},{7,15},{8,0},{9,1},... | collective-permute-start | bytes 405512 | tf_op jit(solution)/shard_map/z_z1/ppermute | solution.py:36
  103.5 1.1 collective-permute-start.26
  104.7 1.7 %collective-permute-start.27 = (s16[16,4224]{1,0:T(8,128)(2,1)S(1)}, s16[16,4224]{1,0:T(8,128)(2,1)S(1)}, u32[]{:S(2)}, u32[]{:S(2)}) collective-permute-start(s16[16,4224]{1,0:T(8,128)(2,1)S(1)} %get-tuple-element.119), channel_id=1, source_target_pairs={{0,24},{1,25},{2,26},{3,27},{4,28},{5,29},{6,30},{7,31},{8,16},{9,... | collective-permute-start | bytes 405512 | tf_op jit(solution)/shard_map/z_z3/ppermute | solution.py:36
  106.4 1.7 %collective-permute-done.25.r1 = s16[16,4224]{1,0:T(8,128)(2,1)S(1)} collective-permute-done((s16[16,4224]{1,0:T(8,128)(2,1)S(1)}, s16[16,4224]{1,0:T(8,128)(2,1)S(1)}, u32[]{:S(2)}, u32[]{:S(2)}) %collective-permute-start.25) | collective-permute-done | bytes 135200 | tf_op jit(solution)/shard_map/z_z1/ppermute | solution.py:36
  108.1 2.6 %collective-permute-done.26.r2 = s16[16,4224]{1,0:T(8,128)(2,1)S(1)} collective-permute-done((s16[16,4224]{1,0:T(8,128)(2,1)S(1)}, s16[16,4224]{1,0:T(8,128)(2,1)S(1)}, u32[]{:S(2)}, u32[]{:S(2)}) %collective-permute-start.26) | collective-permute-done | bytes 135200 | tf_op jit(solution)/shard_map/z_z2/ppermute | solution.py:36
  110.7 2.0 %collective-permute-done.27.r3 = s16[16,4224]{1,0:T(8,128)(2,1)S(1)} collective-permute-done((s16[16,4224]{1,0:T(8,128)(2,1)S(1)}, s16[16,4224]{1,0:T(8,128)(2,1)S(1)}, u32[]{:S(2)}, u32[]{:S(2)}) %collective-permute-start.27) | collective-permute-done | bytes 135200 | tf_op jit(solution)/shard_map/z_z3/ppermute | solution.py:36
  112.7 0.8 finish_second.1
  113.5 0.0 collective-permute-done.14.r0
  113.5 0.0 collective-permute-done.20.r1
  113.5 1.5 %finish_first.1 = bf16[128,2048]{1,0:T(8,128)(2,1)} custom-call(s32[18]{0:T(128)S(1)} %pad_add_fusion.s_ref, f32[64,2048]{1,0:T(8,128)S(1)} %get-tuple-element.87.k0, s16[64,2176]{1,0:T(8,128)(2,1)S(1)} %collective-permute-done.14.r0, f32[64,2048]{1,0:T(8,128)S(1)} %get-tuple-element.108.k1, s16[64,2176]{1,0:T(8,128)(2,1)S(1)} %collective-permute-done.20.r1), custom_call_target="tpu_custom_call" | custom-call | bytes 851996 | tf_op jit(solution)/shard_map/finish_first/pallas_call | solution.py:80
  (10 shorter events, 0.0 us)
Async XLA Ops:
  0.6 13.9 %collective-permute-start.4 = (bf16[128,2048]{1,0:T(8,128)(2,1)}, bf16[128,2048]{1,0:T(8,128)(2,1)S(1)}, u32[]{:S(2)}, u32[]{:S(2)}) collective-permute-start(bf16[128,2048]{1,0:T(8,128)(2,1)} %f0_ref.2), channel_id=1, source_target_pairs={{0,1},{1,0},{2,3},{3,2},{4,5},{5,4},{6,7},{7,6},{8,9},{9,8},{10,11... | collective-permute-start | bytes 1572872 | tf_op jit(solution)/shard_map/first_core1/ppermute | solution.py:36
  0.7 16.1 %collective-permute-start.3 = (bf16[128,2048]{1,0:T(8,128)(2,1)}, bf16[128,2048]{1,0:T(8,128)(2,1)S(1)}, u32[]{:S(2)}, u32[]{:S(2)}) collective-permute-start(bf16[128,2048]{1,0:T(8,128)(2,1)} %f0_ref.2), channel_id=1, source_target_pairs={{0,2},{1,3},{2,0},{3,1},{4,6},{5,7},{6,4},{7,5},{8,10},{9,11},{10,... | collective-permute-start | bytes 1572872 | tf_op jit(solution)/shard_map/first_xh1/ppermute | solution.py:36
  3.9 8.1 %collective-permute-start.1 = (bf16[16,4096]{1,0:T(8,128)(2,1)}, bf16[16,4096]{1,0:T(8,128)(2,1)S(1)}, u32[]{:S(2)}, u32[]{:S(2)}) collective-permute-start(bf16[16,4096]{1,0:T(8,128)(2,1)} %param.5), channel_id=1, source_target_pairs={{0,64},{1,65},{2,66},{3,67},{4,68},{5,69},{6,70},{7,71},{8,72},{9,... | collective-permute-start | bytes 393224 | tf_op jit(solution)/shard_map/second_y2/ppermute | solution.py:36
  7.1 7.2 %collective-permute-start = (bf16[16,4096]{1,0:T(8,128)(2,1)}, bf16[16,4096]{1,0:T(8,128)(2,1)S(1)}, u32[]{:S(2)}, u32[]{:S(2)}) collective-permute-start(bf16[16,4096]{1,0:T(8,128)(2,1)} %param.5), channel_id=1, source_target_pairs={{0,32},{1,33},{2,34},{3,35},{4,36},{5,37},{6,38},{7,39},{8,40},{9,... | collective-permute-start | bytes 393224 | tf_op jit(solution)/shard_map/second_y1/ppermute | solution.py:36
  7.8 6.7 %collective-permute-start.2 = (bf16[16,4096]{1,0:T(8,128)(2,1)}, bf16[16,4096]{1,0:T(8,128)(2,1)S(1)}, u32[]{:S(2)}, u32[]{:S(2)}) collective-permute-start(bf16[16,4096]{1,0:T(8,128)(2,1)} %param.5), channel_id=1, source_target_pairs={{0,96},{1,97},{2,98},{3,99},{4,100},{5,101},{6,102},{7,103},{8,104... | collective-permute-start | bytes 393224 | tf_op jit(solution)/shard_map/second_y3/ppermute | solution.py:36
  16.8 6.5 %collective-permute-start.8 = (bf16[128,2048]{1,0:T(8,128)(2,1)S(1)}, bf16[128,2048]{1,0:T(8,128)(2,1)S(1)}, u32[]{:S(2)}, u32[]{:S(2)}) collective-permute-start(bf16[128,2048]{1,0:T(8,128)(2,1)S(1)} %collective-permute-done.3.f2), channel_id=1, source_target_pairs={{0,1},{1,0},{2,3},{3,2},{4,5},{5,4},{6,7},{7,6},{8,9},{9,8},{10,11... | collective-permute-start | bytes 1572872 | tf_op jit(solution)/shard_map/first_core1/ppermute | solution.py:36
  16.8 16.8 %collective-permute-start.7 = (bf16[64,4096]{1,0:T(8,128)(2,1)S(1)}, bf16[64,4096]{1,0:T(8,128)(2,1)S(1)}, u32[]{:S(2)}, u32[]{:S(2)}) collective-permute-start(bf16[64,4096]{1,0:T(8,128)(2,1)S(1)} %constant_dynamic-update-slice_fusion.n0), channel_id=1, source_target_pairs={{0,24},{1,25},{2,26},{3,27},{4,28},{5,29},{6,30},{7,31},{8,16},{9,... | collective-permute-start | bytes 1572872 | tf_op jit(solution)/shard_map/n_z3/ppermute | solution.py:36
  21.0 14.1 %collective-permute-start.6 = (bf16[64,4096]{1,0:T(8,128)(2,1)S(1)}, bf16[64,4096]{1,0:T(8,128)(2,1)S(1)}, u32[]{:S(2)}, u32[]{:S(2)}) collective-permute-start(bf16[64,4096]{1,0:T(8,128)(2,1)S(1)} %constant_dynamic-update-slice_fusion.n0), channel_id=1, source_target_pairs={{0,8},{1,9},{2,10},{3,11},{4,12},{5,13},{6,14},{7,15},{8,0},{9,1},... | collective-permute-start | bytes 1572872 | tf_op jit(solution)/shard_map/n_z1/ppermute | solution.py:36
  21.0 14.2 %collective-permute-start.5 = (bf16[64,4096]{1,0:T(8,128)(2,1)S(1)}, bf16[64,4096]{1,0:T(8,128)(2,1)}, u32[]{:S(2)}, u32[]{:S(2)}) collective-permute-start(bf16[64,4096]{1,0:T(8,128)(2,1)S(1)} %constant_dynamic-update-slice_fusion.n0), channel_id=1, source_target_pairs={{0,4},{1,5},{2,6},{3,7},{4,0},{5,1},{6,2},{7,3},{8,12},{9,13},{10,... | collective-permute-start | bytes 1572872 | tf_op jit(solution)/shard_map/n_xl1/ppermute | solution.py:36
  23.3 1.0 copy-start
  35.2 14.7 %collective-permute-start.10 = (bf16[64,4096]{1,0:T(8,128)(2,1)}, bf16[64,4096]{1,0:T(8,128)(2,1)S(1)}, u32[]{:S(2)}, u32[]{:S(2)}) collective-permute-start(bf16[64,4096]{1,0:T(8,128)(2,1)} %collective-permute-done.5.n1), channel_id=1, source_target_pairs={{0,24},{1,25},{2,26},{3,27},{4,28},{5,29},{6,30},{7,31},{8,16},{9,... | collective-permute-start | bytes 1572872 | tf_op jit(solution)/shard_map/x_z3/ppermute | solution.py:36
  36.6 13.5 %collective-permute-start.9 = (bf16[64,4096]{1,0:T(8,128)(2,1)}, bf16[64,4096]{1,0:T(8,128)(2,1)S(1)}, u32[]{:S(2)}, u32[]{:S(2)}) collective-permute-start(bf16[64,4096]{1,0:T(8,128)(2,1)} %collective-permute-done.5.n1), channel_id=1, source_target_pairs={{0,8},{1,9},{2,10},{3,11},{4,12},{5,13},{6,14},{7,15},{8,0},{9,1},... | collective-permute-start | bytes 1572872 | tf_op jit(solution)/shard_map/x_z1/ppermute | solution.py:36
  36.9 16.4 %collective-permute-start.11 = (s16[128,2688]{1,0:T(8,128)(2,1)S(1)}, s16[128,2688]{1,0:T(8,128)(2,1)S(1)}, u32[]{:S(2)}, u32[]{:S(2)}) collective-permute-start(s16[128,2688]{1,0:T(8,128)(2,1)S(1)} %get-tuple-element.77), channel_id=1, source_target_pairs={{0,32},{1,33},{2,34},{3,35},{4,36},{5,37},{6,38},{7,39},{8,40},{9,... | collective-permute-start | bytes 2064392 | tf_op jit(solution)/shard_map/p_y1/ppermute | solution.py:36
  38.5 17.4 %collective-permute-start.12 = (s16[128,2688]{1,0:T(8,128)(2,1)S(1)}, s16[128,2688]{1,0:T(8,128)(2,1)S(1)}, u32[]{:S(2)}, u32[]{:S(2)}) collective-permute-start(s16[128,2688]{1,0:T(8,128)(2,1)S(1)} %get-tuple-element.79), channel_id=1, source_target_pairs={{0,96},{1,97},{2,98},{3,99},{4,100},{5,101},{6,102},{7,103},{8,104... | collective-permute-start | bytes 2064392 | tf_op jit(solution)/shard_map/p_y3/ppermute | solution.py:36
  50.1 19.5 %collective-permute-start.18 = (s16[256,1664]{1,0:T(8,128)(2,1)S(1)}, s16[256,1664]{1,0:T(8,128)(2,1)S(1)}, u32[]{:S(2)}, u32[]{:S(2)}) collective-permute-start(s16[256,1664]{1,0:T(8,128)(2,1)S(1)} %get-tuple-element.97), channel_id=1, source_target_pairs={{0,4},{1,5},{2,6},{3,7},{4,0},{5,1},{6,2},{7,3},{8,12},{9,13},{10,... | collective-permute-start | bytes 2555912 | tf_op jit(solution)/shard_map/q_xl1/ppermute | solution.py:36
  55.9 16.7 %collective-permute-start.17 = (s16[128,2688]{1,0:T(8,128)(2,1)S(1)}, s16[128,2688]{1,0:T(8,128)(2,1)S(1)}, u32[]{:S(2)}, u32[]{:S(2)}) collective-permute-start(s16[128,2688]{1,0:T(8,128)(2,1)S(1)} %get-tuple-element.92), channel_id=1, source_target_pairs={{0,64},{1,65},{2,66},{3,67},{4,68},{5,69},{6,70},{7,71},{8,72},{9,... | collective-permute-start | bytes 2064392 | tf_op jit(solution)/shard_map/p_y2/ppermute | solution.py:36
  57.6 16.1 %collective-permute-start.15 = (bf16[64,4096]{1,0:T(8,128)(2,1)S(1)}, bf16[64,4096]{1,0:T(8,128)(2,1)S(1)}, u32[]{:S(2)}, u32[]{:S(2)}) collective-permute-start(bf16[64,4096]{1,0:T(8,128)(2,1)S(1)} %collective-permute-done.7.n3), channel_id=1, source_target_pairs={{0,8},{1,9},{2,10},{3,11},{4,12},{5,13},{6,14},{7,15},{8,0},{9,1},... | collective-permute-start | bytes 1572872 | tf_op jit(solution)/shard_map/n3_z1/ppermute | solution.py:36
  59.3 14.3 %collective-permute-start.16 = (bf16[64,4096]{1,0:T(8,128)(2,1)S(1)}, bf16[64,4096]{1,0:T(8,128)(2,1)S(1)}, u32[]{:S(2)}, u32[]{:S(2)}) collective-permute-start(bf16[64,4096]{1,0:T(8,128)(2,1)S(1)} %collective-permute-done.9.n0), channel_id=1, source_target_pairs={{0,24},{1,25},{2,26},{3,27},{4,28},{5,29},{6,30},{7,31},{8,16},{9,... | collective-permute-start | bytes 1572872 | tf_op jit(solution)/shard_map/x1_z3/ppermute | solution.py:36
  69.4 17.6 %collective-permute-start.13 = (f32[128,2048]{1,0:T(8,128)S(1)}, f32[128,2048]{1,0:T(8,128)S(1)}, u32[]{:S(2)}, u32[]{:S(2)}) collective-permute-start(f32[128,2048]{1,0:T(8,128)S(1)} %get-tuple-element.86), channel_id=1, source_target_pairs={{0,1},{1,0},{2,3},{3,2},{4,5},{5,4},{6,7},{7,6},{8,9},{9,8},{10,11... | collective-permute-start | bytes 3145736 | tf_op jit(solution)/shard_map/chunk0_core1/ppermute | solution.py:36
  81.8 6.6 %collective-permute-start.19 = (f32[128,2048]{1,0:T(8,128)S(1)}, f32[128,2048]{1,0:T(8,128)S(1)}, u32[]{:S(2)}, u32[]{:S(2)}) collective-permute-start(f32[128,2048]{1,0:T(8,128)S(1)} %get-tuple-element.107), channel_id=1, source_target_pairs={{0,1},{1,0},{2,3},{3,2},{4,5},{5,4},{6,7},{7,6},{8,9},{9,8},{10,11... | collective-permute-start | bytes 3145736 | tf_op jit(solution)/shard_map/chunk1_core1/ppermute | solution.py:36
  81.8 9.8 %collective-permute-start.22 = (s16[64,1664]{1,0:T(8,128)(2,1)S(1)}, s16[64,1664]{1,0:T(8,128)(2,1)S(1)}, u32[]{:S(2)}, u32[]{:S(2)}) collective-permute-start(s16[64,1664]{1,0:T(8,128)(2,1)S(1)} %get-tuple-element.113), channel_id=1, source_target_pairs={{0,32},{1,33},{2,34},{3,35},{4,36},{5,37},{6,38},{7,39},{8,40},{9,... | collective-permute-start | bytes 638984 | tf_op jit(solution)/shard_map/q_y1/ppermute | solution.py:36
  82.1 17.5 %collective-permute-start.21 = (s16[64,2688]{1,0:T(8,128)(2,1)S(1)}, s16[64,2688]{1,0:T(8,128)(2,1)S(1)}, u32[]{:S(2)}, u32[]{:S(2)}) collective-permute-start(s16[64,2688]{1,0:T(8,128)(2,1)S(1)} %get-tuple-element.111), channel_id=1, source_target_pairs={{0,4},{1,5},{2,6},{3,7},{4,0},{5,1},{6,2},{7,3},{8,12},{9,13},{10,... | collective-permute-start | bytes 1032200 | tf_op jit(solution)/shard_map/p_xl1/ppermute | solution.py:36
  83.6 12.2 %collective-permute-start.23 = (s16[64,1664]{1,0:T(8,128)(2,1)S(1)}, s16[64,1664]{1,0:T(8,128)(2,1)S(1)}, u32[]{:S(2)}, u32[]{:S(2)}) collective-permute-start(s16[64,1664]{1,0:T(8,128)(2,1)S(1)} %get-tuple-element.114), channel_id=1, source_target_pairs={{0,64},{1,65},{2,66},{3,67},{4,68},{5,69},{6,70},{7,71},{8,72},{9,... | collective-permute-start | bytes 638984 | tf_op jit(solution)/shard_map/q_y2/ppermute | solution.py:36
  87.1 12.5 %collective-permute-start.24 = (s16[64,1664]{1,0:T(8,128)(2,1)S(1)}, s16[64,1664]{1,0:T(8,128)(2,1)S(1)}, u32[]{:S(2)}, u32[]{:S(2)}) collective-permute-start(s16[64,1664]{1,0:T(8,128)(2,1)S(1)} %get-tuple-element.115), channel_id=1, source_target_pairs={{0,96},{1,97},{2,98},{3,99},{4,100},{5,101},{6,102},{7,103},{8,104... | collective-permute-start | bytes 638984 | tf_op jit(solution)/shard_map/q_y3/ppermute | solution.py:36
  88.3 25.2 %collective-permute-start.14 = (s16[64,2176]{1,0:T(8,128)(2,1)S(1)}, s16[64,2176]{1,0:T(8,128)(2,1)S(1)}, u32[]{:S(2)}, u32[]{:S(2)}) collective-permute-start(s16[64,2176]{1,0:T(8,128)(2,1)S(1)} %get-tuple-element.88), channel_id=1, source_target_pairs={{0,2},{1,3},{2,0},{3,1},{4,6},{5,7},{6,4},{7,5},{8,10},{9,11},{10,... | collective-permute-start | bytes 835592 | tf_op jit(solution)/shard_map/chunk0_xh1/ppermute | solution.py:36
  91.6 21.9 %collective-permute-start.20 = (s16[64,2176]{1,0:T(8,128)(2,1)S(1)}, s16[64,2176]{1,0:T(8,128)(2,1)S(1)}, u32[]{:S(2)}, u32[]{:S(2)}) collective-permute-start(s16[64,2176]{1,0:T(8,128)(2,1)S(1)} %get-tuple-element.109), channel_id=1, source_target_pairs={{0,2},{1,3},{2,0},{3,1},{4,6},{5,7},{6,4},{7,5},{8,10},{9,11},{10,... | collective-permute-start | bytes 835592 | tf_op jit(solution)/shard_map/chunk1_xh1/ppermute | solution.py:36
  101.6 6.4 %collective-permute-start.25 = (s16[16,4224]{1,0:T(8,128)(2,1)S(1)}, s16[16,4224]{1,0:T(8,128)(2,1)S(1)}, u32[]{:S(2)}, u32[]{:S(2)}) collective-permute-start(s16[16,4224]{1,0:T(8,128)(2,1)S(1)} %get-tuple-element.117), channel_id=1, source_target_pairs={{0,8},{1,9},{2,10},{3,11},{4,12},{5,13},{6,14},{7,15},{8,0},{9,1},... | collective-permute-start | bytes 405512 | tf_op jit(solution)/shard_map/z_z1/ppermute | solution.py:36
  103.5 7.1 %collective-permute-start.26 = (s16[16,4224]{1,0:T(8,128)(2,1)S(1)}, s16[16,4224]{1,0:T(8,128)(2,1)S(1)}, u32[]{:S(2)}, u32[]{:S(2)}) collective-permute-start(s16[16,4224]{1,0:T(8,128)(2,1)S(1)} %get-tuple-element.118), channel_id=1, source_target_pairs={{0,16},{1,17},{2,18},{3,19},{4,20},{5,21},{6,22},{7,23},{8,24},{9,... | collective-permute-start | bytes 405512 | tf_op jit(solution)/shard_map/z_z2/ppermute | solution.py:36
  104.7 8.0 %collective-permute-start.27 = (s16[16,4224]{1,0:T(8,128)(2,1)S(1)}, s16[16,4224]{1,0:T(8,128)(2,1)S(1)}, u32[]{:S(2)}, u32[]{:S(2)}) collective-permute-start(s16[16,4224]{1,0:T(8,128)(2,1)S(1)} %get-tuple-element.119), channel_id=1, source_target_pairs={{0,24},{1,25},{2,26},{3,27},{4,28},{5,29},{6,30},{7,31},{8,16},{9,... | collective-permute-start | bytes 405512 | tf_op jit(solution)/shard_map/z_z3/ppermute | solution.py:36

commit v3 on v2

v3 whole, which is shorter than its diff:
```python
import functools
import math

import jax
import jax.numpy as jnp
from jax import lax
from jax.experimental import pallas as pl
from jax.experimental.pallas import tpu as pltpu
from jax.sharding import PartitionSpec as P

F32, BF16, I16 = jnp.float32, jnp.bfloat16, jnp.int16
TILE = 256
OCC, NA_D, NB_D, CT = 512, 2048, 4096, 16
TN = 512
CN = 256
P_WIDE = 2560
P_HALF = P_WIDE // 2
Q_WIDE = NB_D - P_WIDE
LEVELS = 32766.0
OCTAVE = math.log(2.0) / 16
VMEM_LIMIT = 16 * 2**20
WEIGHT = 2.5


def exchange_pairs(y=0, z=0, xl=0, xh=0, core=0):
    row_flip = y * 8 + z * 2 + xl
    col_flip = xh * 2 + core
    return [
        (row * 4 + col, (row ^ row_flip) * 4 + (col ^ col_flip))
        for row in range(32)
        for col in range(4)
    ]


def swap(what, value, **flips):
    axis, by = next(iter(flips.items()))
    with jax.named_scope(f"{what}_{axis}{by}"):
        return lax.ppermute(value, ("row", "col"), exchange_pairs(**flips))


class Coder:
    def __init__(self, held, *refs):
        self.held, self.refs = held, refs
        self.lane = lax.broadcasted_iota(jnp.int32, (held.shape[0], 128), 1)
        self.tops = jnp.full((held.shape[0], 128), 1e-30, F32)

    def put(self, t, values):
        self.held[:, t * CN : (t + 1) * CN] = values
        top = jnp.max(jnp.abs(values), axis=1, keepdims=True)
        self.tops = jnp.where(self.lane == t, jnp.maximum(top, 1e-30), self.tops)

    def end(self):
        wide = self.held.shape[1]
        exponents = jnp.ceil(jnp.log(self.tops) * (1 / OCTAVE) + 0.01)
        inverse = jnp.exp(exponents * -OCTAVE) * LEVELS
        exponents = exponents.astype(jnp.int32).astype(I16)
        height = self.refs[0].shape[0]
        for k, ref in enumerate(self.refs):
            rows = slice(k * height, k * height + height)
            ref[:, wide:] = exponents[rows]
            for t in range(wide // CN):
                columns = slice(t * CN, (t + 1) * CN)
                levels = jnp.round(self.held[rows, columns] * inverse[rows, t : t + 1])
                ref[:, columns] = levels.astype(jnp.int32).astype(I16)


def coder_scratch(rows, wide):
    return pltpu.VMEM((rows, wide), F32)


class Decoder:
    def __init__(self, ref):
        self.ref = ref
        exponents = ref[:, ref.shape[1] - 128 :].astype(jnp.int32).astype(F32)
        self.scales = jnp.exp(exponents * OCTAVE) * (1 / LEVELS)

    def get(self, t, rows=slice(None)):
        levels = self.ref[rows, t * CN : (t + 1) * CN].astype(jnp.int32).astype(F32)
        return levels * self.scales[rows, t : t + 1]


def rows_of(shape):
    return jax.ShapeDtypeStruct(shape, F32)


def coded(rows, wide):
    return jax.ShapeDtypeStruct((rows, wide + 128), I16)


def call(kernel, operands, out_shape, scratch, flops, name, scalars=1):
    moved = sum(a.size * a.dtype.itemsize for a in (*operands, *out_shape))
    count = len(operands) - scalars
    return pl.pallas_call(
        kernel,
        in_specs=[pl.BlockSpec(memory_space=pltpu.SMEM)] * scalars
        + [pl.BlockSpec(memory_space=pltpu.VMEM)] * count,
        out_specs=[pl.BlockSpec(memory_space=pltpu.VMEM)] * len(out_shape),
        out_shape=out_shape,
        scratch_shapes=scratch,
        compiler_params=pltpu.CompilerParams(vmem_limit_bytes=VMEM_LIMIT),
        cost_estimate=pl.CostEstimate(
            flops=int(flops * WEIGHT), bytes_accessed=int(moved * WEIGHT), transcendentals=0
        ),
        name=name,
    )(*operands)


def product_lhs(z_xl, blocks, lhs):
    for k, f in enumerate(blocks):
        for zx in range(8):
            rel = zx ^ z_xl
            slot = k * 8 + (rel & 1) * 4 + (rel >> 1)
            lhs[pl.ds(pl.multiple_of(slot * 16, 16), 16), :] = f[zx * 16 : zx * 16 + 16]


def early_kernel(start, s_ref, f0, f1, i_ref, out, lhs):
    product_lhs(s_ref[1], (f0, f1), lhs)
    for t in range(out.shape[1] // TN):
        columns = slice(start + t * TN, start + (t + 1) * TN)
        sums = jnp.dot(lhs[...], i_ref[:, columns], preferred_element_type=F32)
        out[:, t * TN : (t + 1) * TN] = sums


def early(scalars, firsts, integrals, start, wide, name):
    return call(
        functools.partial(early_kernel, start),
        (scalars, *firsts, integrals),
        [rows_of((256, wide))],
        [pltpu.VMEM((256, NA_D), BF16)],
        2 * 256 * NA_D * wide,
        name,
    )[0]


def mirror_p_kernel(
    s_ref,
    f2,
    f3,
    early_ref,
    i_ref,
    keep_a,
    send_a,
    keep_b,
    send_b,
    lhs,
    sums,
    held_a,
    held_b,
):
    y_col = s_ref[0]
    product_lhs(s_ref[1], (f2, f3), lhs)
    coders = [Coder(held_a, send_a), Coder(held_b, send_b)]
    for t in range(P_WIDE // TN):
        columns = slice(t * TN, (t + 1) * TN)
        late = jnp.dot(lhs[...], i_ref[:, columns], preferred_element_type=F32)
        for k in range(2):
            rows = slice(k * 128, k * 128 + 128)
            sums[pl.ds(pl.multiple_of((k ^ y_col) * 128, 128), 128), :] = early_ref[rows, columns]
            sums[pl.ds(pl.multiple_of(((k + 2) ^ y_col) * 128, 128), 128), :] = late[rows]
        for part in range(TN // CN):
            half, tile = divmod(t * (TN // CN) + part, P_HALF // CN)
            y0, y1, y2, y3 = [
                sums[y * 128 : y * 128 + 128, part * CN : part * CN + CN] for y in range(4)
            ]
            place = slice(tile * CN, tile * CN + CN)
            if half == 0:
                keep_a[0:128, place], keep_a[128:256, place] = y0, y1
                coders[0].put(tile, jnp.concatenate([y3, y2]))
            else:
                keep_b[0:128, place], keep_b[128:256, place] = y0, y3
                coders[1].put(tile, jnp.concatenate([y1, y2]))
    for coder in coders:
        coder.end()


def mirror_p(scalars, firsts, first_sums, integrals):
    return call(
        mirror_p_kernel,
        (scalars, *firsts, first_sums, integrals),
        [rows_of((256, P_HALF)), coded(256, P_HALF)] * 2,
        [pltpu.VMEM((256, NA_D), BF16), pltpu.VMEM((OCC, TN), F32)]
        + [coder_scratch(256, P_HALF)] * 2,
        2 * 256 * NA_D * P_WIDE,
        "mirror_p",
    )


def mirror_q_kernel(s_ref, f2, f3, early_ref, i_ref, keep, send, lhs, sums, coding):
    y_col = s_ref[0]
    product_lhs(s_ref[1], (f2, f3), lhs)
    coder = Coder(coding, send)
    for t in range(Q_WIDE // TN):
        columns = slice(P_WIDE + t * TN, P_WIDE + (t + 1) * TN)
        late = jnp.dot(lhs[...], i_ref[:, columns], preferred_element_type=F32)
        for k in range(4):
            for xl in range(2):
                rows = slice((k % 2) * 128 + xl * 64, (k % 2) * 128 + xl * 64 + 64)
                place = pl.ds(pl.multiple_of(xl * 256 + (k ^ y_col) * 64, 64), 64)
                sums[place, :] = early_ref[rows, t * TN : (t + 1) * TN] if k < 2 else late[rows]
        keep[:, t * TN : (t + 1) * TN] = sums[0:256]
        for part in range(TN // CN):
            coder.put(t * (TN // CN) + part, sums[256:512, part * CN : part * CN + CN])
    coder.end()


def mirror_q(scalars, firsts, first_sums, integrals):
    return call(
        mirror_q_kernel,
        (scalars, *firsts, first_sums, integrals),
        [rows_of((256, Q_WIDE)), coded(256, Q_WIDE)],
        [
            pltpu.VMEM((256, NA_D), BF16),
            pltpu.VMEM((OCC, TN), F32),
            coder_scratch(256, Q_WIDE),
        ],
        2 * 256 * NA_D * Q_WIDE,
        "mirror_q",
    )


def direct_kernel(s_ref, n0, n1, n2, n3, i_ref, keep, send, lhs):
    y_col = s_ref[0]
    for place, n in enumerate((n0, n1, n2, n3)):
        for rel_y in range(4):
            slot = (rel_y ^ y_col) * 4 + place
            rows = pl.ds(pl.multiple_of(slot * 16, 16), 16)
            for k in range(CT):
                tile = pl.multiple_of(s_ref[2 + k] * TILE, TILE)
                lhs[rows, k * TILE : (k + 1) * TILE] = n[
                    rel_y * 16 : rel_y * 16 + 16, pl.ds(tile, TILE)
                ]
    for t in range(NA_D // TN):
        columns = slice(t * TN, (t + 1) * TN)
        sums = lax.dot_general(
            lhs[...], i_ref[columns, :], (((1,), (1,)), ((), ())), preferred_element_type=F32
        )
        keep[0:64, columns] = sums[0:64]
        send[0:64, columns] = sums[64:128]
        keep[64:128, columns] = sums[128:192]
        send[64:128, columns] = sums[192:256]


def direct(scalars, blocks, integrals, name):
    return call(
        direct_kernel,
        (scalars, *blocks, integrals),
        [rows_of((128, NA_D))] * 2,
        [pltpu.VMEM((256, NB_D), BF16)],
        2 * 256 * NA_D * NB_D,
        name,
    )


def fold_kernel(own, other, keep, *refs):
    sends, held = refs[:-1], refs[-1]
    other, coder = Decoder(other), Coder(held, *sends)
    height = keep.shape[0]
    for t in range(own.shape[1] // CN):
        total = own[:, t * CN : (t + 1) * CN] + other.get(t)
        keep[:, t * CN : (t + 1) * CN] = total[:height]
        coder.put(t, total[height:])
    coder.end()


def fold(own, other, count, name):
    rows, wide = own.shape
    height = rows // count
    return call(
        fold_kernel,
        (own, other),
        [rows_of((height, wide))] + [coded(height, wide)] * (count - 1),
        [coder_scratch(rows - height, wide)],
        0,
        name,
        scalars=0,
    )


def merge_kernel(a, a1, b, b1, keep, send, held):
    coder = Coder(held, send)
    for half, (own, other) in enumerate(((a, Decoder(a1)), (b, Decoder(b1)))):
        for t in range(P_HALF // CN):
            tile = half * (P_HALF // CN) + t
            total = own[:, t * CN : (t + 1) * CN] + other.get(t)
            keep[:, tile * CN : (tile + 1) * CN] = total[0:64]
            coder.put(tile, total[64:128])
    coder.end()


def merge(parts):
    return call(
        merge_kernel,
        parts,
        [rows_of((64, P_WIDE)), coded(64, P_WIDE)],
        [coder_scratch(64, P_WIDE)],
        0,
        "merge",
        scalars=0,
    )


def core_kernel(own, other, keep, send, held):
    coder = Coder(held, send)
    for t in range(NA_D // CN):
        columns = slice(t * CN, (t + 1) * CN)
        keep[:, columns] = own[0:64, columns] + other[0:64, columns]
        coder.put(t, own[64:128, columns] + other[64:128, columns])
    coder.end()


def core_fold(own, other, name):
    return call(
        core_kernel,
        (own, other),
        [rows_of((64, NA_D)), coded(64, NA_D)],
        [coder_scratch(64, NA_D)],
        0,
        name,
        scalars=0,
    )


PARTS = ((0, 1, 2, 6), (3, 7, 4, 5))


def finish_first_kernel(s_ref, k0, r0, k1, r1, o_ref):
    z_xl = s_ref[1]
    for rels, own, other in ((PARTS[0], k0, r0), (PARTS[1], k1, r1)):
        other = Decoder(other)
        for t in range(NA_D // CN):
            columns = slice(t * CN, (t + 1) * CN)
            total = (own[:, columns] + other.get(t)).astype(BF16)
            for part, rel in enumerate(rels):
                rows = pl.ds(pl.multiple_of((rel ^ z_xl) * 16, 16), 16)
                o_ref[rows, columns] = total[part * 16 : part * 16 + 16]


def finish_first(scalars, parts):
    return call(
        finish_first_kernel,
        (scalars, *parts),
        [jax.ShapeDtypeStruct((128, NA_D), BF16)],
        [],
        0,
        "finish_first",
    )[0]


def join_kernel(p, p1, q, q1, q2, q3, keep, send1, send2, send3, held):
    coder = Coder(held, send1, send2, send3)
    for start, own, others in ((0, p, (p1,)), (P_WIDE // CN, q, (q1, q2, q3))):
        others = [Decoder(r) for r in others]
        for t in range(own.shape[1] // CN):
            total = own[:, t * CN : (t + 1) * CN]
            for other in others:
                total = total + other.get(t)
            keep[:, (start + t) * CN : (start + t + 1) * CN] = total[0:16]
            coder.put(start + t, total[16:64])
    coder.end()


def join(p, q):
    return call(
        join_kernel,
        (*p, *q),
        [rows_of((16, NB_D))] + [coded(16, NB_D)] * 3,
        [coder_scratch(48, NB_D)],
        0,
        "join",
        scalars=0,
    )


def finish_second_kernel(own, r1, r2, r3, o_ref):
    others = [Decoder(r) for r in (r1, r2, r3)]
    for t in range(NB_D // CN):
        total = own[:, t * CN : (t + 1) * CN]
        for other in others:
            total = total + other.get(t)
        o_ref[:, t * CN : (t + 1) * CN] = total.astype(BF16)


def finish_second(parts):
    return call(
        finish_second_kernel,
        parts,
        [jax.ShapeDtypeStruct((16, NB_D), BF16)],
        [],
        0,
        "finish_second",
        scalars=0,
    )[0]


def together(*values):
    return lax.optimization_barrier(values)


def on_device(amp_first, amp_second, integrals, tile_order):
    row, col = lax.axis_index("row"), lax.axis_index("col")
    place = jnp.stack([(row // 8) ^ col, row % 8]).astype(jnp.int32)
    scalars = jnp.concatenate([place, tile_order[0]])

    second = amp_second
    first_xh = swap("first", amp_first, xh=1)
    first_core = swap("first", amp_first, core=1)
    y1, y2, y3 = [swap("second", second, y=r) for r in (1, 2, 3)]
    sums_p = early(scalars, (amp_first, first_core), integrals, 0, P_WIDE, "early_p")
    sums_q = early(scalars, (amp_first, first_core), integrals, P_WIDE, Q_WIDE, "early_q")
    y1, y2, y3, scalars, first_xh, sums_p, sums_q = together(y1, y2, y3, scalars, first_xh, sums_p, sums_q)
    n0 = jnp.concatenate([second, y1, y2, y3])
    first_both = swap("first", first_xh, core=1)
    x0 = swap("n", n0, xl=1)
    n1, n3 = swap("n", n0, z=1), swap("n", n0, z=3)
    pa, pa_send, pb, pb_send = mirror_p(scalars, (first_xh, first_both), sums_p, integrals)
    pa_got, pb_got = swap("pa", pa_send, y=3), swap("pb", pb_send, y=1)
    pa, pb, sums_q, first_xh, first_both = together(pa, pb, sums_q, first_xh, first_both)
    q, q_send = mirror_q(scalars, (first_xh, first_both), sums_q, integrals)
    n0, x0, n1, n3, q, q_send = together(n0, x0, n1, n3, q, q_send)
    q_got = swap("q", q_send, xl=1)
    x1, x3 = swap("x", x0, z=1), swap("x", x0, z=3)
    keep0, send0 = direct(scalars, (n0, x0, n1, n3), integrals, "direct_0")
    pa, pa_got, pb, pb_got = together(pa, pa_got, pb, pb_got)
    pa, pa_send = fold(pa, pa_got, 2, "fold_pa")
    pb, pb_send = fold(pb, pb_got, 2, "fold_pb")
    pa_got, pb_got = swap("pa", pa_send, y=1), swap("pb", pb_send, y=3)
    got0 = swap("chunk0", send0, core=1)
    n3, x1, x3, pa, pb = together(n3, x1, x3, pa, pb)
    q = fold(q, q_got, 4, "fold_q_xl")
    n2, x2 = swap("n3", n3, z=1), swap("x1", x1, z=3)
    p, p_send = merge((pa, pa_got, pb, pb_got))
    p, p_send, *q = together(p, p_send, *q)
    p_got = swap("p", p_send, xl=1)
    q_got = [swap("q", q[r], y=r) for r in (1, 2, 3)]
    keep0, send0 = core_fold(keep0, got0, "core_0")
    got0 = swap("chunk0", send0, xh=1)
    x1, x3, n2, x2, p = together(x1, x3, n2, x2, p)
    keep1, send1 = direct(scalars, (x1, x3, n2, x2), integrals, "direct_1")
    p_got, keep1, send1, *q_got = together(p_got, keep1, send1, *q_got)
    parts = join((p, p_got), (q[0], *q_got))
    got1 = swap("chunk1", send1, core=1)
    keep1, got1, *parts = together(keep1, got1, *parts)
    parts = [parts[0]] + [swap("z", parts[r], z=r) for r in (1, 2, 3)]
    keep1, send1 = core_fold(keep1, got1, "core_1")
    got1 = swap("chunk1", send1, xh=1)
    ladder_first = finish_first(scalars, (keep0, got0, keep1, got1))
    ladder_first, *parts = together(ladder_first, *parts)
    ladder_second = finish_second(parts)
    return ladder_first, ladder_second


def solution(mesh):
    in_specs = (P("col", "row"), P("row", "col"), P("row", "col"), P("col", None))
    out_specs = (P("col", "row"), P("row", "col"))
    return jax.shard_map(
        on_device, mesh=mesh, in_specs=in_specs, out_specs=out_specs, check_vma=False
    )
```

time: 115 us -> 105 us (0.913)
  waiting for transfers between devices: 31.6 us -> 22.3 us
  Pallas kernels: 39.1 us -> 32.8 us
  local copies, waits for them, and re-layouts: 2.02 us -> 7.77 us
  starting transfers between devices: 40.8 us -> 39.5 us
    ppermute x28 -> x29, waiting for transfers between devices: 31.6 us -> 22.3 us  [swap(): return lax.ppermute(value, ('row', 'col'), exchange_pairs(**flips))]
    pallas_call x11 -> x15, Pallas kernels: 39.1 us -> 32.8 us  [call(): pl.pallas_call(kernel, in_specs=[pl.BlockSpec(memory_space=pltpu.SMEM)] *...]
    unnamed x5 -> x15, local copies, waits for them, and re-layouts: 2.01 us -> 7.76 us
    ppermute x28 -> x29, starting transfers between devices: 40.8 us -> 39.5 us  [swap(): return lax.ppermute(value, ('row', 'col'), exchange_pairs(**flips))]
  transfers between devices with their start and end apart: 28 -> 29, of which waited for: 17 -> 8; matrix products, arithmetic and copies ran while one was open for 1% -> 2% of each run, Pallas kernels for 33% -> 31%
where the time goes in v3:
time: 105 us; the launch traced here: 104 us
  starting transfers between devices  39.5 us (38%)
  Pallas kernels  32.8 us (31%)
  waiting for transfers between devices  22.3 us (21%)
  local copies, waits for them, and re-layouts  7.77 us (7%)
    ppermute x29, starting transfers between devices, swap(): return lax.ppermute(value, ('row', 'col'), exchange_pairs(**flips))  39.5 us
    pallas_call x15, Pallas kernels, call(): pl.pallas_call(kernel, in_specs=[pl.BlockSpec(memory_space=pltpu.SMEM)] *...  32.8 us
    ppermute x29, waiting for transfers between devices, swap(): return lax.ppermute(value, ('row', 'col'), exchange_pairs(**flips))  22.3 us
    unnamed x15, local copies, waits for them, and re-layouts  7.76 us
  transfers between devices with their start and end apart: 29, of which 8 were waited for; matrix products, arithmetic and copies ran while one was open for 2% of the time, Pallas kernels for 31%

profile of v3, /device:TPU:0, one launch (start us, length us, event | category | flops | bytes accessed | tf_op | source)
XLA Modules:
  0.0 104.1 jit_solution(16072544632192469890)
XLA Ops:
  0.6 0.1 collective-permute-start.4
  0.7 3.2 %collective-permute-start.3 = (bf16[128,2048]{1,0:T(8,128)(2,1)}, bf16[128,2048]{1,0:T(8,128)(2,1)S(1)}, u32[]{:S(2)}, u32[]{:S(2)}) collective-permute-start(bf16[128,2048]{1,0:T(8,128)(2,1)} %f0.3), channel_id=1, source_target_pairs={{0,2},{1,3},{2,0},{3,1},{4,6},{5,7},{6,4},{7,5},{8,10},{9,11},{10,... | collective-permute-start | bytes 1572872 | tf_op jit(solution)/shard_map/first_xh1/ppermute | solution.py:38
  3.9 1.6 %collective-permute-start = (bf16[16,4096]{1,0:T(8,128)(2,1)}, bf16[16,4096]{1,0:T(8,128)(2,1)S(1)}, u32[]{:S(2)}, u32[]{:S(2)}) collective-permute-start(bf16[16,4096]{1,0:T(8,128)(2,1)} %param.5), channel_id=1, source_target_pairs={{0,32},{1,33},{2,34},{3,35},{4,36},{5,37},{6,38},{7,39},{8,40},{9,... | collective-permute-start | bytes 393224 | tf_op jit(solution)/shard_map/second_y1/ppermute | solution.py:38
  5.5 2.9 %collective-permute-start.1 = (bf16[16,4096]{1,0:T(8,128)(2,1)}, bf16[16,4096]{1,0:T(8,128)(2,1)S(1)}, u32[]{:S(2)}, u32[]{:S(2)}) collective-permute-start(bf16[16,4096]{1,0:T(8,128)(2,1)} %param.5), channel_id=1, source_target_pairs={{0,64},{1,65},{2,66},{3,67},{4,68},{5,69},{6,70},{7,71},{8,72},{9,... | collective-permute-start | bytes 393224 | tf_op jit(solution)/shard_map/second_y2/ppermute | solution.py:38
  8.4 0.2 collective-permute-start.2
  8.6 0.7 pad_add_fusion.s_ref
  9.3 0.9 constant_dynamic-update-slice_fusion.3
  10.3 0.0 collective-permute-done.4.f1
  10.3 0.0 copy-start
  10.3 5.8 %copy-done = bf16[2048,4096]{1,0:T(8,128)(2,1)S(1)} copy-done((bf16[2048,4096]{1,0:T(8,128)(2,1)S(1)}, bf16[2048,4096]{1,0:T(8,128)(2,1)}, u32[]{:S(2)}) %copy-start) | copy-done | bytes 16777240
  16.0 1.0 copy-done.1
  17.1 3.5 %early_p.1.early_ref = f32[256,2560]{1,0:T(8,128)S(1)} custom-call(s32[18]{0:T(128)S(1)} %pad_add_fusion.s_ref, bf16[128,2048]{1,0:T(8,128)(2,1)S(1)} %copy-done.1, bf16[128,2048]{1,0:T(8,128)(2,1)S(1)} %collective-permute-done.4.f1, bf16[2048,4096]{1,0:T(8,128)(2,1)S(1)} %copy-done), custom_call_target="tpu_custom_call" | custom-call | flops 6710886400 | bytes 51118260 | tf_op jit(solution)/shard_map/early_p/pallas_call | solution.py:93
  20.6 2.4 %early_q.1.early_ref = f32[256,1536]{1,0:T(8,128)S(1)} custom-call(s32[18]{0:T(128)S(1)} %pad_add_fusion.s_ref, bf16[128,2048]{1,0:T(8,128)(2,1)S(1)} %copy-done.1, bf16[128,2048]{1,0:T(8,128)(2,1)S(1)} %collective-permute-done.4.f1, bf16[2048,4096]{1,0:T(8,128)(2,1)S(1)} %copy-done), custom_call_target="tpu_custom_call" | custom-call | flops 4026531840 | bytes 48496820 | tf_op jit(solution)/shard_map/early_q/pallas_call | solution.py:93
  23.0 0.0 collective-permute-done
  23.1 0.0 collective-permute-done.3.f2
  23.1 0.1 collective-permute-start.8
  23.2 0.7 collective-permute-start.5
  23.9 1.9 %collective-permute-start.6 = (bf16[64,4096]{1,0:T(8,128)(2,1)S(1)}, bf16[64,4096]{1,0:T(8,128)(2,1)S(1)}, u32[]{:S(2)}, u32[]{:S(2)}) collective-permute-start(bf16[64,4096]{1,0:T(8,128)(2,1)S(1)} %constant_dynamic-update-slice_fusion.n0), channel_id=1, source_target_pairs={{0,8},{1,9},{2,10},{3,11},{4,12},{5,13},{6,14},{7,15},{8,0},{9,1},... | collective-permute-start | bytes 1572872 | tf_op jit(solution)/shard_map/n_z1/ppermute | solution.py:38
  25.8 2.5 %collective-permute-start.7 = (bf16[64,4096]{1,0:T(8,128)(2,1)S(1)}, bf16[64,4096]{1,0:T(8,128)(2,1)S(1)}, u32[]{:S(2)}, u32[]{:S(2)}) collective-permute-start(bf16[64,4096]{1,0:T(8,128)(2,1)S(1)} %constant_dynamic-update-slice_fusion.n0), channel_id=1, source_target_pairs={{0,24},{1,25},{2,26},{3,27},{4,28},{5,29},{6,30},{7,31},{8,16},{9,... | collective-permute-start | bytes 1572872 | tf_op jit(solution)/shard_map/n_z3/ppermute | solution.py:38
  28.4 4.3 %mirror_p.1 = (f32[256,1280]{1,0:T(8,128)S(1)}, s16[256,1408]{1,0:T(8,128)(2,1)S(1)}, f32[256,1280]{1,0:T(8,128)S(1)}, s16[256,1408]{1,0:T(8,128)(2,1)S(1)}) custom-call(s32[18]{0:T(128)S(1)} %pad_add_fusion.s_ref, bf16[128,2048]{1,0:T(8,128)(2,1)S(1)} %collective-permute-done.3.f2, bf16[128,2048]{1,0:T(8,128)(2,1)S(1)} %collective-permute-done.8.f3, ...), custom_call_target="tpu_custom_call" | custom-call | flops 6710886400 | bytes 61276340 | tf_op jit(solution)/shard_map/mirror_p/pallas_call | solution.py:93
  32.6 3.1 %collective-permute-start.13 = (s16[256,1408]{1,0:T(8,128)(2,1)S(1)}, s16[256,1408]{1,0:T(8,128)(2,1)S(1)}, u32[]{:S(2)}, u32[]{:S(2)}) collective-permute-start(s16[256,1408]{1,0:T(8,128)(2,1)S(1)} %get-tuple-element.108), channel_id=1, source_target_pairs={{0,96},{1,97},{2,98},{3,99},{4,100},{5,101},{6,102},{7,103},{8,104... | collective-permute-start | bytes 2162696 | tf_op jit(solution)/shard_map/pa_y3/ppermute | solution.py:38
  35.8 3.0 %mirror_q.1 = (f32[256,1536]{1,0:T(8,128)S(1)}, s16[256,1664]{1,0:T(8,128)(2,1)S(1)}) custom-call(s32[18]{0:T(128)S(1)} %pad_add_fusion.s_ref, bf16[128,2048]{1,0:T(8,128)(2,1)S(1)} %collective-permute-done.3.f2, bf16[128,2048]{1,0:T(8,128)(2,1)S(1)} %collective-permute-done.8.f3, f32[256,1536]{1,0:T(8,128)S(1)} %early_q.1.early_ref, ...), custom_call_target="tpu_custom_call" | custom-call | flops 4026531840 | bytes 54558900 | tf_op jit(solution)/shard_map/mirror_q/pallas_call | solution.py:93
  38.7 0.0 collective-permute-done.5.n1
  38.8 2.0 %collective-permute-done.7.n3 = bf16[64,4096]{1,0:T(8,128)(2,1)S(1)} collective-permute-done((bf16[64,4096]{1,0:T(8,128)(2,1)S(1)}, bf16[64,4096]{1,0:T(8,128)(2,1)S(1)}, u32[]{:S(2)}, u32[]{:S(2)}) %collective-permute-start.7) | collective-permute-done | bytes 524320 | tf_op jit(solution)/shard_map/n_z3/ppermute | solution.py:38
  40.8 0.6 collective-permute-start.11
  41.4 2.3 %collective-permute-start.12 = (bf16[64,4096]{1,0:T(8,128)(2,1)S(1)}, bf16[64,4096]{1,0:T(8,128)(2,1)S(1)}, u32[]{:S(2)}, u32[]{:S(2)}) collective-permute-start(bf16[64,4096]{1,0:T(8,128)(2,1)S(1)} %collective-permute-done.5.n1), channel_id=1, source_target_pairs={{0,24},{1,25},{2,26},{3,27},{4,28},{5,29},{6,30},{7,31},{8,16},{9,... | collective-permute-start | bytes 1572872 | tf_op jit(solution)/shard_map/x_z3/ppermute | solution.py:38
  43.7 1.4 %collective-permute-start.17 = (s16[256,1664]{1,0:T(8,128)(2,1)S(1)}, s16[256,1664]{1,0:T(8,128)(2,1)S(1)}, u32[]{:S(2)}, u32[]{:S(2)}) collective-permute-start(s16[256,1664]{1,0:T(8,128)(2,1)S(1)} %get-tuple-element.124), channel_id=1, source_target_pairs={{0,4},{1,5},{2,6},{3,7},{4,0},{5,1},{6,2},{7,3},{8,12},{9,13},{10,... | collective-permute-start | bytes 2555912 | tf_op jit(solution)/shard_map/q_xl1/ppermute | solution.py:38
  45.2 6.5 %collective-permute-done.13.other = s16[256,1408]{1,0:T(8,128)(2,1)S(1)} collective-permute-done((s16[256,1408]{1,0:T(8,128)(2,1)S(1)}, s16[256,1408]{1,0:T(8,128)(2,1)S(1)}, u32[]{:S(2)}, u32[]{:S(2)}) %collective-permute-start.13) | collective-permute-done | bytes 720928 | tf_op jit(solution)/shard_map/pa_y3/ppermute | solution.py:38
  51.7 1.5 %collective-permute-done.14.other = s16[256,1408]{1,0:T(8,128)(2,1)S(1)} collective-permute-done((s16[256,1408]{1,0:T(8,128)(2,1)S(1)}, s16[256,1408]{1,0:T(8,128)(2,1)S(1)}, u32[]{:S(2)}, u32[]{:S(2)}) %collective-permute-start.14) | collective-permute-done | bytes 720928 | tf_op jit(solution)/shard_map/pb_y1/ppermute | solution.py:38
  53.1 0.8 fold_pb.1
  54.0 1.6 %collective-permute-start.16 = (s16[128,1408]{1,0:T(8,128)(2,1)S(1)}, s16[128,1408]{1,0:T(8,128)(2,1)S(1)}, u32[]{:S(2)}, u32[]{:S(2)}) collective-permute-start(s16[128,1408]{1,0:T(8,128)(2,1)S(1)} %get-tuple-element.120), channel_id=1, source_target_pairs={{0,96},{1,97},{2,98},{3,99},{4,100},{5,101},{6,102},{7,103},{8,104... | collective-permute-start | bytes 1081352 | tf_op jit(solution)/shard_map/pb_y3/ppermute | solution.py:38
  55.6 0.8 fold_pa.1
  56.4 0.0 collective-permute-done.12.n1
  56.4 0.1 collective-permute-start.15
  56.5 1.1 %collective-permute-start.19 = (bf16[64,4096]{1,0:T(8,128)(2,1)S(1)}, bf16[64,4096]{1,0:T(8,128)(2,1)S(1)}, u32[]{:S(2)}, u32[]{:S(2)}) collective-permute-start(bf16[64,4096]{1,0:T(8,128)(2,1)S(1)} %collective-permute-done.7.n3), channel_id=1, source_target_pairs={{0,8},{1,9},{2,10},{3,11},{4,12},{5,13},{6,14},{7,15},{8,0},{9,1},... | collective-permute-start | bytes 1572872 | tf_op jit(solution)/shard_map/n3_z1/ppermute | solution.py:38
  57.6 0.9 collective-permute-start.20
  58.5 5.3 %direct_0.1 = (f32[128,2048]{1,0:T(8,128)S(1)}, f32[128,2048]{1,0:T(8,128)S(1)}) custom-call(s32[18]{0:T(128)S(1)} %pad_add_fusion.s_ref, bf16[64,4096]{1,0:T(8,128)(2,1)S(1)} %constant_dynamic-update-slice_fusion.n0, bf16[64,4096]{1,0:T(8,128)(2,1)S(1)} %collective-permute-done.5.n1, bf16[64,4096]{1,0:T(8,128)(2,1)S(1)} %collective-permute-done.6.n2, ...), custom_call_target="tpu_custom_call" | custom-call | flops 10737418240 | bytes 52428980 | tf_op jit(solution)/shard_map/direct_0/pallas_call | solution.py:93
  63.9 0.0 collective-permute-done.17.other
  63.9 0.1 collective-permute-start.9
  64.0 1.0 fold_q_xl.1
  65.0 0.0 collective-permute-done.16.b1
  65.0 0.3 collective-permute-done.15.a1
  65.3 1.2 %merge.1 = (f32[64,2560]{1,0:T(8,128)S(1)}, s16[64,2688]{1,0:T(8,128)(2,1)S(1)}) custom-call(f32[128,1280]{1,0:T(8,128)S(1)} %get-tuple-element.117.a, s16[128,1408]{1,0:T(8,128)(2,1)S(1)} %collective-permute-done.15.a1, f32[128,1280]{1,0:T(8,128)S(1)} %get-tuple-element.119.b, s16[128,1408]{1,0:T(8,128)(2,1)S(1)} %collective-permute-done.16.b1), custom_call_target="tpu_custom_call" | custom-call | bytes 7577600 | tf_op jit(solution)/shard_map/merge/pallas_call | solution.py:93
  66.5 1.5 %collective-permute-start.18 = (s16[64,2688]{1,0:T(8,128)(2,1)S(1)}, s16[64,2688]{1,0:T(8,128)(2,1)S(1)}, u32[]{:S(2)}, u32[]{:S(2)}) collective-permute-start(s16[64,2688]{1,0:T(8,128)(2,1)S(1)} %get-tuple-element.129), channel_id=1, source_target_pairs={{0,4},{1,5},{2,6},{3,7},{4,0},{5,1},{6,2},{7,3},{8,12},{9,13},{10,... | collective-permute-start | bytes 1032200 | tf_op jit(solution)/shard_map/p_xl1/ppermute | solution.py:38
  68.0 1.7 %collective-permute-start.21 = (s16[64,1664]{1,0:T(8,128)(2,1)S(1)}, s16[64,1664]{1,0:T(8,128)(2,1)S(1)}, u32[]{:S(2)}, u32[]{:S(2)}) collective-permute-start(s16[64,1664]{1,0:T(8,128)(2,1)S(1)} %get-tuple-element.140), channel_id=1, source_target_pairs={{0,32},{1,33},{2,34},{3,35},{4,36},{5,37},{6,38},{7,39},{8,40},{9,... | collective-permute-start | bytes 638984 | tf_op jit(solution)/shard_map/q_y1/ppermute | solution.py:38
  69.7 0.0 collective-permute-done.19.n2
  69.7 2.1 %collective-permute-start.22 = (s16[64,1664]{1,0:T(8,128)(2,1)S(1)}, s16[64,1664]{1,0:T(8,128)(2,1)S(1)}, u32[]{:S(2)}, u32[]{:S(2)}) collective-permute-start(s16[64,1664]{1,0:T(8,128)(2,1)S(1)} %get-tuple-element.141), channel_id=1, source_target_pairs={{0,64},{1,65},{2,66},{3,67},{4,68},{5,69},{6,70},{7,71},{8,72},{9,... | collective-permute-start | bytes 638984 | tf_op jit(solution)/shard_map/q_y2/ppermute | solution.py:38
  71.7 0.0 collective-permute-done.20.n3
  71.7 1.5 %collective-permute-start.23 = (s16[64,1664]{1,0:T(8,128)(2,1)S(1)}, s16[64,1664]{1,0:T(8,128)(2,1)S(1)}, u32[]{:S(2)}, u32[]{:S(2)}) collective-permute-start(s16[64,1664]{1,0:T(8,128)(2,1)S(1)} %get-tuple-element.142), channel_id=1, source_target_pairs={{0,96},{1,97},{2,98},{3,99},{4,100},{5,101},{6,102},{7,103},{8,104... | collective-permute-start | bytes 638984 | tf_op jit(solution)/shard_map/q_y3/ppermute | solution.py:38
  73.2 5.3 %direct_1.1 = (f32[128,2048]{1,0:T(8,128)S(1)}, f32[128,2048]{1,0:T(8,128)S(1)}) custom-call(s32[18]{0:T(128)S(1)} %pad_add_fusion.s_ref, bf16[64,4096]{1,0:T(8,128)(2,1)S(1)} %collective-permute-done.11.n0, bf16[64,4096]{1,0:T(8,128)(2,1)S(1)} %collective-permute-done.12.n1, bf16[64,4096]{1,0:T(8,128)(2,1)S(1)} %collective-permute-done.19.n2, ...), custom_call_target="tpu_custom_call" | custom-call | flops 10737418240 | bytes 52428980 | tf_op jit(solution)/shard_map/direct_1/pallas_call | solution.py:93
  78.5 3.4 %collective-permute-done.22.q2 = s16[64,1664]{1,0:T(8,128)(2,1)S(1)} collective-permute-done((s16[64,1664]{1,0:T(8,128)(2,1)S(1)}, s16[64,1664]{1,0:T(8,128)(2,1)S(1)}, u32[]{:S(2)}, u32[]{:S(2)}) %collective-permute-start.22) | collective-permute-done | bytes 213024 | tf_op jit(solution)/shard_map/q_y2/ppermute | solution.py:38
  81.9 2.6 %collective-permute-done.23.q3 = s16[64,1664]{1,0:T(8,128)(2,1)S(1)} collective-permute-done((s16[64,1664]{1,0:T(8,128)(2,1)S(1)}, s16[64,1664]{1,0:T(8,128)(2,1)S(1)}, u32[]{:S(2)}, u32[]{:S(2)}) %collective-permute-start.23) | collective-permute-done | bytes 213024 | tf_op jit(solution)/shard_map/q_y3/ppermute | solution.py:38
  84.5 0.4 core_0.1
  85.0 1.4 %collective-permute-start.10 = (s16[64,2176]{1,0:T(8,128)(2,1)S(1)}, s16[64,2176]{1,0:T(8,128)(2,1)S(1)}, u32[]{:S(2)}, u32[]{:S(2)}) collective-permute-start(s16[64,2176]{1,0:T(8,128)(2,1)S(1)} %get-tuple-element.106), channel_id=1, source_target_pairs={{0,2},{1,3},{2,0},{3,1},{4,6},{5,7},{6,4},{7,5},{8,10},{9,11},{10,... | collective-permute-start | bytes 835592 | tf_op jit(solution)/shard_map/chunk0_xh1/ppermute | solution.py:38
  86.3 1.8 %join.1 = (f32[16,4096]{1,0:T(8,128)S(1)}, s16[16,4224]{1,0:T(8,128)(2,1)S(1)}, s16[16,4224]{1,0:T(8,128)(2,1)S(1)}, s16[16,4224]{1,0:T(8,128)(2,1)S(1)}) custom-call(f32[64,2560]{1,0:T(8,128)S(1)} %get-tuple-element.145.p, s16[64,2688]{1,0:T(8,128)(2,1)S(1)} %collective-permute-done.18.p1, f32[64,1536]{1,0:T(8,128)S(1)} %get-tuple-element.147.q, ...), custom_call_target="tpu_custom_call" | custom-call | bytes 6748160 | tf_op jit(solution)/shard_map/join/pallas_call | solution.py:93
  88.1 0.4 core_1.1
  88.6 2.3 %collective-permute-start.25 = (s16[64,2176]{1,0:T(8,128)(2,1)S(1)}, s16[64,2176]{1,0:T(8,128)(2,1)S(1)}, u32[]{:S(2)}, u32[]{:S(2)}) collective-permute-start(s16[64,2176]{1,0:T(8,128)(2,1)S(1)} %get-tuple-element.158), channel_id=1, source_target_pairs={{0,2},{1,3},{2,0},{3,1},{4,6},{5,7},{6,4},{7,5},{8,10},{9,11},{10,... | collective-permute-start | bytes 835592 | tf_op jit(solution)/shard_map/chunk1_xh1/ppermute | solution.py:38
  90.9 1.0 collective-permute-start.26
  91.9 2.0 %collective-permute-start.27 = (s16[16,4224]{1,0:T(8,128)(2,1)S(1)}, s16[16,4224]{1,0:T(8,128)(2,1)S(1)}, u32[]{:S(2)}, u32[]{:S(2)}) collective-permute-start(s16[16,4224]{1,0:T(8,128)(2,1)S(1)} %get-tuple-element.161), channel_id=1, source_target_pairs={{0,16},{1,17},{2,18},{3,19},{4,20},{5,21},{6,22},{7,23},{8,24},{9,... | collective-permute-start | bytes 405512 | tf_op jit(solution)/shard_map/z_z2/ppermute | solution.py:38
  93.9 1.7 %collective-permute-start.28 = (s16[16,4224]{1,0:T(8,128)(2,1)S(1)}, s16[16,4224]{1,0:T(8,128)(2,1)S(1)}, u32[]{:S(2)}, u32[]{:S(2)}) collective-permute-start(s16[16,4224]{1,0:T(8,128)(2,1)S(1)} %get-tuple-element.162), channel_id=1, source_target_pairs={{0,24},{1,25},{2,26},{3,27},{4,28},{5,29},{6,30},{7,31},{8,16},{9,... | collective-permute-start | bytes 405512 | tf_op jit(solution)/shard_map/z_z3/ppermute | solution.py:38
  95.6 0.4 collective-permute-done.10.r0
  96.0 5.6 %collective-permute-done.25.r1 = s16[64,2176]{1,0:T(8,128)(2,1)S(1)} collective-permute-done((s16[64,2176]{1,0:T(8,128)(2,1)S(1)}, s16[64,2176]{1,0:T(8,128)(2,1)S(1)}, u32[]{:S(2)}, u32[]{:S(2)}) %collective-permute-start.25) | collective-permute-done | bytes 278560 | tf_op jit(solution)/shard_map/chunk1_xh1/ppermute | solution.py:38
  101.6 1.6 %finish_first.1 = bf16[128,2048]{1,0:T(8,128)(2,1)} custom-call(s32[18]{0:T(128)S(1)} %pad_add_fusion.s_ref, f32[64,2048]{1,0:T(8,128)S(1)} %get-tuple-element.105.k0, s16[64,2176]{1,0:T(8,128)(2,1)S(1)} %collective-permute-done.10.r0, f32[64,2048]{1,0:T(8,128)S(1)} %get-tuple-element.157.k1, s16[64,2176]{1,0:T(8,128)(2,1)S(1)} %collective-permute-done.25.r1), custom_call_target="tpu_custom_call" | custom-call | bytes 5324980 | tf_op jit(solution)/shard_map/finish_first/pallas_call | solution.py:93
  103.2 0.9 finish_second.1
  (27 shorter events, 0.1 us)
Async XLA Ops:
  0.6 9.6 %collective-permute-start.4 = (bf16[128,2048]{1,0:T(8,128)(2,1)}, bf16[128,2048]{1,0:T(8,128)(2,1)S(1)}, u32[]{:S(2)}, u32[]{:S(2)}) collective-permute-start(bf16[128,2048]{1,0:T(8,128)(2,1)} %f0.3), channel_id=1, source_target_pairs={{0,1},{1,0},{2,3},{3,2},{4,5},{5,4},{6,7},{7,6},{8,9},{9,8},{10,11... | collective-permute-start | bytes 1572872 | tf_op jit(solution)/shard_map/first_core1/ppermute | solution.py:38
  0.7 22.3 %collective-permute-start.3 = (bf16[128,2048]{1,0:T(8,128)(2,1)}, bf16[128,2048]{1,0:T(8,128)(2,1)S(1)}, u32[]{:S(2)}, u32[]{:S(2)}) collective-permute-start(bf16[128,2048]{1,0:T(8,128)(2,1)} %f0.3), channel_id=1, source_target_pairs={{0,2},{1,3},{2,0},{3,1},{4,6},{5,7},{6,4},{7,5},{8,10},{9,11},{10,... | collective-permute-start | bytes 1572872 | tf_op jit(solution)/shard_map/first_xh1/ppermute | solution.py:38
  3.9 19.1 %collective-permute-start = (bf16[16,4096]{1,0:T(8,128)(2,1)}, bf16[16,4096]{1,0:T(8,128)(2,1)S(1)}, u32[]{:S(2)}, u32[]{:S(2)}) collective-permute-start(bf16[16,4096]{1,0:T(8,128)(2,1)} %param.5), channel_id=1, source_target_pairs={{0,32},{1,33},{2,34},{3,35},{4,36},{5,37},{6,38},{7,39},{8,40},{9,... | collective-permute-start | bytes 393224 | tf_op jit(solution)/shard_map/second_y1/ppermute | solution.py:38
  5.5 17.6 %collective-permute-start.1 = (bf16[16,4096]{1,0:T(8,128)(2,1)}, bf16[16,4096]{1,0:T(8,128)(2,1)S(1)}, u32[]{:S(2)}, u32[]{:S(2)}) collective-permute-start(bf16[16,4096]{1,0:T(8,128)(2,1)} %param.5), channel_id=1, source_target_pairs={{0,64},{1,65},{2,66},{3,67},{4,68},{5,69},{6,70},{7,71},{8,72},{9,... | collective-permute-start | bytes 393224 | tf_op jit(solution)/shard_map/second_y2/ppermute | solution.py:38
  8.4 14.7 %collective-permute-start.2 = (bf16[16,4096]{1,0:T(8,128)(2,1)}, bf16[16,4096]{1,0:T(8,128)(2,1)S(1)}, u32[]{:S(2)}, u32[]{:S(2)}) collective-permute-start(bf16[16,4096]{1,0:T(8,128)(2,1)} %param.5), channel_id=1, source_target_pairs={{0,96},{1,97},{2,98},{3,99},{4,100},{5,101},{6,102},{7,103},{8,104... | collective-permute-start | bytes 393224 | tf_op jit(solution)/shard_map/second_y3/ppermute | solution.py:38
  10.3 5.8 %copy-start = (bf16[2048,4096]{1,0:T(8,128)(2,1)S(1)}, bf16[2048,4096]{1,0:T(8,128)(2,1)}, u32[]{:S(2)}) copy-start(bf16[2048,4096]{1,0:T(8,128)(2,1)} %i_ref.11) | copy-start | bytes 50331652
  16.0 1.0 %copy-start.1 = (bf16[128,2048]{1,0:T(8,128)(2,1)S(1)}, bf16[128,2048]{1,0:T(8,128)(2,1)}, u32[]{:S(2)}) copy-start(bf16[128,2048]{1,0:T(8,128)(2,1)} %f0.3) | copy-start | bytes 1572868
  23.1 5.3 %collective-permute-start.8 = (bf16[128,2048]{1,0:T(8,128)(2,1)S(1)}, bf16[128,2048]{1,0:T(8,128)(2,1)S(1)}, u32[]{:S(2)}, u32[]{:S(2)}) collective-permute-start(bf16[128,2048]{1,0:T(8,128)(2,1)S(1)} %collective-permute-done.3.f2), channel_id=1, source_target_pairs={{0,1},{1,0},{2,3},{3,2},{4,5},{5,4},{6,7},{7,6},{8,9},{9,8},{10,11... | collective-permute-start | bytes 1572872 | tf_op jit(solution)/shard_map/first_core1/ppermute | solution.py:38
  23.2 15.5 %collective-permute-start.5 = (bf16[64,4096]{1,0:T(8,128)(2,1)S(1)}, bf16[64,4096]{1,0:T(8,128)(2,1)S(1)}, u32[]{:S(2)}, u32[]{:S(2)}) collective-permute-start(bf16[64,4096]{1,0:T(8,128)(2,1)S(1)} %constant_dynamic-update-slice_fusion.n0), channel_id=1, source_target_pairs={{0,4},{1,5},{2,6},{3,7},{4,0},{5,1},{6,2},{7,3},{8,12},{9,13},{10,... | collective-permute-start | bytes 1572872 | tf_op jit(solution)/shard_map/n_xl1/ppermute | solution.py:38
  23.9 14.9 %collective-permute-start.6 = (bf16[64,4096]{1,0:T(8,128)(2,1)S(1)}, bf16[64,4096]{1,0:T(8,128)(2,1)S(1)}, u32[]{:S(2)}, u32[]{:S(2)}) collective-permute-start(bf16[64,4096]{1,0:T(8,128)(2,1)S(1)} %constant_dynamic-update-slice_fusion.n0), channel_id=1, source_target_pairs={{0,8},{1,9},{2,10},{3,11},{4,12},{5,13},{6,14},{7,15},{8,0},{9,1},... | collective-permute-start | bytes 1572872 | tf_op jit(solution)/shard_map/n_z1/ppermute | solution.py:38
  25.8 15.0 %collective-permute-start.7 = (bf16[64,4096]{1,0:T(8,128)(2,1)S(1)}, bf16[64,4096]{1,0:T(8,128)(2,1)S(1)}, u32[]{:S(2)}, u32[]{:S(2)}) collective-permute-start(bf16[64,4096]{1,0:T(8,128)(2,1)S(1)} %constant_dynamic-update-slice_fusion.n0), channel_id=1, source_target_pairs={{0,24},{1,25},{2,26},{3,27},{4,28},{5,29},{6,30},{7,31},{8,16},{9,... | collective-permute-start | bytes 1572872 | tf_op jit(solution)/shard_map/n_z3/ppermute | solution.py:38
  28.3 30.2 %slice-start = ((s8[16777216]{0:T(1024)(128)(4,1)}), s8[4194304]{0:T(1024)(128)(4,1)S(1)}, s32[]{:S(2)}) async-start(s8[16777216]{0:T(1024)(128)(4,1)} %bitcast.3), calls=%async_computation | async-start | bytes 8388608
  28.3 30.2 %slice-start.1 = ((s8[16777216]{0:T(1024)(128)(4,1)}), s8[4194304]{0:T(1024)(128)(4,1)S(1)}, s32[]{:S(2)}) async-start(s8[16777216]{0:T(1024)(128)(4,1)} %bitcast.3), calls=%async_computation.1 | async-start | bytes 8388608
  28.3 30.2 %slice-start.2 = ((s8[16777216]{0:T(1024)(128)(4,1)}), s8[4194304]{0:T(1024)(128)(4,1)S(1)}, s32[]{:S(2)}) async-start(s8[16777216]{0:T(1024)(128)(4,1)} %bitcast.3), calls=%async_computation.2 | async-start | bytes 8388608
  32.6 19.0 %collective-permute-start.13 = (s16[256,1408]{1,0:T(8,128)(2,1)S(1)}, s16[256,1408]{1,0:T(8,128)(2,1)S(1)}, u32[]{:S(2)}, u32[]{:S(2)}) collective-permute-start(s16[256,1408]{1,0:T(8,128)(2,1)S(1)} %get-tuple-element.108), channel_id=1, source_target_pairs={{0,96},{1,97},{2,98},{3,99},{4,100},{5,101},{6,102},{7,103},{8,104... | collective-permute-start | bytes 2162696 | tf_op jit(solution)/shard_map/pa_y3/ppermute | solution.py:38
  35.7 22.8 %slice-start.3 = ((s8[16777216]{0:T(1024)(128)(4,1)}), s8[4194304]{0:T(1024)(128)(4,1)S(1)}, s32[]{:S(2)}) async-start(s8[16777216]{0:T(1024)(128)(4,1)} %bitcast.3), calls=%async_computation.3 | async-start | bytes 8388608
  35.7 17.4 %collective-permute-start.14 = (s16[256,1408]{1,0:T(8,128)(2,1)S(1)}, s16[256,1408]{1,0:T(8,128)(2,1)S(1)}, u32[]{:S(2)}, u32[]{:S(2)}) collective-permute-start(s16[256,1408]{1,0:T(8,128)(2,1)S(1)} %get-tuple-element.110), channel_id=1, source_target_pairs={{0,32},{1,33},{2,34},{3,35},{4,36},{5,37},{6,38},{7,39},{8,40},{9,... | collective-permute-start | bytes 2162696 | tf_op jit(solution)/shard_map/pb_y1/ppermute | solution.py:38
  40.8 15.6 %collective-permute-start.11 = (bf16[64,4096]{1,0:T(8,128)(2,1)S(1)}, bf16[64,4096]{1,0:T(8,128)(2,1)S(1)}, u32[]{:S(2)}, u32[]{:S(2)}) collective-permute-start(bf16[64,4096]{1,0:T(8,128)(2,1)S(1)} %collective-permute-done.5.n1), channel_id=1, source_target_pairs={{0,8},{1,9},{2,10},{3,11},{4,12},{5,13},{6,14},{7,15},{8,0},{9,1},... | collective-permute-start | bytes 1572872 | tf_op jit(solution)/shard_map/x_z1/ppermute | solution.py:38
  41.4 15.1 %collective-permute-start.12 = (bf16[64,4096]{1,0:T(8,128)(2,1)S(1)}, bf16[64,4096]{1,0:T(8,128)(2,1)S(1)}, u32[]{:S(2)}, u32[]{:S(2)}) collective-permute-start(bf16[64,4096]{1,0:T(8,128)(2,1)S(1)} %collective-permute-done.5.n1), channel_id=1, source_target_pairs={{0,24},{1,25},{2,26},{3,27},{4,28},{5,29},{6,30},{7,31},{8,16},{9,... | collective-permute-start | bytes 1572872 | tf_op jit(solution)/shard_map/x_z3/ppermute | solution.py:38
  43.7 20.2 %collective-permute-start.17 = (s16[256,1664]{1,0:T(8,128)(2,1)S(1)}, s16[256,1664]{1,0:T(8,128)(2,1)S(1)}, u32[]{:S(2)}, u32[]{:S(2)}) collective-permute-start(s16[256,1664]{1,0:T(8,128)(2,1)S(1)} %get-tuple-element.124), channel_id=1, source_target_pairs={{0,4},{1,5},{2,6},{3,7},{4,0},{5,1},{6,2},{7,3},{8,12},{9,13},{10,... | collective-permute-start | bytes 2555912 | tf_op jit(solution)/shard_map/q_xl1/ppermute | solution.py:38
  54.0 11.0 %collective-permute-start.16 = (s16[128,1408]{1,0:T(8,128)(2,1)S(1)}, s16[128,1408]{1,0:T(8,128)(2,1)S(1)}, u32[]{:S(2)}, u32[]{:S(2)}) collective-permute-start(s16[128,1408]{1,0:T(8,128)(2,1)S(1)} %get-tuple-element.120), channel_id=1, source_target_pairs={{0,96},{1,97},{2,98},{3,99},{4,100},{5,101},{6,102},{7,103},{8,104... | collective-permute-start | bytes 1081352 | tf_op jit(solution)/shard_map/pb_y3/ppermute | solution.py:38
  56.4 8.9 %collective-permute-start.15 = (s16[128,1408]{1,0:T(8,128)(2,1)S(1)}, s16[128,1408]{1,0:T(8,128)(2,1)S(1)}, u32[]{:S(2)}, u32[]{:S(2)}) collective-permute-start(s16[128,1408]{1,0:T(8,128)(2,1)S(1)} %get-tuple-element.118), channel_id=1, source_target_pairs={{0,32},{1,33},{2,34},{3,35},{4,36},{5,37},{6,38},{7,39},{8,40},{9,... | collective-permute-start | bytes 1081352 | tf_op jit(solution)/shard_map/pa_y1/ppermute | solution.py:38
  56.5 13.2 %collective-permute-start.19 = (bf16[64,4096]{1,0:T(8,128)(2,1)S(1)}, bf16[64,4096]{1,0:T(8,128)(2,1)S(1)}, u32[]{:S(2)}, u32[]{:S(2)}) collective-permute-start(bf16[64,4096]{1,0:T(8,128)(2,1)S(1)} %collective-permute-done.7.n3), channel_id=1, source_target_pairs={{0,8},{1,9},{2,10},{3,11},{4,12},{5,13},{6,14},{7,15},{8,0},{9,1},... | collective-permute-start | bytes 1572872 | tf_op jit(solution)/shard_map/n3_z1/ppermute | solution.py:38
  57.6 14.1 %collective-permute-start.20 = (bf16[64,4096]{1,0:T(8,128)(2,1)S(1)}, bf16[64,4096]{1,0:T(8,128)(2,1)S(1)}, u32[]{:S(2)}, u32[]{:S(2)}) collective-permute-start(bf16[64,4096]{1,0:T(8,128)(2,1)S(1)} %collective-permute-done.11.n0), channel_id=1, source_target_pairs={{0,24},{1,25},{2,26},{3,27},{4,28},{5,29},{6,30},{7,31},{8,16},{9,... | collective-permute-start | bytes 1572872 | tf_op jit(solution)/shard_map/x1_z3/ppermute | solution.py:38
  63.9 20.7 %collective-permute-start.9 = (f32[128,2048]{1,0:T(8,128)S(1)}, f32[128,2048]{1,0:T(8,128)S(1)}, u32[]{:S(2)}, u32[]{:S(2)}) collective-permute-start(f32[128,2048]{1,0:T(8,128)S(1)} %get-tuple-element.104), channel_id=1, source_target_pairs={{0,1},{1,0},{2,3},{3,2},{4,5},{5,4},{6,7},{7,6},{8,9},{9,8},{10,11... | collective-permute-start | bytes 3145736 | tf_op jit(solution)/shard_map/chunk0_core1/ppermute | solution.py:38
  66.5 18.1 %collective-permute-start.18 = (s16[64,2688]{1,0:T(8,128)(2,1)S(1)}, s16[64,2688]{1,0:T(8,128)(2,1)S(1)}, u32[]{:S(2)}, u32[]{:S(2)}) collective-permute-start(s16[64,2688]{1,0:T(8,128)(2,1)S(1)} %get-tuple-element.129), channel_id=1, source_target_pairs={{0,4},{1,5},{2,6},{3,7},{4,0},{5,1},{6,2},{7,3},{8,12},{9,13},{10,... | collective-permute-start | bytes 1032200 | tf_op jit(solution)/shard_map/p_xl1/ppermute | solution.py:38
  68.0 10.5 %collective-permute-start.21 = (s16[64,1664]{1,0:T(8,128)(2,1)S(1)}, s16[64,1664]{1,0:T(8,128)(2,1)S(1)}, u32[]{:S(2)}, u32[]{:S(2)}) collective-permute-start(s16[64,1664]{1,0:T(8,128)(2,1)S(1)} %get-tuple-element.140), channel_id=1, source_target_pairs={{0,32},{1,33},{2,34},{3,35},{4,36},{5,37},{6,38},{7,39},{8,40},{9,... | collective-permute-start | bytes 638984 | tf_op jit(solution)/shard_map/q_y1/ppermute | solution.py:38
  69.7 12.3 %collective-permute-start.22 = (s16[64,1664]{1,0:T(8,128)(2,1)S(1)}, s16[64,1664]{1,0:T(8,128)(2,1)S(1)}, u32[]{:S(2)}, u32[]{:S(2)}) collective-permute-start(s16[64,1664]{1,0:T(8,128)(2,1)S(1)} %get-tuple-element.141), channel_id=1, source_target_pairs={{0,64},{1,65},{2,66},{3,67},{4,68},{5,69},{6,70},{7,71},{8,72},{9,... | collective-permute-start | bytes 638984 | tf_op jit(solution)/shard_map/q_y2/ppermute | solution.py:38
  71.7 12.8 %collective-permute-start.23 = (s16[64,1664]{1,0:T(8,128)(2,1)S(1)}, s16[64,1664]{1,0:T(8,128)(2,1)S(1)}, u32[]{:S(2)}, u32[]{:S(2)}) collective-permute-start(s16[64,1664]{1,0:T(8,128)(2,1)S(1)} %get-tuple-element.142), channel_id=1, source_target_pairs={{0,96},{1,97},{2,98},{3,99},{4,100},{5,101},{6,102},{7,103},{8,104... | collective-permute-start | bytes 638984 | tf_op jit(solution)/shard_map/q_y3/ppermute | solution.py:38
  84.5 3.6 %collective-permute-start.24 = (f32[128,2048]{1,0:T(8,128)S(1)}, f32[128,2048]{1,0:T(8,128)S(1)}, u32[]{:S(2)}, u32[]{:S(2)}) collective-permute-start(f32[128,2048]{1,0:T(8,128)S(1)} %get-tuple-element.144), channel_id=1, source_target_pairs={{0,1},{1,0},{2,3},{3,2},{4,5},{5,4},{6,7},{7,6},{8,9},{9,8},{10,11... | collective-permute-start | bytes 3145736 | tf_op jit(solution)/shard_map/chunk1_core1/ppermute | solution.py:38
  85.0 11.0 %collective-permute-start.10 = (s16[64,2176]{1,0:T(8,128)(2,1)S(1)}, s16[64,2176]{1,0:T(8,128)(2,1)S(1)}, u32[]{:S(2)}, u32[]{:S(2)}) collective-permute-start(s16[64,2176]{1,0:T(8,128)(2,1)S(1)} %get-tuple-element.106), channel_id=1, source_target_pairs={{0,2},{1,3},{2,0},{3,1},{4,6},{5,7},{6,4},{7,5},{8,10},{9,11},{10,... | collective-permute-start | bytes 835592 | tf_op jit(solution)/shard_map/chunk0_xh1/ppermute | solution.py:38
  88.6 13.0 %collective-permute-start.25 = (s16[64,2176]{1,0:T(8,128)(2,1)S(1)}, s16[64,2176]{1,0:T(8,128)(2,1)S(1)}, u32[]{:S(2)}, u32[]{:S(2)}) collective-permute-start(s16[64,2176]{1,0:T(8,128)(2,1)S(1)} %get-tuple-element.158), channel_id=1, source_target_pairs={{0,2},{1,3},{2,0},{3,1},{4,6},{5,7},{6,4},{7,5},{8,10},{9,11},{10,... | collective-permute-start | bytes 835592 | tf_op jit(solution)/shard_map/chunk1_xh1/ppermute | solution.py:38
  90.9 12.3 %collective-permute-start.26 = (s16[16,4224]{1,0:T(8,128)(2,1)S(1)}, s16[16,4224]{1,0:T(8,128)(2,1)S(1)}, u32[]{:S(2)}, u32[]{:S(2)}) collective-permute-start(s16[16,4224]{1,0:T(8,128)(2,1)S(1)} %get-tuple-element.160), channel_id=1, source_target_pairs={{0,8},{1,9},{2,10},{3,11},{4,12},{5,13},{6,14},{7,15},{8,0},{9,1},... | collective-permute-start | bytes 405512 | tf_op jit(solution)/shard_map/z_z1/ppermute | solution.py:38
  91.9 11.3 %collective-permute-start.27 = (s16[16,4224]{1,0:T(8,128)(2,1)S(1)}, s16[16,4224]{1,0:T(8,128)(2,1)S(1)}, u32[]{:S(2)}, u32[]{:S(2)}) collective-permute-start(s16[16,4224]{1,0:T(8,128)(2,1)S(1)} %get-tuple-element.161), channel_id=1, source_target_pairs={{0,16},{1,17},{2,18},{3,19},{4,20},{5,21},{6,22},{7,23},{8,24},{9,... | collective-permute-start | bytes 405512 | tf_op jit(solution)/shard_map/z_z2/ppermute | solution.py:38
  93.9 9.3 %collective-permute-start.28 = (s16[16,4224]{1,0:T(8,128)(2,1)S(1)}, s16[16,4224]{1,0:T(8,128)(2,1)S(1)}, u32[]{:S(2)}, u32[]{:S(2)}) collective-permute-start(s16[16,4224]{1,0:T(8,128)(2,1)S(1)} %get-tuple-element.162), channel_id=1, source_target_pairs={{0,24},{1,25},{2,26},{3,27},{4,28},{5,29},{6,30},{7,31},{8,16},{9,... | collective-permute-start | bytes 405512 | tf_op jit(solution)/shard_map/z_z3/ppermute | solution.py:38

commit v4 on v3

--- a/solution.py
+++ b/solution.py
@@ -12,8 +12,8 @@
 TILE = 256
 OCC, NA_D, NB_D, CT = 512, 2048, 4096, 16
 TN = 512
-CN = 256
-P_WIDE = 2560
+CN = 512
+P_WIDE = 3072
 P_HALF = P_WIDE // 2
 Q_WIDE = NB_D - P_WIDE
 LEVELS = 32766.0
@@ -407,7 +407,7 @@
     y1, y2, y3 = [swap("second", second, y=r) for r in (1, 2, 3)]
     sums_p = early(scalars, (amp_first, first_core), integrals, 0, P_WIDE, "early_p")
     sums_q = early(scalars, (amp_first, first_core), integrals, P_WIDE, Q_WIDE, "early_q")
-    y1, y2, y3, scalars, first_xh, sums_p, sums_q = together(y1, y2, y3, scalars, first_xh, sums_p, sums_q)
+    y1, y2, y3, scalars, sums_p = together(y1, y2, y3, scalars, sums_p)
     n0 = jnp.concatenate([second, y1, y2, y3])
     first_both = swap("first", first_xh, core=1)
     x0 = swap("n", n0, xl=1)

time: 105 us -> 101 us (0.962)
  Pallas kernels: 32.8 us -> 30.2 us
    pallas_call x15, Pallas kernels: 32.8 us -> 30.2 us  [call(): pl.pallas_call(kernel, in_specs=[pl.BlockSpec(memory_space=pltpu.SMEM)] *...]
    unnamed x15 -> x17, local copies, waits for them, and re-layouts: 7.76 us -> 7.77 us
  transfers between devices with their start and end apart: 29 -> 29, of which waited for: 8 -> 9; matrix products, arithmetic and copies ran while one was open for 2% -> 2% of each run, Pallas kernels for 31% -> 29%
where the time goes in v4:
time: 101 us
  starting transfers between devices  38.7 us (38%)
  Pallas kernels  30.2 us (30%)
  waiting for transfers between devices  22.1 us (22%)
  local copies, waits for them, and re-layouts  7.78 us (8%)
    ppermute x29, starting transfers between devices, swap(): return lax.ppermute(value, ('row', 'col'), exchange_pairs(**flips))  38.7 us
    pallas_call x15, Pallas kernels, call(): pl.pallas_call(kernel, in_specs=[pl.BlockSpec(memory_space=pltpu.SMEM)] *...  30.2 us
    ppermute x29, waiting for transfers between devices, swap(): return lax.ppermute(value, ('row', 'col'), exchange_pairs(**flips))  22.1 us
    unnamed x17, local copies, waits for them, and re-layouts  7.77 us
  transfers between devices with their start and end apart: 29, of which 9 were waited for; matrix products, arithmetic and copies ran while one was open for 2% of the time, Pallas kernels for 29%

profile of v4, /device:TPU:0, one launch (start us, length us, event | category | flops | bytes accessed | tf_op | source)
XLA Modules:
  0.0 100.5 jit_solution(1579685283646564356)
XLA Ops:
  0.6 1.7 %collective-permute-start = (bf16[16,4096]{1,0:T(8,128)(2,1)}, bf16[16,4096]{1,0:T(8,128)(2,1)S(1)}, u32[]{:S(2)}, u32[]{:S(2)}) collective-permute-start(bf16[16,4096]{1,0:T(8,128)(2,1)} %param.5), channel_id=1, source_target_pairs={{0,32},{1,33},{2,34},{3,35},{4,36},{5,37},{6,38},{7,39},{8,40},{9,... | collective-permute-start | bytes 393224 | tf_op jit(solution)/shard_map/second_y1/ppermute | solution.py:38
  2.4 2.9 %collective-permute-start.1 = (bf16[16,4096]{1,0:T(8,128)(2,1)}, bf16[16,4096]{1,0:T(8,128)(2,1)S(1)}, u32[]{:S(2)}, u32[]{:S(2)}) collective-permute-start(bf16[16,4096]{1,0:T(8,128)(2,1)} %param.5), channel_id=1, source_target_pairs={{0,64},{1,65},{2,66},{3,67},{4,68},{5,69},{6,70},{7,71},{8,72},{9,... | collective-permute-start | bytes 393224 | tf_op jit(solution)/shard_map/second_y2/ppermute | solution.py:38
  5.3 0.1 collective-permute-start.2
  5.4 0.0 collective-permute-start.3
  5.4 3.1 %collective-permute-start.7 = (bf16[128,2048]{1,0:T(8,128)(2,1)}, bf16[128,2048]{1,0:T(8,128)(2,1)S(1)}, u32[]{:S(2)}, u32[]{:S(2)}) collective-permute-start(bf16[128,2048]{1,0:T(8,128)(2,1)} %f0.3), channel_id=1, source_target_pairs={{0,2},{1,3},{2,0},{3,1},{4,6},{5,7},{6,4},{7,5},{8,10},{9,11},{10,... | collective-permute-start | bytes 1572872 | tf_op jit(solution)/shard_map/first_xh1/ppermute | solution.py:38
  8.5 0.7 pad_add_fusion.s_ref
  9.2 0.9 constant_dynamic-update-slice_fusion.3
  10.2 0.0 collective-permute-done.3.f1
  10.2 0.0 copy-start
  10.2 5.8 %copy-done = bf16[2048,4096]{1,0:T(8,128)(2,1)S(1)} copy-done((bf16[2048,4096]{1,0:T(8,128)(2,1)S(1)}, bf16[2048,4096]{1,0:T(8,128)(2,1)}, u32[]{:S(2)}) %copy-start) | copy-done | bytes 16777240
  16.0 1.0 %copy-done.1 = bf16[128,2048]{1,0:T(8,128)(2,1)S(1)} copy-done((bf16[128,2048]{1,0:T(8,128)(2,1)S(1)}, bf16[128,2048]{1,0:T(8,128)(2,1)}, u32[]{:S(2)}) %copy-start.1) | copy-done | bytes 524312
  17.0 4.1 %early_p.1.early_ref = f32[256,3072]{1,0:T(8,128)S(1)} custom-call(s32[18]{0:T(128)S(1)} %pad_add_fusion.s_ref, bf16[128,2048]{1,0:T(8,128)(2,1)S(1)} %copy-done.1, bf16[128,2048]{1,0:T(8,128)(2,1)S(1)} %collective-permute-done.3.f1, bf16[2048,4096]{1,0:T(8,128)(2,1)S(1)} %copy-done), custom_call_target="tpu_custom_call" | custom-call | flops 8053063680 | bytes 52428980 | tf_op jit(solution)/shard_map/early_p/pallas_call | solution.py:93
  21.1 0.0 collective-permute-done
  21.1 0.0 collective-permute-done.1
  21.1 0.3 collective-permute-done.7.f2
  21.5 0.0 collective-permute-start.8
  21.5 0.0 copy-start.2
  21.5 1.7 %collective-permute-start.4 = (bf16[64,4096]{1,0:T(8,128)(2,1)S(1)}, bf16[64,4096]{1,0:T(8,128)(2,1)S(1)}, u32[]{:S(2)}, u32[]{:S(2)}) collective-permute-start(bf16[64,4096]{1,0:T(8,128)(2,1)S(1)} %constant_dynamic-update-slice_fusion.n0), channel_id=1, source_target_pairs={{0,4},{1,5},{2,6},{3,7},{4,0},{5,1},{6,2},{7,3},{8,12},{9,13},{10,... | collective-permute-start | bytes 1572872 | tf_op jit(solution)/shard_map/n_xl1/ppermute | solution.py:38
  23.2 1.9 %collective-permute-start.5 = (bf16[64,4096]{1,0:T(8,128)(2,1)S(1)}, bf16[64,4096]{1,0:T(8,128)(2,1)S(1)}, u32[]{:S(2)}, u32[]{:S(2)}) collective-permute-start(bf16[64,4096]{1,0:T(8,128)(2,1)S(1)} %constant_dynamic-update-slice_fusion.n0), channel_id=1, source_target_pairs={{0,8},{1,9},{2,10},{3,11},{4,12},{5,13},{6,14},{7,15},{8,0},{9,1},... | collective-permute-start | bytes 1572872 | tf_op jit(solution)/shard_map/n_z1/ppermute | solution.py:38
  25.1 2.5 %collective-permute-start.6 = (bf16[64,4096]{1,0:T(8,128)(2,1)S(1)}, bf16[64,4096]{1,0:T(8,128)(2,1)S(1)}, u32[]{:S(2)}, u32[]{:S(2)}) collective-permute-start(bf16[64,4096]{1,0:T(8,128)(2,1)S(1)} %constant_dynamic-update-slice_fusion.n0), channel_id=1, source_target_pairs={{0,24},{1,25},{2,26},{3,27},{4,28},{5,29},{6,30},{7,31},{8,16},{9,... | collective-permute-start | bytes 1572872 | tf_op jit(solution)/shard_map/n_z3/ppermute | solution.py:38
  27.6 0.0 collective-permute-done.8.f3
  27.6 4.9 %mirror_p.1 = (f32[256,1536]{1,0:T(8,128)S(1)}, s16[256,1664]{1,0:T(8,128)(2,1)S(1)}, f32[256,1536]{1,0:T(8,128)S(1)}, s16[256,1664]{1,0:T(8,128)(2,1)S(1)}) custom-call(s32[18]{0:T(128)S(1)} %pad_add_fusion.s_ref, bf16[128,2048]{1,0:T(8,128)(2,1)S(1)} %collective-permute-done.7.f2, bf16[128,2048]{1,0:T(8,128)(2,1)S(1)} %collective-permute-done.8.f3, ...), custom_call_target="tpu_custom_call" | custom-call | flops 8053063680 | bytes 64553140 | tf_op jit(solution)/shard_map/mirror_p/pallas_call | solution.py:93
  32.5 3.1 %collective-permute-start.13 = (s16[256,1664]{1,0:T(8,128)(2,1)S(1)}, s16[256,1664]{1,0:T(8,128)(2,1)S(1)}, u32[]{:S(2)}, u32[]{:S(2)}) collective-permute-start(s16[256,1664]{1,0:T(8,128)(2,1)S(1)} %get-tuple-element.104), channel_id=1, source_target_pairs={{0,96},{1,97},{2,98},{3,99},{4,100},{5,101},{6,102},{7,103},{8,104... | collective-permute-start | bytes 2555912 | tf_op jit(solution)/shard_map/pa_y3/ppermute | solution.py:38
  35.6 1.9 %early_q.1.early_ref = f32[256,1024]{1,0:T(8,128)S(1)} custom-call(s32[18]{0:T(128)S(1)} %pad_add_fusion.s_ref, bf16[128,2048]{1,0:T(8,128)(2,1)S(1)} %copy-done.2, bf16[128,2048]{1,0:T(8,128)(2,1)S(1)} %collective-permute-done.3.f1, bf16[2048,4096]{1,0:T(8,128)(2,1)S(1)} %copy-done), custom_call_target="tpu_custom_call" | custom-call | flops 2684354560 | bytes 47186100 | tf_op jit(solution)/shard_map/early_q/pallas_call | solution.py:93
  37.5 0.0 slice-start.2
  37.5 0.0 slice-start.3
  37.5 2.2 %mirror_q.1 = (f32[256,1024]{1,0:T(8,128)S(1)}, s16[256,1152]{1,0:T(8,128)(2,1)S(1)}) custom-call(s32[18]{0:T(128)S(1)} %pad_add_fusion.s_ref, bf16[128,2048]{1,0:T(8,128)(2,1)S(1)} %collective-permute-done.7.f2, bf16[128,2048]{1,0:T(8,128)(2,1)S(1)} %collective-permute-done.8.f3, f32[256,1024]{1,0:T(8,128)S(1)} %early_q.1.early_ref, ...), custom_call_target="tpu_custom_call" | custom-call | flops 2684354560 | bytes 51282100 | tf_op jit(solution)/shard_map/mirror_q/pallas_call | solution.py:93
  39.8 0.3 collective-permute-done.6.n3
  40.1 0.8 collective-permute-start.11
  40.9 2.1 %collective-permute-start.12 = (bf16[64,4096]{1,0:T(8,128)(2,1)S(1)}, bf16[64,4096]{1,0:T(8,128)(2,1)S(1)}, u32[]{:S(2)}, u32[]{:S(2)}) collective-permute-start(bf16[64,4096]{1,0:T(8,128)(2,1)S(1)} %collective-permute-done.4.n1), channel_id=1, source_target_pairs={{0,24},{1,25},{2,26},{3,27},{4,28},{5,29},{6,30},{7,31},{8,16},{9,... | collective-permute-start | bytes 1572872 | tf_op jit(solution)/shard_map/x_z3/ppermute | solution.py:38
  43.0 0.5 collective-permute-start.17
  43.5 10.8 %collective-permute-done.13.other = s16[256,1664]{1,0:T(8,128)(2,1)S(1)} collective-permute-done((s16[256,1664]{1,0:T(8,128)(2,1)S(1)}, s16[256,1664]{1,0:T(8,128)(2,1)S(1)}, u32[]{:S(2)}, u32[]{:S(2)}) %collective-permute-start.13) | collective-permute-done | bytes 852000 | tf_op jit(solution)/shard_map/pa_y3/ppermute | solution.py:38
  54.4 1.5 %collective-permute-done.14.other = s16[256,1664]{1,0:T(8,128)(2,1)S(1)} collective-permute-done((s16[256,1664]{1,0:T(8,128)(2,1)S(1)}, s16[256,1664]{1,0:T(8,128)(2,1)S(1)}, u32[]{:S(2)}, u32[]{:S(2)}) %collective-permute-start.14) | collective-permute-done | bytes 852000 | tf_op jit(solution)/shard_map/pb_y1/ppermute | solution.py:38
  55.8 0.6 fold_pb.1
  56.5 1.6 %collective-permute-start.16 = (s16[128,1664]{1,0:T(8,128)(2,1)S(1)}, s16[128,1664]{1,0:T(8,128)(2,1)S(1)}, u32[]{:S(2)}, u32[]{:S(2)}) collective-permute-start(s16[128,1664]{1,0:T(8,128)(2,1)S(1)} %get-tuple-element.116), channel_id=1, source_target_pairs={{0,96},{1,97},{2,98},{3,99},{4,100},{5,101},{6,102},{7,103},{8,104... | collective-permute-start | bytes 1277960 | tf_op jit(solution)/shard_map/pb_y3/ppermute | solution.py:38
  58.0 0.6 fold_pa.1
  58.7 0.1 collective-permute-start.15
  58.8 1.1 %collective-permute-start.19 = (bf16[64,4096]{1,0:T(8,128)(2,1)S(1)}, bf16[64,4096]{1,0:T(8,128)(2,1)S(1)}, u32[]{:S(2)}, u32[]{:S(2)}) collective-permute-start(bf16[64,4096]{1,0:T(8,128)(2,1)S(1)} %collective-permute-done.6.n3), channel_id=1, source_target_pairs={{0,8},{1,9},{2,10},{3,11},{4,12},{5,13},{6,14},{7,15},{8,0},{9,1},... | collective-permute-start | bytes 1572872 | tf_op jit(solution)/shard_map/n3_z1/ppermute | solution.py:38
  59.9 0.9 collective-permute-start.20
  60.8 5.3 %direct_0.1 = (f32[128,2048]{1,0:T(8,128)S(1)}, f32[128,2048]{1,0:T(8,128)S(1)}) custom-call(s32[18]{0:T(128)S(1)} %pad_add_fusion.s_ref, bf16[64,4096]{1,0:T(8,128)(2,1)S(1)} %constant_dynamic-update-slice_fusion.n0, bf16[64,4096]{1,0:T(8,128)(2,1)S(1)} %collective-permute-done.4.n1, bf16[64,4096]{1,0:T(8,128)(2,1)S(1)} %collective-permute-done.5.n2, ...), custom_call_target="tpu_custom_call" | custom-call | flops 10737418240 | bytes 52428980 | tf_op jit(solution)/shard_map/direct_0/pallas_call | solution.py:93
  66.1 0.1 collective-permute-start.9
  66.2 0.5 fold_q_xl.1
  66.7 1.2 %collective-permute-done.16.b1 = s16[128,1664]{1,0:T(8,128)(2,1)S(1)} collective-permute-done((s16[128,1664]{1,0:T(8,128)(2,1)S(1)}, s16[128,1664]{1,0:T(8,128)(2,1)S(1)}, u32[]{:S(2)}, u32[]{:S(2)}) %collective-permute-start.16) | collective-permute-done | bytes 426016 | tf_op jit(solution)/shard_map/pb_y3/ppermute | solution.py:38
  67.9 1.0 %collective-permute-done.15.a1 = s16[128,1664]{1,0:T(8,128)(2,1)S(1)} collective-permute-done((s16[128,1664]{1,0:T(8,128)(2,1)S(1)}, s16[128,1664]{1,0:T(8,128)(2,1)S(1)}, u32[]{:S(2)}, u32[]{:S(2)}) %collective-permute-start.15) | collective-permute-done | bytes 426016 | tf_op jit(solution)/shard_map/pa_y1/ppermute | solution.py:38
  69.0 0.8 merge.1
  69.8 0.6 collective-permute-start.18
  70.4 0.3 collective-permute-start.21
  70.7 0.5 collective-permute-done.19.n2
  71.2 2.5 %collective-permute-start.22 = (s16[64,1152]{1,0:T(8,128)(2,1)S(1)}, s16[64,1152]{1,0:T(8,128)(2,1)S(1)}, u32[]{:S(2)}, u32[]{:S(2)}) collective-permute-start(s16[64,1152]{1,0:T(8,128)(2,1)S(1)} %get-tuple-element.137), channel_id=1, source_target_pairs={{0,64},{1,65},{2,66},{3,67},{4,68},{5,69},{6,70},{7,71},{8,72},{9,... | collective-permute-start | bytes 442376 | tf_op jit(solution)/shard_map/q_y2/ppermute | solution.py:38
  73.7 1.8 %collective-permute-start.23 = (s16[64,1152]{1,0:T(8,128)(2,1)S(1)}, s16[64,1152]{1,0:T(8,128)(2,1)S(1)}, u32[]{:S(2)}, u32[]{:S(2)}) collective-permute-start(s16[64,1152]{1,0:T(8,128)(2,1)S(1)} %get-tuple-element.138), channel_id=1, source_target_pairs={{0,96},{1,97},{2,98},{3,99},{4,100},{5,101},{6,102},{7,103},{8,104... | collective-permute-start | bytes 442376 | tf_op jit(solution)/shard_map/q_y3/ppermute | solution.py:38
  75.5 5.3 %direct_1.1 = (f32[128,2048]{1,0:T(8,128)S(1)}, f32[128,2048]{1,0:T(8,128)S(1)}) custom-call(s32[18]{0:T(128)S(1)} %pad_add_fusion.s_ref, bf16[64,4096]{1,0:T(8,128)(2,1)S(1)} %collective-permute-done.11.n0, bf16[64,4096]{1,0:T(8,128)(2,1)S(1)} %collective-permute-done.12.n1, bf16[64,4096]{1,0:T(8,128)(2,1)S(1)} %collective-permute-done.19.n2, ...), custom_call_target="tpu_custom_call" | custom-call | flops 10737418240 | bytes 52428980 | tf_op jit(solution)/shard_map/direct_1/pallas_call | solution.py:93
  80.9 0.3 collective-permute-start.24
  81.2 0.3 core_0.1
  81.6 2.8 %collective-permute-start.10 = (s16[64,2176]{1,0:T(8,128)(2,1)S(1)}, s16[64,2176]{1,0:T(8,128)(2,1)S(1)}, u32[]{:S(2)}, u32[]{:S(2)}) collective-permute-start(s16[64,2176]{1,0:T(8,128)(2,1)S(1)} %get-tuple-element.102), channel_id=1, source_target_pairs={{0,2},{1,3},{2,0},{3,1},{4,6},{5,7},{6,4},{7,5},{8,10},{9,11},{10,... | collective-permute-start | bytes 835592 | tf_op jit(solution)/shard_map/chunk0_xh1/ppermute | solution.py:38
  84.4 0.9 join.1
  85.3 0.4 core_1.1
  85.7 1.3 %collective-permute-start.25 = (s16[64,2176]{1,0:T(8,128)(2,1)S(1)}, s16[64,2176]{1,0:T(8,128)(2,1)S(1)}, u32[]{:S(2)}, u32[]{:S(2)}) collective-permute-start(s16[64,2176]{1,0:T(8,128)(2,1)S(1)} %get-tuple-element.154), channel_id=1, source_target_pairs={{0,2},{1,3},{2,0},{3,1},{4,6},{5,7},{6,4},{7,5},{8,10},{9,11},{10,... | collective-permute-start | bytes 835592 | tf_op jit(solution)/shard_map/chunk1_xh1/ppermute | solution.py:38
  87.0 1.0 %collective-permute-start.26 = (s16[16,4224]{1,0:T(8,128)(2,1)S(1)}, s16[16,4224]{1,0:T(8,128)(2,1)S(1)}, u32[]{:S(2)}, u32[]{:S(2)}) collective-permute-start(s16[16,4224]{1,0:T(8,128)(2,1)S(1)} %get-tuple-element.156), channel_id=1, source_target_pairs={{0,8},{1,9},{2,10},{3,11},{4,12},{5,13},{6,14},{7,15},{8,0},{9,1},... | collective-permute-start | bytes 405512 | tf_op jit(solution)/shard_map/z_z1/ppermute | solution.py:38
  88.0 2.8 %collective-permute-start.27 = (s16[16,4224]{1,0:T(8,128)(2,1)S(1)}, s16[16,4224]{1,0:T(8,128)(2,1)S(1)}, u32[]{:S(2)}, u32[]{:S(2)}) collective-permute-start(s16[16,4224]{1,0:T(8,128)(2,1)S(1)} %get-tuple-element.157), channel_id=1, source_target_pairs={{0,16},{1,17},{2,18},{3,19},{4,20},{5,21},{6,22},{7,23},{8,24},{9,... | collective-permute-start | bytes 405512 | tf_op jit(solution)/shard_map/z_z2/ppermute | solution.py:38
  90.8 0.9 collective-permute-start.28
  91.7 0.9 collective-permute-done.10.r0
  92.6 5.6 %collective-permute-done.25.r1 = s16[64,2176]{1,0:T(8,128)(2,1)S(1)} collective-permute-done((s16[64,2176]{1,0:T(8,128)(2,1)S(1)}, s16[64,2176]{1,0:T(8,128)(2,1)S(1)}, u32[]{:S(2)}, u32[]{:S(2)}) %collective-permute-start.25) | collective-permute-done | bytes 278560 | tf_op jit(solution)/shard_map/chunk1_xh1/ppermute | solution.py:38
  98.2 1.6 %finish_first.1 = bf16[128,2048]{1,0:T(8,128)(2,1)} custom-call(s32[18]{0:T(128)S(1)} %pad_add_fusion.s_ref, f32[64,2048]{1,0:T(8,128)S(1)} %get-tuple-element.101.k0, s16[64,2176]{1,0:T(8,128)(2,1)S(1)} %collective-permute-done.10.r0, f32[64,2048]{1,0:T(8,128)S(1)} %get-tuple-element.153.k1, s16[64,2176]{1,0:T(8,128)(2,1)S(1)} %collective-permute-done.25.r1), custom_call_target="tpu_custom_call" | custom-call | bytes 5324980 | tf_op jit(solution)/shard_map/finish_first/pallas_call | solution.py:93
  99.7 0.8 finish_second.1
  (29 shorter events, 0.1 us)
Async XLA Ops:
  0.6 20.4 %collective-permute-start = (bf16[16,4096]{1,0:T(8,128)(2,1)}, bf16[16,4096]{1,0:T(8,128)(2,1)S(1)}, u32[]{:S(2)}, u32[]{:S(2)}) collective-permute-start(bf16[16,4096]{1,0:T(8,128)(2,1)} %param.5), channel_id=1, source_target_pairs={{0,32},{1,33},{2,34},{3,35},{4,36},{5,37},{6,38},{7,39},{8,40},{9,... | collective-permute-start | bytes 393224 | tf_op jit(solution)/shard_map/second_y1/ppermute | solution.py:38
  2.4 18.7 %collective-permute-start.1 = (bf16[16,4096]{1,0:T(8,128)(2,1)}, bf16[16,4096]{1,0:T(8,128)(2,1)S(1)}, u32[]{:S(2)}, u32[]{:S(2)}) collective-permute-start(bf16[16,4096]{1,0:T(8,128)(2,1)} %param.5), channel_id=1, source_target_pairs={{0,64},{1,65},{2,66},{3,67},{4,68},{5,69},{6,70},{7,71},{8,72},{9,... | collective-permute-start | bytes 393224 | tf_op jit(solution)/shard_map/second_y2/ppermute | solution.py:38
  5.3 15.8 %collective-permute-start.2 = (bf16[16,4096]{1,0:T(8,128)(2,1)}, bf16[16,4096]{1,0:T(8,128)(2,1)S(1)}, u32[]{:S(2)}, u32[]{:S(2)}) collective-permute-start(bf16[16,4096]{1,0:T(8,128)(2,1)} %param.5), channel_id=1, source_target_pairs={{0,96},{1,97},{2,98},{3,99},{4,100},{5,101},{6,102},{7,103},{8,104... | collective-permute-start | bytes 393224 | tf_op jit(solution)/shard_map/second_y3/ppermute | solution.py:38
  5.4 4.8 %collective-permute-start.3 = (bf16[128,2048]{1,0:T(8,128)(2,1)}, bf16[128,2048]{1,0:T(8,128)(2,1)S(1)}, u32[]{:S(2)}, u32[]{:S(2)}) collective-permute-start(bf16[128,2048]{1,0:T(8,128)(2,1)} %f0.3), channel_id=1, source_target_pairs={{0,1},{1,0},{2,3},{3,2},{4,5},{5,4},{6,7},{7,6},{8,9},{9,8},{10,11... | collective-permute-start | bytes 1572872 | tf_op jit(solution)/shard_map/first_core1/ppermute | solution.py:38
  5.4 16.1 %collective-permute-start.7 = (bf16[128,2048]{1,0:T(8,128)(2,1)}, bf16[128,2048]{1,0:T(8,128)(2,1)S(1)}, u32[]{:S(2)}, u32[]{:S(2)}) collective-permute-start(bf16[128,2048]{1,0:T(8,128)(2,1)} %f0.3), channel_id=1, source_target_pairs={{0,2},{1,3},{2,0},{3,1},{4,6},{5,7},{6,4},{7,5},{8,10},{9,11},{10,... | collective-permute-start | bytes 1572872 | tf_op jit(solution)/shard_map/first_xh1/ppermute | solution.py:38
  10.2 5.8 %copy-start = (bf16[2048,4096]{1,0:T(8,128)(2,1)S(1)}, bf16[2048,4096]{1,0:T(8,128)(2,1)}, u32[]{:S(2)}) copy-start(bf16[2048,4096]{1,0:T(8,128)(2,1)} %i_ref.11) | copy-start | bytes 50331652
  16.0 1.0 %copy-start.1 = (bf16[128,2048]{1,0:T(8,128)(2,1)S(1)}, bf16[128,2048]{1,0:T(8,128)(2,1)}, u32[]{:S(2)}) copy-start(bf16[128,2048]{1,0:T(8,128)(2,1)} %f0.3) | copy-start | bytes 1572868
  21.5 6.1 %collective-permute-start.8 = (bf16[128,2048]{1,0:T(8,128)(2,1)S(1)}, bf16[128,2048]{1,0:T(8,128)(2,1)S(1)}, u32[]{:S(2)}, u32[]{:S(2)}) collective-permute-start(bf16[128,2048]{1,0:T(8,128)(2,1)S(1)} %collective-permute-done.7.f2), channel_id=1, source_target_pairs={{0,1},{1,0},{2,3},{3,2},{4,5},{5,4},{6,7},{7,6},{8,9},{9,8},{10,11... | collective-permute-start | bytes 1572872 | tf_op jit(solution)/shard_map/first_core1/ppermute | solution.py:38
  21.5 14.1 %copy-start.2 = (bf16[128,2048]{1,0:T(8,128)(2,1)S(1)}, bf16[128,2048]{1,0:T(8,128)(2,1)}, u32[]{:S(2)}) copy-start(bf16[128,2048]{1,0:T(8,128)(2,1)} %f0.3) | copy-start | bytes 1572868
  21.5 18.3 %collective-permute-start.4 = (bf16[64,4096]{1,0:T(8,128)(2,1)S(1)}, bf16[64,4096]{1,0:T(8,128)(2,1)S(1)}, u32[]{:S(2)}, u32[]{:S(2)}) collective-permute-start(bf16[64,4096]{1,0:T(8,128)(2,1)S(1)} %constant_dynamic-update-slice_fusion.n0), channel_id=1, source_target_pairs={{0,4},{1,5},{2,6},{3,7},{4,0},{5,1},{6,2},{7,3},{8,12},{9,13},{10,... | collective-permute-start | bytes 1572872 | tf_op jit(solution)/shard_map/n_xl1/ppermute | solution.py:38
  23.2 16.6 %collective-permute-start.5 = (bf16[64,4096]{1,0:T(8,128)(2,1)S(1)}, bf16[64,4096]{1,0:T(8,128)(2,1)S(1)}, u32[]{:S(2)}, u32[]{:S(2)}) collective-permute-start(bf16[64,4096]{1,0:T(8,128)(2,1)S(1)} %constant_dynamic-update-slice_fusion.n0), channel_id=1, source_target_pairs={{0,8},{1,9},{2,10},{3,11},{4,12},{5,13},{6,14},{7,15},{8,0},{9,1},... | collective-permute-start | bytes 1572872 | tf_op jit(solution)/shard_map/n_z1/ppermute | solution.py:38
  25.1 15.0 %collective-permute-start.6 = (bf16[64,4096]{1,0:T(8,128)(2,1)S(1)}, bf16[64,4096]{1,0:T(8,128)(2,1)S(1)}, u32[]{:S(2)}, u32[]{:S(2)}) collective-permute-start(bf16[64,4096]{1,0:T(8,128)(2,1)S(1)} %constant_dynamic-update-slice_fusion.n0), channel_id=1, source_target_pairs={{0,24},{1,25},{2,26},{3,27},{4,28},{5,29},{6,30},{7,31},{8,16},{9,... | collective-permute-start | bytes 1572872 | tf_op jit(solution)/shard_map/n_z3/ppermute | solution.py:38
  32.5 21.9 %collective-permute-start.13 = (s16[256,1664]{1,0:T(8,128)(2,1)S(1)}, s16[256,1664]{1,0:T(8,128)(2,1)S(1)}, u32[]{:S(2)}, u32[]{:S(2)}) collective-permute-start(s16[256,1664]{1,0:T(8,128)(2,1)S(1)} %get-tuple-element.104), channel_id=1, source_target_pairs={{0,96},{1,97},{2,98},{3,99},{4,100},{5,101},{6,102},{7,103},{8,104... | collective-permute-start | bytes 2555912 | tf_op jit(solution)/shard_map/pa_y3/ppermute | solution.py:38
  35.6 20.2 %collective-permute-start.14 = (s16[256,1664]{1,0:T(8,128)(2,1)S(1)}, s16[256,1664]{1,0:T(8,128)(2,1)S(1)}, u32[]{:S(2)}, u32[]{:S(2)}) collective-permute-start(s16[256,1664]{1,0:T(8,128)(2,1)S(1)} %get-tuple-element.106), channel_id=1, source_target_pairs={{0,32},{1,33},{2,34},{3,35},{4,36},{5,37},{6,38},{7,39},{8,40},{9,... | collective-permute-start | bytes 2555912 | tf_op jit(solution)/shard_map/pb_y1/ppermute | solution.py:38
  35.6 25.2 %slice-start = ((s8[16777216]{0:T(1024)(128)(4,1)}), s8[4194304]{0:T(1024)(128)(4,1)S(1)}, s32[]{:S(2)}) async-start(s8[16777216]{0:T(1024)(128)(4,1)} %bitcast.3), calls=%async_computation | async-start | bytes 8388608
  35.6 25.2 %slice-start.1 = ((s8[16777216]{0:T(1024)(128)(4,1)}), s8[4194304]{0:T(1024)(128)(4,1)S(1)}, s32[]{:S(2)}) async-start(s8[16777216]{0:T(1024)(128)(4,1)} %bitcast.3), calls=%async_computation.1 | async-start | bytes 8388608
  37.5 23.3 %slice-start.2 = ((s8[16777216]{0:T(1024)(128)(4,1)}), s8[4194304]{0:T(1024)(128)(4,1)S(1)}, s32[]{:S(2)}) async-start(s8[16777216]{0:T(1024)(128)(4,1)} %bitcast.3), calls=%async_computation.2 | async-start | bytes 8388608
  37.5 23.3 %slice-start.3 = ((s8[16777216]{0:T(1024)(128)(4,1)}), s8[4194304]{0:T(1024)(128)(4,1)S(1)}, s32[]{:S(2)}) async-start(s8[16777216]{0:T(1024)(128)(4,1)} %bitcast.3), calls=%async_computation.3 | async-start | bytes 8388608
  40.1 18.6 %collective-permute-start.11 = (bf16[64,4096]{1,0:T(8,128)(2,1)S(1)}, bf16[64,4096]{1,0:T(8,128)(2,1)S(1)}, u32[]{:S(2)}, u32[]{:S(2)}) collective-permute-start(bf16[64,4096]{1,0:T(8,128)(2,1)S(1)} %collective-permute-done.4.n1), channel_id=1, source_target_pairs={{0,8},{1,9},{2,10},{3,11},{4,12},{5,13},{6,14},{7,15},{8,0},{9,1},... | collective-permute-start | bytes 1572872 | tf_op jit(solution)/shard_map/x_z1/ppermute | solution.py:38
  40.9 17.8 %collective-permute-start.12 = (bf16[64,4096]{1,0:T(8,128)(2,1)S(1)}, bf16[64,4096]{1,0:T(8,128)(2,1)S(1)}, u32[]{:S(2)}, u32[]{:S(2)}) collective-permute-start(bf16[64,4096]{1,0:T(8,128)(2,1)S(1)} %collective-permute-done.4.n1), channel_id=1, source_target_pairs={{0,24},{1,25},{2,26},{3,27},{4,28},{5,29},{6,30},{7,31},{8,16},{9,... | collective-permute-start | bytes 1572872 | tf_op jit(solution)/shard_map/x_z3/ppermute | solution.py:38
  43.0 23.1 %collective-permute-start.17 = (s16[256,1152]{1,0:T(8,128)(2,1)S(1)}, s16[256,1152]{1,0:T(8,128)(2,1)S(1)}, u32[]{:S(2)}, u32[]{:S(2)}) collective-permute-start(s16[256,1152]{1,0:T(8,128)(2,1)S(1)} %get-tuple-element.120), channel_id=1, source_target_pairs={{0,4},{1,5},{2,6},{3,7},{4,0},{5,1},{6,2},{7,3},{8,12},{9,13},{10,... | collective-permute-start | bytes 1769480 | tf_op jit(solution)/shard_map/q_xl1/ppermute | solution.py:38
  56.5 11.5 %collective-permute-start.16 = (s16[128,1664]{1,0:T(8,128)(2,1)S(1)}, s16[128,1664]{1,0:T(8,128)(2,1)S(1)}, u32[]{:S(2)}, u32[]{:S(2)}) collective-permute-start(s16[128,1664]{1,0:T(8,128)(2,1)S(1)} %get-tuple-element.116), channel_id=1, source_target_pairs={{0,96},{1,97},{2,98},{3,99},{4,100},{5,101},{6,102},{7,103},{8,104... | collective-permute-start | bytes 1277960 | tf_op jit(solution)/shard_map/pb_y3/ppermute | solution.py:38
  58.7 10.3 %collective-permute-start.15 = (s16[128,1664]{1,0:T(8,128)(2,1)S(1)}, s16[128,1664]{1,0:T(8,128)(2,1)S(1)}, u32[]{:S(2)}, u32[]{:S(2)}) collective-permute-start(s16[128,1664]{1,0:T(8,128)(2,1)S(1)} %get-tuple-element.114), channel_id=1, source_target_pairs={{0,32},{1,33},{2,34},{3,35},{4,36},{5,37},{6,38},{7,39},{8,40},{9,... | collective-permute-start | bytes 1277960 | tf_op jit(solution)/shard_map/pa_y1/ppermute | solution.py:38
  58.8 12.4 %collective-permute-start.19 = (bf16[64,4096]{1,0:T(8,128)(2,1)S(1)}, bf16[64,4096]{1,0:T(8,128)(2,1)S(1)}, u32[]{:S(2)}, u32[]{:S(2)}) collective-permute-start(bf16[64,4096]{1,0:T(8,128)(2,1)S(1)} %collective-permute-done.6.n3), channel_id=1, source_target_pairs={{0,8},{1,9},{2,10},{3,11},{4,12},{5,13},{6,14},{7,15},{8,0},{9,1},... | collective-permute-start | bytes 1572872 | tf_op jit(solution)/shard_map/n3_z1/ppermute | solution.py:38
  59.9 13.8 %collective-permute-start.20 = (bf16[64,4096]{1,0:T(8,128)(2,1)S(1)}, bf16[64,4096]{1,0:T(8,128)(2,1)S(1)}, u32[]{:S(2)}, u32[]{:S(2)}) collective-permute-start(bf16[64,4096]{1,0:T(8,128)(2,1)S(1)} %collective-permute-done.11.n0), channel_id=1, source_target_pairs={{0,24},{1,25},{2,26},{3,27},{4,28},{5,29},{6,30},{7,31},{8,16},{9,... | collective-permute-start | bytes 1572872 | tf_op jit(solution)/shard_map/x1_z3/ppermute | solution.py:38
  66.1 15.1 %collective-permute-start.9 = (f32[128,2048]{1,0:T(8,128)S(1)}, f32[128,2048]{1,0:T(8,128)S(1)}, u32[]{:S(2)}, u32[]{:S(2)}) collective-permute-start(f32[128,2048]{1,0:T(8,128)S(1)} %get-tuple-element.100), channel_id=1, source_target_pairs={{0,1},{1,0},{2,3},{3,2},{4,5},{5,4},{6,7},{7,6},{8,9},{9,8},{10,11... | collective-permute-start | bytes 3145736 | tf_op jit(solution)/shard_map/chunk0_core1/ppermute | solution.py:38
  69.8 11.1 %collective-permute-start.18 = (s16[64,3200]{1,0:T(8,128)(2,1)S(1)}, s16[64,3200]{1,0:T(8,128)(2,1)S(1)}, u32[]{:S(2)}, u32[]{:S(2)}) collective-permute-start(s16[64,3200]{1,0:T(8,128)(2,1)S(1)} %get-tuple-element.125), channel_id=1, source_target_pairs={{0,4},{1,5},{2,6},{3,7},{4,0},{5,1},{6,2},{7,3},{8,12},{9,13},{10,... | collective-permute-start | bytes 1228808 | tf_op jit(solution)/shard_map/p_xl1/ppermute | solution.py:38
  70.4 10.4 %collective-permute-start.21 = (s16[64,1152]{1,0:T(8,128)(2,1)S(1)}, s16[64,1152]{1,0:T(8,128)(2,1)S(1)}, u32[]{:S(2)}, u32[]{:S(2)}) collective-permute-start(s16[64,1152]{1,0:T(8,128)(2,1)S(1)} %get-tuple-element.136), channel_id=1, source_target_pairs={{0,32},{1,33},{2,34},{3,35},{4,36},{5,37},{6,38},{7,39},{8,40},{9,... | collective-permute-start | bytes 442376 | tf_op jit(solution)/shard_map/q_y1/ppermute | solution.py:38
  71.2 9.7 %collective-permute-start.22 = (s16[64,1152]{1,0:T(8,128)(2,1)S(1)}, s16[64,1152]{1,0:T(8,128)(2,1)S(1)}, u32[]{:S(2)}, u32[]{:S(2)}) collective-permute-start(s16[64,1152]{1,0:T(8,128)(2,1)S(1)} %get-tuple-element.137), channel_id=1, source_target_pairs={{0,64},{1,65},{2,66},{3,67},{4,68},{5,69},{6,70},{7,71},{8,72},{9,... | collective-permute-start | bytes 442376 | tf_op jit(solution)/shard_map/q_y2/ppermute | solution.py:38
  73.7 7.1 %collective-permute-start.23 = (s16[64,1152]{1,0:T(8,128)(2,1)S(1)}, s16[64,1152]{1,0:T(8,128)(2,1)S(1)}, u32[]{:S(2)}, u32[]{:S(2)}) collective-permute-start(s16[64,1152]{1,0:T(8,128)(2,1)S(1)} %get-tuple-element.138), channel_id=1, source_target_pairs={{0,96},{1,97},{2,98},{3,99},{4,100},{5,101},{6,102},{7,103},{8,104... | collective-permute-start | bytes 442376 | tf_op jit(solution)/shard_map/q_y3/ppermute | solution.py:38
  80.9 4.4 %collective-permute-start.24 = (f32[128,2048]{1,0:T(8,128)S(1)}, f32[128,2048]{1,0:T(8,128)S(1)}, u32[]{:S(2)}, u32[]{:S(2)}) collective-permute-start(f32[128,2048]{1,0:T(8,128)S(1)} %get-tuple-element.140), channel_id=1, source_target_pairs={{0,1},{1,0},{2,3},{3,2},{4,5},{5,4},{6,7},{7,6},{8,9},{9,8},{10,11... | collective-permute-start | bytes 3145736 | tf_op jit(solution)/shard_map/chunk1_core1/ppermute | solution.py:38
  81.6 11.0 %collective-permute-start.10 = (s16[64,2176]{1,0:T(8,128)(2,1)S(1)}, s16[64,2176]{1,0:T(8,128)(2,1)S(1)}, u32[]{:S(2)}, u32[]{:S(2)}) collective-permute-start(s16[64,2176]{1,0:T(8,128)(2,1)S(1)} %get-tuple-element.102), channel_id=1, source_target_pairs={{0,2},{1,3},{2,0},{3,1},{4,6},{5,7},{6,4},{7,5},{8,10},{9,11},{10,... | collective-permute-start | bytes 835592 | tf_op jit(solution)/shard_map/chunk0_xh1/ppermute | solution.py:38
  85.7 12.5 %collective-permute-start.25 = (s16[64,2176]{1,0:T(8,128)(2,1)S(1)}, s16[64,2176]{1,0:T(8,128)(2,1)S(1)}, u32[]{:S(2)}, u32[]{:S(2)}) collective-permute-start(s16[64,2176]{1,0:T(8,128)(2,1)S(1)} %get-tuple-element.154), channel_id=1, source_target_pairs={{0,2},{1,3},{2,0},{3,1},{4,6},{5,7},{6,4},{7,5},{8,10},{9,11},{10,... | collective-permute-start | bytes 835592 | tf_op jit(solution)/shard_map/chunk1_xh1/ppermute | solution.py:38
  87.0 12.7 %collective-permute-start.26 = (s16[16,4224]{1,0:T(8,128)(2,1)S(1)}, s16[16,4224]{1,0:T(8,128)(2,1)S(1)}, u32[]{:S(2)}, u32[]{:S(2)}) collective-permute-start(s16[16,4224]{1,0:T(8,128)(2,1)S(1)} %get-tuple-element.156), channel_id=1, source_target_pairs={{0,8},{1,9},{2,10},{3,11},{4,12},{5,13},{6,14},{7,15},{8,0},{9,1},... | collective-permute-start | bytes 405512 | tf_op jit(solution)/shard_map/z_z1/ppermute | solution.py:38
  88.0 11.7 %collective-permute-start.27 = (s16[16,4224]{1,0:T(8,128)(2,1)S(1)}, s16[16,4224]{1,0:T(8,128)(2,1)S(1)}, u32[]{:S(2)}, u32[]{:S(2)}) collective-permute-start(s16[16,4224]{1,0:T(8,128)(2,1)S(1)} %get-tuple-element.157), channel_id=1, source_target_pairs={{0,16},{1,17},{2,18},{3,19},{4,20},{5,21},{6,22},{7,23},{8,24},{9,... | collective-permute-start | bytes 405512 | tf_op jit(solution)/shard_map/z_z2/ppermute | solution.py:38
  90.8 8.9 %collective-permute-start.28 = (s16[16,4224]{1,0:T(8,128)(2,1)S(1)}, s16[16,4224]{1,0:T(8,128)(2,1)S(1)}, u32[]{:S(2)}, u32[]{:S(2)}) collective-permute-start(s16[16,4224]{1,0:T(8,128)(2,1)S(1)} %get-tuple-element.158), channel_id=1, source_target_pairs={{0,24},{1,25},{2,26},{3,27},{4,28},{5,29},{6,30},{7,31},{8,16},{9,... | collective-permute-start | bytes 405512 | tf_op jit(solution)/shard_map/z_z3/ppermute | solution.py:38

commit v5 on v4

--- a/solution.py
+++ b/solution.py
@@ -11,7 +11,7 @@
 F32, BF16, I16 = jnp.float32, jnp.bfloat16, jnp.int16
 TILE = 256
 OCC, NA_D, NB_D, CT = 512, 2048, 4096, 16
-TN = 512
+TN = 1024
 CN = 512
 P_WIDE = 3072
 P_HALF = P_WIDE // 2

time: 101 us -> 102 us (level)
  no operation moved by 1% of the time
where the time goes in v5:
time: 102 us; the launch traced here: 101 us
  starting transfers between devices  38.6 us (38%)
  Pallas kernels  30.4 us (30%)
  waiting for transfers between devices  22.2 us (22%)
  local copies, waits for them, and re-layouts  7.78 us (8%)
    ppermute x29, starting transfers between devices, swap(): return lax.ppermute(value, ('row', 'col'), exchange_pairs(**flips))  38.6 us
    pallas_call x15, Pallas kernels, call(): pl.pallas_call(kernel, in_specs=[pl.BlockSpec(memory_space=pltpu.SMEM)] *...  30.4 us
    ppermute x29, waiting for transfers between devices, swap(): return lax.ppermute(value, ('row', 'col'), exchange_pairs(**flips))  22.2 us
    unnamed x17, local copies, waits for them, and re-layouts  7.77 us
  transfers between devices with their start and end apart: 29, of which 9 were waited for; matrix products, arithmetic and copies ran while one was open for 2% of the time, Pallas kernels for 29%

profile of v5, /device:TPU:0, one launch (start us, length us, event | category | flops | bytes accessed | tf_op | source)
XLA Modules:
  0.0 100.7 jit_solution(339892947917097928)
XLA Ops:
  0.6 1.7 %collective-permute-start = (bf16[16,4096]{1,0:T(8,128)(2,1)}, bf16[16,4096]{1,0:T(8,128)(2,1)S(1)}, u32[]{:S(2)}, u32[]{:S(2)}) collective-permute-start(bf16[16,4096]{1,0:T(8,128)(2,1)} %param.5), channel_id=1, source_target_pairs={{0,32},{1,33},{2,34},{3,35},{4,36},{5,37},{6,38},{7,39},{8,40},{9,... | collective-permute-start | bytes 393224 | tf_op jit(solution)/shard_map/second_y1/ppermute | solution.py:38
  2.4 2.9 %collective-permute-start.1 = (bf16[16,4096]{1,0:T(8,128)(2,1)}, bf16[16,4096]{1,0:T(8,128)(2,1)S(1)}, u32[]{:S(2)}, u32[]{:S(2)}) collective-permute-start(bf16[16,4096]{1,0:T(8,128)(2,1)} %param.5), channel_id=1, source_target_pairs={{0,64},{1,65},{2,66},{3,67},{4,68},{5,69},{6,70},{7,71},{8,72},{9,... | collective-permute-start | bytes 393224 | tf_op jit(solution)/shard_map/second_y2/ppermute | solution.py:38
  5.3 0.1 collective-permute-start.2
  5.4 3.1 %collective-permute-start.7 = (bf16[128,2048]{1,0:T(8,128)(2,1)}, bf16[128,2048]{1,0:T(8,128)(2,1)S(1)}, u32[]{:S(2)}, u32[]{:S(2)}) collective-permute-start(bf16[128,2048]{1,0:T(8,128)(2,1)} %f0.3), channel_id=1, source_target_pairs={{0,2},{1,3},{2,0},{3,1},{4,6},{5,7},{6,4},{7,5},{8,10},{9,11},{10,... | collective-permute-start | bytes 1572872 | tf_op jit(solution)/shard_map/first_xh1/ppermute | solution.py:38
  8.5 0.7 pad_add_fusion.s_ref
  9.2 0.9 constant_dynamic-update-slice_fusion.3
  10.2 0.0 copy-start
  10.2 5.8 %copy-done = bf16[2048,4096]{1,0:T(8,128)(2,1)S(1)} copy-done((bf16[2048,4096]{1,0:T(8,128)(2,1)S(1)}, bf16[2048,4096]{1,0:T(8,128)(2,1)}, u32[]{:S(2)}) %copy-start) | copy-done | bytes 16777240
  16.0 1.0 %copy-done.1 = bf16[128,2048]{1,0:T(8,128)(2,1)S(1)} copy-done((bf16[128,2048]{1,0:T(8,128)(2,1)S(1)}, bf16[128,2048]{1,0:T(8,128)(2,1)}, u32[]{:S(2)}) %copy-start.1) | copy-done | bytes 524312
  17.0 4.1 %early_p.1.early_ref = f32[256,3072]{1,0:T(8,128)S(1)} custom-call(s32[18]{0:T(128)S(1)} %pad_add_fusion.s_ref, bf16[128,2048]{1,0:T(8,128)(2,1)S(1)} %copy-done.1, bf16[128,2048]{1,0:T(8,128)(2,1)S(1)} %collective-permute-done.3.f1, bf16[2048,4096]{1,0:T(8,128)(2,1)S(1)} %copy-done), custom_call_target="tpu_custom_call" | custom-call | flops 8053063680 | bytes 52428980 | tf_op jit(solution)/shard_map/early_p/pallas_call | solution.py:93
  21.1 0.0 collective-permute-done
  21.1 0.0 collective-permute-done.1
  21.1 0.4 collective-permute-done.7.f2
  21.5 0.0 copy-start.2
  21.5 1.7 %collective-permute-start.4 = (bf16[64,4096]{1,0:T(8,128)(2,1)S(1)}, bf16[64,4096]{1,0:T(8,128)(2,1)S(1)}, u32[]{:S(2)}, u32[]{:S(2)}) collective-permute-start(bf16[64,4096]{1,0:T(8,128)(2,1)S(1)} %constant_dynamic-update-slice_fusion.n0), channel_id=1, source_target_pairs={{0,4},{1,5},{2,6},{3,7},{4,0},{5,1},{6,2},{7,3},{8,12},{9,13},{10,... | collective-permute-start | bytes 1572872 | tf_op jit(solution)/shard_map/n_xl1/ppermute | solution.py:38
  23.2 1.9 %collective-permute-start.5 = (bf16[64,4096]{1,0:T(8,128)(2,1)S(1)}, bf16[64,4096]{1,0:T(8,128)(2,1)S(1)}, u32[]{:S(2)}, u32[]{:S(2)}) collective-permute-start(bf16[64,4096]{1,0:T(8,128)(2,1)S(1)} %constant_dynamic-update-slice_fusion.n0), channel_id=1, source_target_pairs={{0,8},{1,9},{2,10},{3,11},{4,12},{5,13},{6,14},{7,15},{8,0},{9,1},... | collective-permute-start | bytes 1572872 | tf_op jit(solution)/shard_map/n_z1/ppermute | solution.py:38
  25.1 2.5 %collective-permute-start.6 = (bf16[64,4096]{1,0:T(8,128)(2,1)S(1)}, bf16[64,4096]{1,0:T(8,128)(2,1)S(1)}, u32[]{:S(2)}, u32[]{:S(2)}) collective-permute-start(bf16[64,4096]{1,0:T(8,128)(2,1)S(1)} %constant_dynamic-update-slice_fusion.n0), channel_id=1, source_target_pairs={{0,24},{1,25},{2,26},{3,27},{4,28},{5,29},{6,30},{7,31},{8,16},{9,... | collective-permute-start | bytes 1572872 | tf_op jit(solution)/shard_map/n_z3/ppermute | solution.py:38
  27.6 5.0 %mirror_p.1 = (f32[256,1536]{1,0:T(8,128)S(1)}, s16[256,1664]{1,0:T(8,128)(2,1)S(1)}, f32[256,1536]{1,0:T(8,128)S(1)}, s16[256,1664]{1,0:T(8,128)(2,1)S(1)}) custom-call(s32[18]{0:T(128)S(1)} %pad_add_fusion.s_ref, bf16[128,2048]{1,0:T(8,128)(2,1)S(1)} %collective-permute-done.7.f2, bf16[128,2048]{1,0:T(8,128)(2,1)S(1)} %collective-permute-done.8.f3, ...), custom_call_target="tpu_custom_call" | custom-call | flops 8053063680 | bytes 64553140 | tf_op jit(solution)/shard_map/mirror_p/pallas_call | solution.py:93
  32.6 3.1 %collective-permute-start.13 = (s16[256,1664]{1,0:T(8,128)(2,1)S(1)}, s16[256,1664]{1,0:T(8,128)(2,1)S(1)}, u32[]{:S(2)}, u32[]{:S(2)}) collective-permute-start(s16[256,1664]{1,0:T(8,128)(2,1)S(1)} %get-tuple-element.104), channel_id=1, source_target_pairs={{0,96},{1,97},{2,98},{3,99},{4,100},{5,101},{6,102},{7,103},{8,104... | collective-permute-start | bytes 2555912 | tf_op jit(solution)/shard_map/pa_y3/ppermute | solution.py:38
  35.7 0.0 collective-permute-start.14
  35.7 1.9 %early_q.1.early_ref = f32[256,1024]{1,0:T(8,128)S(1)} custom-call(s32[18]{0:T(128)S(1)} %pad_add_fusion.s_ref, bf16[128,2048]{1,0:T(8,128)(2,1)S(1)} %copy-done.2, bf16[128,2048]{1,0:T(8,128)(2,1)S(1)} %collective-permute-done.3.f1, bf16[2048,4096]{1,0:T(8,128)(2,1)S(1)} %copy-done), custom_call_target="tpu_custom_call" | custom-call | flops 2684354560 | bytes 47186100 | tf_op jit(solution)/shard_map/early_q/pallas_call | solution.py:93
  37.6 0.0 slice-start.2
  37.6 2.3 %mirror_q.1 = (f32[256,1024]{1,0:T(8,128)S(1)}, s16[256,1152]{1,0:T(8,128)(2,1)S(1)}) custom-call(s32[18]{0:T(128)S(1)} %pad_add_fusion.s_ref, bf16[128,2048]{1,0:T(8,128)(2,1)S(1)} %collective-permute-done.7.f2, bf16[128,2048]{1,0:T(8,128)(2,1)S(1)} %collective-permute-done.8.f3, f32[256,1024]{1,0:T(8,128)S(1)} %early_q.1.early_ref, ...), custom_call_target="tpu_custom_call" | custom-call | flops 2684354560 | bytes 51282100 | tf_op jit(solution)/shard_map/mirror_q/pallas_call | solution.py:93
  39.9 0.0 collective-permute-done.4.n1
  39.9 0.1 collective-permute-done.6.n3
  40.1 1.0 collective-permute-start.11
  41.0 2.0 %collective-permute-start.12 = (bf16[64,4096]{1,0:T(8,128)(2,1)S(1)}, bf16[64,4096]{1,0:T(8,128)(2,1)S(1)}, u32[]{:S(2)}, u32[]{:S(2)}) collective-permute-start(bf16[64,4096]{1,0:T(8,128)(2,1)S(1)} %collective-permute-done.4.n1), channel_id=1, source_target_pairs={{0,24},{1,25},{2,26},{3,27},{4,28},{5,29},{6,30},{7,31},{8,16},{9,... | collective-permute-start | bytes 1572872 | tf_op jit(solution)/shard_map/x_z3/ppermute | solution.py:38
  43.0 0.5 collective-permute-start.17
  43.5 11.0 %collective-permute-done.13.other = s16[256,1664]{1,0:T(8,128)(2,1)S(1)} collective-permute-done((s16[256,1664]{1,0:T(8,128)(2,1)S(1)}, s16[256,1664]{1,0:T(8,128)(2,1)S(1)}, u32[]{:S(2)}, u32[]{:S(2)}) %collective-permute-start.13) | collective-permute-done | bytes 852000 | tf_op jit(solution)/shard_map/pa_y3/ppermute | solution.py:38
  54.5 1.5 %collective-permute-done.14.other = s16[256,1664]{1,0:T(8,128)(2,1)S(1)} collective-permute-done((s16[256,1664]{1,0:T(8,128)(2,1)S(1)}, s16[256,1664]{1,0:T(8,128)(2,1)S(1)}, u32[]{:S(2)}, u32[]{:S(2)}) %collective-permute-start.14) | collective-permute-done | bytes 852000 | tf_op jit(solution)/shard_map/pb_y1/ppermute | solution.py:38
  56.0 0.6 fold_pb.1
  56.6 1.6 %collective-permute-start.16 = (s16[128,1664]{1,0:T(8,128)(2,1)S(1)}, s16[128,1664]{1,0:T(8,128)(2,1)S(1)}, u32[]{:S(2)}, u32[]{:S(2)}) collective-permute-start(s16[128,1664]{1,0:T(8,128)(2,1)S(1)} %get-tuple-element.116), channel_id=1, source_target_pairs={{0,96},{1,97},{2,98},{3,99},{4,100},{5,101},{6,102},{7,103},{8,104... | collective-permute-start | bytes 1277960 | tf_op jit(solution)/shard_map/pb_y3/ppermute | solution.py:38
  58.2 0.6 fold_pa.1
  58.8 0.0 collective-permute-done.11.n0
  58.8 0.1 collective-permute-start.15
  58.9 1.1 %collective-permute-start.19 = (bf16[64,4096]{1,0:T(8,128)(2,1)S(1)}, bf16[64,4096]{1,0:T(8,128)(2,1)S(1)}, u32[]{:S(2)}, u32[]{:S(2)}) collective-permute-start(bf16[64,4096]{1,0:T(8,128)(2,1)S(1)} %collective-permute-done.6.n3), channel_id=1, source_target_pairs={{0,8},{1,9},{2,10},{3,11},{4,12},{5,13},{6,14},{7,15},{8,0},{9,1},... | collective-permute-start | bytes 1572872 | tf_op jit(solution)/shard_map/n3_z1/ppermute | solution.py:38
  60.0 0.9 collective-permute-start.20
  60.9 5.3 %direct_0.1 = (f32[128,2048]{1,0:T(8,128)S(1)}, f32[128,2048]{1,0:T(8,128)S(1)}) custom-call(s32[18]{0:T(128)S(1)} %pad_add_fusion.s_ref, bf16[64,4096]{1,0:T(8,128)(2,1)S(1)} %constant_dynamic-update-slice_fusion.n0, bf16[64,4096]{1,0:T(8,128)(2,1)S(1)} %collective-permute-done.4.n1, bf16[64,4096]{1,0:T(8,128)(2,1)S(1)} %collective-permute-done.5.n2, ...), custom_call_target="tpu_custom_call" | custom-call | flops 10737418240 | bytes 52428980 | tf_op jit(solution)/shard_map/direct_0/pallas_call | solution.py:93
  66.3 0.1 collective-permute-start.9
  66.3 0.5 fold_q_xl.1
  66.8 1.2 %collective-permute-done.16.b1 = s16[128,1664]{1,0:T(8,128)(2,1)S(1)} collective-permute-done((s16[128,1664]{1,0:T(8,128)(2,1)S(1)}, s16[128,1664]{1,0:T(8,128)(2,1)S(1)}, u32[]{:S(2)}, u32[]{:S(2)}) %collective-permute-start.16) | collective-permute-done | bytes 426016 | tf_op jit(solution)/shard_map/pb_y3/ppermute | solution.py:38
  68.1 1.0 %collective-permute-done.15.a1 = s16[128,1664]{1,0:T(8,128)(2,1)S(1)} collective-permute-done((s16[128,1664]{1,0:T(8,128)(2,1)S(1)}, s16[128,1664]{1,0:T(8,128)(2,1)S(1)}, u32[]{:S(2)}, u32[]{:S(2)}) %collective-permute-start.15) | collective-permute-done | bytes 426016 | tf_op jit(solution)/shard_map/pa_y1/ppermute | solution.py:38
  69.1 0.8 merge.1
  69.9 0.6 collective-permute-start.18
  70.5 0.3 collective-permute-start.21
  70.8 0.5 collective-permute-done.19.n2
  71.3 2.5 %collective-permute-start.22 = (s16[64,1152]{1,0:T(8,128)(2,1)S(1)}, s16[64,1152]{1,0:T(8,128)(2,1)S(1)}, u32[]{:S(2)}, u32[]{:S(2)}) collective-permute-start(s16[64,1152]{1,0:T(8,128)(2,1)S(1)} %get-tuple-element.137), channel_id=1, source_target_pairs={{0,64},{1,65},{2,66},{3,67},{4,68},{5,69},{6,70},{7,71},{8,72},{9,... | collective-permute-start | bytes 442376 | tf_op jit(solution)/shard_map/q_y2/ppermute | solution.py:38
  73.8 0.0 collective-permute-done.20.n3
  73.8 1.8 %collective-permute-start.23 = (s16[64,1152]{1,0:T(8,128)(2,1)S(1)}, s16[64,1152]{1,0:T(8,128)(2,1)S(1)}, u32[]{:S(2)}, u32[]{:S(2)}) collective-permute-start(s16[64,1152]{1,0:T(8,128)(2,1)S(1)} %get-tuple-element.138), channel_id=1, source_target_pairs={{0,96},{1,97},{2,98},{3,99},{4,100},{5,101},{6,102},{7,103},{8,104... | collective-permute-start | bytes 442376 | tf_op jit(solution)/shard_map/q_y3/ppermute | solution.py:38
  75.6 5.3 %direct_1.1 = (f32[128,2048]{1,0:T(8,128)S(1)}, f32[128,2048]{1,0:T(8,128)S(1)}) custom-call(s32[18]{0:T(128)S(1)} %pad_add_fusion.s_ref, bf16[64,4096]{1,0:T(8,128)(2,1)S(1)} %collective-permute-done.11.n0, bf16[64,4096]{1,0:T(8,128)(2,1)S(1)} %collective-permute-done.12.n1, bf16[64,4096]{1,0:T(8,128)(2,1)S(1)} %collective-permute-done.19.n2, ...), custom_call_target="tpu_custom_call" | custom-call | flops 10737418240 | bytes 52428980 | tf_op jit(solution)/shard_map/direct_1/pallas_call | solution.py:93
  81.0 0.0 collective-permute-done.22.q2
  81.0 0.3 collective-permute-start.24
  81.3 0.3 core_0.1
  81.7 2.8 %collective-permute-start.10 = (s16[64,2176]{1,0:T(8,128)(2,1)S(1)}, s16[64,2176]{1,0:T(8,128)(2,1)S(1)}, u32[]{:S(2)}, u32[]{:S(2)}) collective-permute-start(s16[64,2176]{1,0:T(8,128)(2,1)S(1)} %get-tuple-element.102), channel_id=1, source_target_pairs={{0,2},{1,3},{2,0},{3,1},{4,6},{5,7},{6,4},{7,5},{8,10},{9,11},{10,... | collective-permute-start | bytes 835592 | tf_op jit(solution)/shard_map/chunk0_xh1/ppermute | solution.py:38
  84.5 0.9 join.1
  85.4 0.4 core_1.1
  85.8 1.3 %collective-permute-start.25 = (s16[64,2176]{1,0:T(8,128)(2,1)S(1)}, s16[64,2176]{1,0:T(8,128)(2,1)S(1)}, u32[]{:S(2)}, u32[]{:S(2)}) collective-permute-start(s16[64,2176]{1,0:T(8,128)(2,1)S(1)} %get-tuple-element.154), channel_id=1, source_target_pairs={{0,2},{1,3},{2,0},{3,1},{4,6},{5,7},{6,4},{7,5},{8,10},{9,11},{10,... | collective-permute-start | bytes 835592 | tf_op jit(solution)/shard_map/chunk1_xh1/ppermute | solution.py:38
  87.1 1.0 %collective-permute-start.26 = (s16[16,4224]{1,0:T(8,128)(2,1)S(1)}, s16[16,4224]{1,0:T(8,128)(2,1)S(1)}, u32[]{:S(2)}, u32[]{:S(2)}) collective-permute-start(s16[16,4224]{1,0:T(8,128)(2,1)S(1)} %get-tuple-element.156), channel_id=1, source_target_pairs={{0,8},{1,9},{2,10},{3,11},{4,12},{5,13},{6,14},{7,15},{8,0},{9,1},... | collective-permute-start | bytes 405512 | tf_op jit(solution)/shard_map/z_z1/ppermute | solution.py:38
  88.2 2.8 %collective-permute-start.27 = (s16[16,4224]{1,0:T(8,128)(2,1)S(1)}, s16[16,4224]{1,0:T(8,128)(2,1)S(1)}, u32[]{:S(2)}, u32[]{:S(2)}) collective-permute-start(s16[16,4224]{1,0:T(8,128)(2,1)S(1)} %get-tuple-element.157), channel_id=1, source_target_pairs={{0,16},{1,17},{2,18},{3,19},{4,20},{5,21},{6,22},{7,23},{8,24},{9,... | collective-permute-start | bytes 405512 | tf_op jit(solution)/shard_map/z_z2/ppermute | solution.py:38
  91.0 0.9 collective-permute-start.28
  91.8 0.9 collective-permute-done.10.r0
  92.7 5.6 %collective-permute-done.25.r1 = s16[64,2176]{1,0:T(8,128)(2,1)S(1)} collective-permute-done((s16[64,2176]{1,0:T(8,128)(2,1)S(1)}, s16[64,2176]{1,0:T(8,128)(2,1)S(1)}, u32[]{:S(2)}, u32[]{:S(2)}) %collective-permute-start.25) | collective-permute-done | bytes 278560 | tf_op jit(solution)/shard_map/chunk1_xh1/ppermute | solution.py:38
  98.3 1.6 %finish_first.1 = bf16[128,2048]{1,0:T(8,128)(2,1)} custom-call(s32[18]{0:T(128)S(1)} %pad_add_fusion.s_ref, f32[64,2048]{1,0:T(8,128)S(1)} %get-tuple-element.101.k0, s16[64,2176]{1,0:T(8,128)(2,1)S(1)} %collective-permute-done.10.r0, f32[64,2048]{1,0:T(8,128)S(1)} %get-tuple-element.153.k1, s16[64,2176]{1,0:T(8,128)(2,1)S(1)} %collective-permute-done.25.r1), custom_call_target="tpu_custom_call" | custom-call | bytes 5324980 | tf_op jit(solution)/shard_map/finish_first/pallas_call | solution.py:93
  99.9 0.8 finish_second.1
  (29 shorter events, 0.1 us)
Async XLA Ops:
  0.6 20.4 %collective-permute-start = (bf16[16,4096]{1,0:T(8,128)(2,1)}, bf16[16,4096]{1,0:T(8,128)(2,1)S(1)}, u32[]{:S(2)}, u32[]{:S(2)}) collective-permute-start(bf16[16,4096]{1,0:T(8,128)(2,1)} %param.5), channel_id=1, source_target_pairs={{0,32},{1,33},{2,34},{3,35},{4,36},{5,37},{6,38},{7,39},{8,40},{9,... | collective-permute-start | bytes 393224 | tf_op jit(solution)/shard_map/second_y1/ppermute | solution.py:38
  2.4 18.7 %collective-permute-start.1 = (bf16[16,4096]{1,0:T(8,128)(2,1)}, bf16[16,4096]{1,0:T(8,128)(2,1)S(1)}, u32[]{:S(2)}, u32[]{:S(2)}) collective-permute-start(bf16[16,4096]{1,0:T(8,128)(2,1)} %param.5), channel_id=1, source_target_pairs={{0,64},{1,65},{2,66},{3,67},{4,68},{5,69},{6,70},{7,71},{8,72},{9,... | collective-permute-start | bytes 393224 | tf_op jit(solution)/shard_map/second_y2/ppermute | solution.py:38
  5.3 15.8 %collective-permute-start.2 = (bf16[16,4096]{1,0:T(8,128)(2,1)}, bf16[16,4096]{1,0:T(8,128)(2,1)S(1)}, u32[]{:S(2)}, u32[]{:S(2)}) collective-permute-start(bf16[16,4096]{1,0:T(8,128)(2,1)} %param.5), channel_id=1, source_target_pairs={{0,96},{1,97},{2,98},{3,99},{4,100},{5,101},{6,102},{7,103},{8,104... | collective-permute-start | bytes 393224 | tf_op jit(solution)/shard_map/second_y3/ppermute | solution.py:38
  5.4 4.8 %collective-permute-start.3 = (bf16[128,2048]{1,0:T(8,128)(2,1)}, bf16[128,2048]{1,0:T(8,128)(2,1)S(1)}, u32[]{:S(2)}, u32[]{:S(2)}) collective-permute-start(bf16[128,2048]{1,0:T(8,128)(2,1)} %f0.3), channel_id=1, source_target_pairs={{0,1},{1,0},{2,3},{3,2},{4,5},{5,4},{6,7},{7,6},{8,9},{9,8},{10,11... | collective-permute-start | bytes 1572872 | tf_op jit(solution)/shard_map/first_core1/ppermute | solution.py:38
  5.4 16.1 %collective-permute-start.7 = (bf16[128,2048]{1,0:T(8,128)(2,1)}, bf16[128,2048]{1,0:T(8,128)(2,1)S(1)}, u32[]{:S(2)}, u32[]{:S(2)}) collective-permute-start(bf16[128,2048]{1,0:T(8,128)(2,1)} %f0.3), channel_id=1, source_target_pairs={{0,2},{1,3},{2,0},{3,1},{4,6},{5,7},{6,4},{7,5},{8,10},{9,11},{10,... | collective-permute-start | bytes 1572872 | tf_op jit(solution)/shard_map/first_xh1/ppermute | solution.py:38
  10.2 5.8 %copy-start = (bf16[2048,4096]{1,0:T(8,128)(2,1)S(1)}, bf16[2048,4096]{1,0:T(8,128)(2,1)}, u32[]{:S(2)}) copy-start(bf16[2048,4096]{1,0:T(8,128)(2,1)} %i_ref.11) | copy-start | bytes 50331652
  16.0 1.0 %copy-start.1 = (bf16[128,2048]{1,0:T(8,128)(2,1)S(1)}, bf16[128,2048]{1,0:T(8,128)(2,1)}, u32[]{:S(2)}) copy-start(bf16[128,2048]{1,0:T(8,128)(2,1)} %f0.3) | copy-start | bytes 1572868
  21.5 6.1 %collective-permute-start.8 = (bf16[128,2048]{1,0:T(8,128)(2,1)S(1)}, bf16[128,2048]{1,0:T(8,128)(2,1)S(1)}, u32[]{:S(2)}, u32[]{:S(2)}) collective-permute-start(bf16[128,2048]{1,0:T(8,128)(2,1)S(1)} %collective-permute-done.7.f2), channel_id=1, source_target_pairs={{0,1},{1,0},{2,3},{3,2},{4,5},{5,4},{6,7},{7,6},{8,9},{9,8},{10,11... | collective-permute-start | bytes 1572872 | tf_op jit(solution)/shard_map/first_core1/ppermute | solution.py:38
  21.5 14.2 %copy-start.2 = (bf16[128,2048]{1,0:T(8,128)(2,1)S(1)}, bf16[128,2048]{1,0:T(8,128)(2,1)}, u32[]{:S(2)}) copy-start(bf16[128,2048]{1,0:T(8,128)(2,1)} %f0.3) | copy-start | bytes 1572868
  21.5 18.4 %collective-permute-start.4 = (bf16[64,4096]{1,0:T(8,128)(2,1)S(1)}, bf16[64,4096]{1,0:T(8,128)(2,1)S(1)}, u32[]{:S(2)}, u32[]{:S(2)}) collective-permute-start(bf16[64,4096]{1,0:T(8,128)(2,1)S(1)} %constant_dynamic-update-slice_fusion.n0), channel_id=1, source_target_pairs={{0,4},{1,5},{2,6},{3,7},{4,0},{5,1},{6,2},{7,3},{8,12},{9,13},{10,... | collective-permute-start | bytes 1572872 | tf_op jit(solution)/shard_map/n_xl1/ppermute | solution.py:38
  23.2 16.8 %collective-permute-start.5 = (bf16[64,4096]{1,0:T(8,128)(2,1)S(1)}, bf16[64,4096]{1,0:T(8,128)(2,1)S(1)}, u32[]{:S(2)}, u32[]{:S(2)}) collective-permute-start(bf16[64,4096]{1,0:T(8,128)(2,1)S(1)} %constant_dynamic-update-slice_fusion.n0), channel_id=1, source_target_pairs={{0,8},{1,9},{2,10},{3,11},{4,12},{5,13},{6,14},{7,15},{8,0},{9,1},... | collective-permute-start | bytes 1572872 | tf_op jit(solution)/shard_map/n_z1/ppermute | solution.py:38
  25.1 15.0 %collective-permute-start.6 = (bf16[64,4096]{1,0:T(8,128)(2,1)S(1)}, bf16[64,4096]{1,0:T(8,128)(2,1)S(1)}, u32[]{:S(2)}, u32[]{:S(2)}) collective-permute-start(bf16[64,4096]{1,0:T(8,128)(2,1)S(1)} %constant_dynamic-update-slice_fusion.n0), channel_id=1, source_target_pairs={{0,24},{1,25},{2,26},{3,27},{4,28},{5,29},{6,30},{7,31},{8,16},{9,... | collective-permute-start | bytes 1572872 | tf_op jit(solution)/shard_map/n_z3/ppermute | solution.py:38
  32.6 21.9 %collective-permute-start.13 = (s16[256,1664]{1,0:T(8,128)(2,1)S(1)}, s16[256,1664]{1,0:T(8,128)(2,1)S(1)}, u32[]{:S(2)}, u32[]{:S(2)}) collective-permute-start(s16[256,1664]{1,0:T(8,128)(2,1)S(1)} %get-tuple-element.104), channel_id=1, source_target_pairs={{0,96},{1,97},{2,98},{3,99},{4,100},{5,101},{6,102},{7,103},{8,104... | collective-permute-start | bytes 2555912 | tf_op jit(solution)/shard_map/pa_y3/ppermute | solution.py:38
  35.7 20.2 %collective-permute-start.14 = (s16[256,1664]{1,0:T(8,128)(2,1)S(1)}, s16[256,1664]{1,0:T(8,128)(2,1)S(1)}, u32[]{:S(2)}, u32[]{:S(2)}) collective-permute-start(s16[256,1664]{1,0:T(8,128)(2,1)S(1)} %get-tuple-element.106), channel_id=1, source_target_pairs={{0,32},{1,33},{2,34},{3,35},{4,36},{5,37},{6,38},{7,39},{8,40},{9,... | collective-permute-start | bytes 2555912 | tf_op jit(solution)/shard_map/pb_y1/ppermute | solution.py:38
  35.7 25.2 %slice-start = ((s8[16777216]{0:T(1024)(128)(4,1)}), s8[4194304]{0:T(1024)(128)(4,1)S(1)}, s32[]{:S(2)}) async-start(s8[16777216]{0:T(1024)(128)(4,1)} %bitcast.3), calls=%async_computation | async-start | bytes 8388608
  35.7 25.2 %slice-start.1 = ((s8[16777216]{0:T(1024)(128)(4,1)}), s8[4194304]{0:T(1024)(128)(4,1)S(1)}, s32[]{:S(2)}) async-start(s8[16777216]{0:T(1024)(128)(4,1)} %bitcast.3), calls=%async_computation.1 | async-start | bytes 8388608
  37.6 23.3 %slice-start.2 = ((s8[16777216]{0:T(1024)(128)(4,1)}), s8[4194304]{0:T(1024)(128)(4,1)S(1)}, s32[]{:S(2)}) async-start(s8[16777216]{0:T(1024)(128)(4,1)} %bitcast.3), calls=%async_computation.2 | async-start | bytes 8388608
  37.6 23.3 %slice-start.3 = ((s8[16777216]{0:T(1024)(128)(4,1)}), s8[4194304]{0:T(1024)(128)(4,1)S(1)}, s32[]{:S(2)}) async-start(s8[16777216]{0:T(1024)(128)(4,1)} %bitcast.3), calls=%async_computation.3 | async-start | bytes 8388608
  40.1 18.7 %collective-permute-start.11 = (bf16[64,4096]{1,0:T(8,128)(2,1)S(1)}, bf16[64,4096]{1,0:T(8,128)(2,1)S(1)}, u32[]{:S(2)}, u32[]{:S(2)}) collective-permute-start(bf16[64,4096]{1,0:T(8,128)(2,1)S(1)} %collective-permute-done.4.n1), channel_id=1, source_target_pairs={{0,8},{1,9},{2,10},{3,11},{4,12},{5,13},{6,14},{7,15},{8,0},{9,1},... | collective-permute-start | bytes 1572872 | tf_op jit(solution)/shard_map/x_z1/ppermute | solution.py:38
  41.0 17.8 %collective-permute-start.12 = (bf16[64,4096]{1,0:T(8,128)(2,1)S(1)}, bf16[64,4096]{1,0:T(8,128)(2,1)S(1)}, u32[]{:S(2)}, u32[]{:S(2)}) collective-permute-start(bf16[64,4096]{1,0:T(8,128)(2,1)S(1)} %collective-permute-done.4.n1), channel_id=1, source_target_pairs={{0,24},{1,25},{2,26},{3,27},{4,28},{5,29},{6,30},{7,31},{8,16},{9,... | collective-permute-start | bytes 1572872 | tf_op jit(solution)/shard_map/x_z3/ppermute | solution.py:38
  43.0 23.2 %collective-permute-start.17 = (s16[256,1152]{1,0:T(8,128)(2,1)S(1)}, s16[256,1152]{1,0:T(8,128)(2,1)S(1)}, u32[]{:S(2)}, u32[]{:S(2)}) collective-permute-start(s16[256,1152]{1,0:T(8,128)(2,1)S(1)} %get-tuple-element.120), channel_id=1, source_target_pairs={{0,4},{1,5},{2,6},{3,7},{4,0},{5,1},{6,2},{7,3},{8,12},{9,13},{10,... | collective-permute-start | bytes 1769480 | tf_op jit(solution)/shard_map/q_xl1/ppermute | solution.py:38
  56.6 11.5 %collective-permute-start.16 = (s16[128,1664]{1,0:T(8,128)(2,1)S(1)}, s16[128,1664]{1,0:T(8,128)(2,1)S(1)}, u32[]{:S(2)}, u32[]{:S(2)}) collective-permute-start(s16[128,1664]{1,0:T(8,128)(2,1)S(1)} %get-tuple-element.116), channel_id=1, source_target_pairs={{0,96},{1,97},{2,98},{3,99},{4,100},{5,101},{6,102},{7,103},{8,104... | collective-permute-start | bytes 1277960 | tf_op jit(solution)/shard_map/pb_y3/ppermute | solution.py:38
  58.8 10.3 %collective-permute-start.15 = (s16[128,1664]{1,0:T(8,128)(2,1)S(1)}, s16[128,1664]{1,0:T(8,128)(2,1)S(1)}, u32[]{:S(2)}, u32[]{:S(2)}) collective-permute-start(s16[128,1664]{1,0:T(8,128)(2,1)S(1)} %get-tuple-element.114), channel_id=1, source_target_pairs={{0,32},{1,33},{2,34},{3,35},{4,36},{5,37},{6,38},{7,39},{8,40},{9,... | collective-permute-start | bytes 1277960 | tf_op jit(solution)/shard_map/pa_y1/ppermute | solution.py:38
  58.9 12.4 %collective-permute-start.19 = (bf16[64,4096]{1,0:T(8,128)(2,1)S(1)}, bf16[64,4096]{1,0:T(8,128)(2,1)S(1)}, u32[]{:S(2)}, u32[]{:S(2)}) collective-permute-start(bf16[64,4096]{1,0:T(8,128)(2,1)S(1)} %collective-permute-done.6.n3), channel_id=1, source_target_pairs={{0,8},{1,9},{2,10},{3,11},{4,12},{5,13},{6,14},{7,15},{8,0},{9,1},... | collective-permute-start | bytes 1572872 | tf_op jit(solution)/shard_map/n3_z1/ppermute | solution.py:38
  60.0 13.8 %collective-permute-start.20 = (bf16[64,4096]{1,0:T(8,128)(2,1)S(1)}, bf16[64,4096]{1,0:T(8,128)(2,1)S(1)}, u32[]{:S(2)}, u32[]{:S(2)}) collective-permute-start(bf16[64,4096]{1,0:T(8,128)(2,1)S(1)} %collective-permute-done.11.n0), channel_id=1, source_target_pairs={{0,24},{1,25},{2,26},{3,27},{4,28},{5,29},{6,30},{7,31},{8,16},{9,... | collective-permute-start | bytes 1572872 | tf_op jit(solution)/shard_map/x1_z3/ppermute | solution.py:38
  66.3 15.1 %collective-permute-start.9 = (f32[128,2048]{1,0:T(8,128)S(1)}, f32[128,2048]{1,0:T(8,128)S(1)}, u32[]{:S(2)}, u32[]{:S(2)}) collective-permute-start(f32[128,2048]{1,0:T(8,128)S(1)} %get-tuple-element.100), channel_id=1, source_target_pairs={{0,1},{1,0},{2,3},{3,2},{4,5},{5,4},{6,7},{7,6},{8,9},{9,8},{10,11... | collective-permute-start | bytes 3145736 | tf_op jit(solution)/shard_map/chunk0_core1/ppermute | solution.py:38
  69.9 11.1 %collective-permute-start.18 = (s16[64,3200]{1,0:T(8,128)(2,1)S(1)}, s16[64,3200]{1,0:T(8,128)(2,1)S(1)}, u32[]{:S(2)}, u32[]{:S(2)}) collective-permute-start(s16[64,3200]{1,0:T(8,128)(2,1)S(1)} %get-tuple-element.125), channel_id=1, source_target_pairs={{0,4},{1,5},{2,6},{3,7},{4,0},{5,1},{6,2},{7,3},{8,12},{9,13},{10,... | collective-permute-start | bytes 1228808 | tf_op jit(solution)/shard_map/p_xl1/ppermute | solution.py:38
  70.5 10.5 %collective-permute-start.21 = (s16[64,1152]{1,0:T(8,128)(2,1)S(1)}, s16[64,1152]{1,0:T(8,128)(2,1)S(1)}, u32[]{:S(2)}, u32[]{:S(2)}) collective-permute-start(s16[64,1152]{1,0:T(8,128)(2,1)S(1)} %get-tuple-element.136), channel_id=1, source_target_pairs={{0,32},{1,33},{2,34},{3,35},{4,36},{5,37},{6,38},{7,39},{8,40},{9,... | collective-permute-start | bytes 442376 | tf_op jit(solution)/shard_map/q_y1/ppermute | solution.py:38
  71.3 9.7 %collective-permute-start.22 = (s16[64,1152]{1,0:T(8,128)(2,1)S(1)}, s16[64,1152]{1,0:T(8,128)(2,1)S(1)}, u32[]{:S(2)}, u32[]{:S(2)}) collective-permute-start(s16[64,1152]{1,0:T(8,128)(2,1)S(1)} %get-tuple-element.137), channel_id=1, source_target_pairs={{0,64},{1,65},{2,66},{3,67},{4,68},{5,69},{6,70},{7,71},{8,72},{9,... | collective-permute-start | bytes 442376 | tf_op jit(solution)/shard_map/q_y2/ppermute | solution.py:38
  73.8 7.1 %collective-permute-start.23 = (s16[64,1152]{1,0:T(8,128)(2,1)S(1)}, s16[64,1152]{1,0:T(8,128)(2,1)S(1)}, u32[]{:S(2)}, u32[]{:S(2)}) collective-permute-start(s16[64,1152]{1,0:T(8,128)(2,1)S(1)} %get-tuple-element.138), channel_id=1, source_target_pairs={{0,96},{1,97},{2,98},{3,99},{4,100},{5,101},{6,102},{7,103},{8,104... | collective-permute-start | bytes 442376 | tf_op jit(solution)/shard_map/q_y3/ppermute | solution.py:38
  81.0 4.4 %collective-permute-start.24 = (f32[128,2048]{1,0:T(8,128)S(1)}, f32[128,2048]{1,0:T(8,128)S(1)}, u32[]{:S(2)}, u32[]{:S(2)}) collective-permute-start(f32[128,2048]{1,0:T(8,128)S(1)} %get-tuple-element.140), channel_id=1, source_target_pairs={{0,1},{1,0},{2,3},{3,2},{4,5},{5,4},{6,7},{7,6},{8,9},{9,8},{10,11... | collective-permute-start | bytes 3145736 | tf_op jit(solution)/shard_map/chunk1_core1/ppermute | solution.py:38
  81.7 11.0 %collective-permute-start.10 = (s16[64,2176]{1,0:T(8,128)(2,1)S(1)}, s16[64,2176]{1,0:T(8,128)(2,1)S(1)}, u32[]{:S(2)}, u32[]{:S(2)}) collective-permute-start(s16[64,2176]{1,0:T(8,128)(2,1)S(1)} %get-tuple-element.102), channel_id=1, source_target_pairs={{0,2},{1,3},{2,0},{3,1},{4,6},{5,7},{6,4},{7,5},{8,10},{9,11},{10,... | collective-permute-start | bytes 835592 | tf_op jit(solution)/shard_map/chunk0_xh1/ppermute | solution.py:38
  85.8 12.5 %collective-permute-start.25 = (s16[64,2176]{1,0:T(8,128)(2,1)S(1)}, s16[64,2176]{1,0:T(8,128)(2,1)S(1)}, u32[]{:S(2)}, u32[]{:S(2)}) collective-permute-start(s16[64,2176]{1,0:T(8,128)(2,1)S(1)} %get-tuple-element.154), channel_id=1, source_target_pairs={{0,2},{1,3},{2,0},{3,1},{4,6},{5,7},{6,4},{7,5},{8,10},{9,11},{10,... | collective-permute-start | bytes 835592 | tf_op jit(solution)/shard_map/chunk1_xh1/ppermute | solution.py:38
  87.1 12.7 %collective-permute-start.26 = (s16[16,4224]{1,0:T(8,128)(2,1)S(1)}, s16[16,4224]{1,0:T(8,128)(2,1)S(1)}, u32[]{:S(2)}, u32[]{:S(2)}) collective-permute-start(s16[16,4224]{1,0:T(8,128)(2,1)S(1)} %get-tuple-element.156), channel_id=1, source_target_pairs={{0,8},{1,9},{2,10},{3,11},{4,12},{5,13},{6,14},{7,15},{8,0},{9,1},... | collective-permute-start | bytes 405512 | tf_op jit(solution)/shard_map/z_z1/ppermute | solution.py:38
  88.2 11.7 %collective-permute-start.27 = (s16[16,4224]{1,0:T(8,128)(2,1)S(1)}, s16[16,4224]{1,0:T(8,128)(2,1)S(1)}, u32[]{:S(2)}, u32[]{:S(2)}) collective-permute-start(s16[16,4224]{1,0:T(8,128)(2,1)S(1)} %get-tuple-element.157), channel_id=1, source_target_pairs={{0,16},{1,17},{2,18},{3,19},{4,20},{5,21},{6,22},{7,23},{8,24},{9,... | collective-permute-start | bytes 405512 | tf_op jit(solution)/shard_map/z_z2/ppermute | solution.py:38
  91.0 8.9 %collective-permute-start.28 = (s16[16,4224]{1,0:T(8,128)(2,1)S(1)}, s16[16,4224]{1,0:T(8,128)(2,1)S(1)}, u32[]{:S(2)}, u32[]{:S(2)}) collective-permute-start(s16[16,4224]{1,0:T(8,128)(2,1)S(1)} %get-tuple-element.158), channel_id=1, source_target_pairs={{0,24},{1,25},{2,26},{3,27},{4,28},{5,29},{6,30},{7,31},{8,16},{9,... | collective-permute-start | bytes 405512 | tf_op jit(solution)/shard_map/z_z3/ppermute | solution.py:38
